TPU v7x, 32 devices: a whole 2x2x4 slice. The times are simulated.
32 devices in a mesh: dp: 32 (over z, y, x, core).
Axes of the slice: x: 2, y: 2, z: 4, core: 2. Of those that a mesh axis runs over, the one named last changes fastest.
Arguments:
- clip_tokens: bfloat16 [32, 8, 256, 512], P('dp'), may hold values from -6 to 6
- cotangent: bfloat16 [32, 8, 256, 512], P('dp'), may hold values from -6 to 6
- lengths: int32 [32], P('dp'), may hold values from 1 to 8
- params: float32 [2, 3145728], P(None, 'dp'), may hold values from -0.35355339 to 0.35355339, as said below
- param_moment: float32 [2, 3145728], P(None, 'dp'), may hold values from -80 to 80
- param_second: float32 [2, 3145728], P(None, 'dp'), may hold values from 13.1072 to 52.4288
- norm_par: float32 [4096], P('dp'), may hold values from -1.2 to 1.3, as said below
- norm_moment: float32 [4096], P('dp'), may hold values from -192 to 192
- norm_second: float32 [4096], P('dp'), may hold values from 98.304 to 393.216
Outputs:
- output: float32 [32, 8, 256, 512], P('dp')
- grad_input: float32 [32, 8, 256, 512], P('dp')
- new_params: float32 [2, 3145728], P(None, 'dp')
- new_moment: float32 [2, 3145728], P(None, 'dp')
- new_second: float32 [2, 3145728], P(None, 'dp')
- params_copy: bfloat16 [2, 3145728], P(None, 'dp')
- new_norm: float32 [4096], P('dp')
- new_norm_moment: float32 [4096], P('dp')
- new_norm_second: float32 [4096], P('dp')
Inputs may be any that keep to these rules, and one draw needn't show every extreme that they name: Slots 0 to lengths - 1 of a clip are its real steps. `params`: master matrices of both blocks, packed as the steps say. `norm_par`: gains and biases of the four norms, packed as the steps say.
All inputs are finite; a program needn't handle non-finite values.
Results may differ from a plain program's by a relative error of at most 0.02.
The roundings to bfloat16 on the way count: a program that leaves them out, or rounds other values in their place, can miss the bound.
Values may be sent and summed in bfloat16 or wider, within the bound.
A program may use at most 320 MiB of HBM per device.

v0:
```python
from functools import partial

import jax
import jax.numpy as jnp
from jax import lax
from jax.sharding import PartitionSpec as P

HEADS = 8
HEAD_DIM = 64
FF = 2048
STEP = 7


norm_epsilon = 1e-05
beta_first = 0.9
beta_second = 0.999
learn_rate = 0.05
norm_rate = 0.5
weight_decay = 0.1
adam_floor = 1e-08
masked_score = -1e30


def norm_apply(token_rows, norm_gain, norm_shift):
    center = token_rows - jnp.mean(token_rows, axis=-1, keepdims=True)
    spread = jnp.mean(center * center, axis=-1, keepdims=True)
    return center * lax.rsqrt(spread + norm_epsilon) * norm_gain + norm_shift


def unpack(flat_weights, model_width, hidden_width):
    cut_qkv = 3 * model_width * model_width
    cut_out = 4 * model_width * model_width
    cut_up = cut_out + model_width * hidden_width
    return (
        flat_weights[:cut_qkv].reshape(model_width, 3 * model_width),
        flat_weights[cut_qkv:cut_out].reshape(model_width, model_width),
        flat_weights[cut_out:cut_up].reshape(model_width, hidden_width),
        flat_weights[cut_up:].reshape(hidden_width, model_width),
    )


def matmul(left_side, right_side):
    return jnp.dot(left_side, right_side, preferred_element_type=jnp.float32)


def weight_grad(inputs, grad_rows):
    return lax.dot_general(
        inputs, grad_rows, (((0,), (0,)), ((), ())), preferred_element_type=jnp.float32
    )


def input_grad(grad_rows, weights):
    return lax.dot_general(
        grad_rows, weights, (((1,), (1,)), ((), ())), preferred_element_type=jnp.float32
    )


def head_slices(token_grid, head_number, model_width):
    offset = head_number * HEAD_DIM
    query_head = token_grid[:, :, offset : offset + HEAD_DIM]
    key_head = token_grid[:, :, model_width + offset : model_width + offset + HEAD_DIM]
    value_head = token_grid[:, :, 2 * model_width + offset : 2 * model_width + offset + HEAD_DIM]
    return (query_head, key_head, value_head)


def frame_scores(query_head, key_head):
    return jnp.einsum(
        "fpe,fqe->fpq", query_head, key_head, preferred_element_type=jnp.float32
    ) * HEAD_DIM ** (-0.5)


def spatial_forward(packed, frame_count):
    model_width = packed.shape[1] // 3
    token_grid = packed.reshape(frame_count, -1, 3 * model_width)
    mixtures = []
    logsums = []
    for head_number in range(HEADS):
        query_head, key_head, value_head = head_slices(token_grid, head_number, model_width)
        scores = frame_scores(query_head, key_head)
        maxima = jnp.max(scores, axis=-1, keepdims=True)
        logsum = maxima + jnp.log(jnp.sum(jnp.exp(scores - maxima), axis=-1, keepdims=True))
        soft_low = jnp.exp(scores - logsum).astype(jnp.bfloat16)
        mixtures.append(
            jnp.einsum(
                "fpq,fqe->fpe", soft_low, value_head, preferred_element_type=jnp.float32
            ).astype(jnp.bfloat16)
        )
        logsums.append(logsum)
    return (jnp.concatenate(mixtures, axis=-1).reshape(-1, model_width), logsums)


def spatial_backward(packed, logsums, grad_mix, frame_count):
    model_width = packed.shape[1] // 3
    token_grid = packed.reshape(frame_count, -1, 3 * model_width)
    grad_grid = grad_mix.reshape(frame_count, -1, model_width)
    sections = ([], [], [])
    for head_number in range(HEADS):
        query_head, key_head, value_head = head_slices(token_grid, head_number, model_width)
        offset = head_number * HEAD_DIM
        grad_head = grad_grid[:, :, offset : offset + HEAD_DIM]
        soft_weights = jnp.exp(frame_scores(query_head, key_head) - logsums[head_number])
        soft_low = soft_weights.astype(jnp.bfloat16)
        grad_values = jnp.einsum(
            "fpq,fpe->fqe", soft_low, grad_head, preferred_element_type=jnp.float32
        )
        grad_soft = jnp.einsum(
            "fpe,fqe->fpq", grad_head, value_head, preferred_element_type=jnp.float32
        )
        inner_sum = jnp.sum(grad_soft * soft_weights, axis=-1, keepdims=True)
        grad_scores = (soft_weights * (grad_soft - inner_sum)).astype(jnp.bfloat16)
        sections[0].append(
            jnp.einsum("fpq,fqe->fpe", grad_scores, key_head, preferred_element_type=jnp.float32)
            * HEAD_DIM ** (-0.5)
        )
        sections[1].append(
            jnp.einsum("fpq,fpe->fqe", grad_scores, query_head, preferred_element_type=jnp.float32)
            * HEAD_DIM ** (-0.5)
        )
        sections[2].append(grad_values)
    joined = jnp.concatenate([jnp.concatenate(section, axis=-1) for section in sections], axis=-1)
    return joined.reshape(-1, 3 * model_width)


def temporal_parts(packed, shape_info):
    clip_count, step_slots, patch_count, model_width = shape_info
    token_grid = packed.reshape(clip_count, step_slots, patch_count, 3, HEADS, HEAD_DIM)
    return (token_grid[:, :, :, 0], token_grid[:, :, :, 1], token_grid[:, :, :, 2])


def temporal_scores(queries, keys, allowed):
    scores = jnp.einsum(
        "ctphe,cuphe->chtup", queries, keys, preferred_element_type=jnp.float32
    ) * HEAD_DIM ** (-0.5)
    return jnp.where(allowed, scores, masked_score)


def temporal_forward(packed, allowed, shape_info):
    queries, keys, values = temporal_parts(packed, shape_info)
    scores = temporal_scores(queries, keys, allowed)
    maxima = jnp.max(scores, axis=3, keepdims=True)
    logsum = maxima + jnp.log(jnp.sum(jnp.exp(scores - maxima), axis=3, keepdims=True))
    soft_low = jnp.exp(scores - logsum).astype(jnp.bfloat16)
    mixture = jnp.einsum(
        "chtup,cuphe->ctphe", soft_low, values, preferred_element_type=jnp.float32
    ).astype(jnp.bfloat16)
    return (mixture.reshape(-1, shape_info[3]), logsum)


def temporal_backward(packed, logsum, grad_mix, allowed, shape_info):
    queries, keys, values = temporal_parts(packed, shape_info)
    grad_out = grad_mix.reshape(queries.shape)
    soft_weights = jnp.exp(temporal_scores(queries, keys, allowed) - logsum)
    soft_low = soft_weights.astype(jnp.bfloat16)
    grad_values = jnp.einsum(
        "chtup,ctphe->cuphe", soft_low, grad_out, preferred_element_type=jnp.float32
    )
    grad_soft = jnp.einsum(
        "ctphe,cuphe->chtup", grad_out, values, preferred_element_type=jnp.float32
    )
    inner_sum = jnp.sum(grad_soft * soft_weights, axis=3, keepdims=True)
    grad_scores = (soft_weights * (grad_soft - inner_sum)).astype(jnp.bfloat16)
    grad_queries = jnp.einsum(
        "chtup,cuphe->ctphe", grad_scores, keys, preferred_element_type=jnp.float32
    ) * HEAD_DIM ** (-0.5)
    grad_keys = jnp.einsum(
        "chtup,ctphe->cuphe", grad_scores, queries, preferred_element_type=jnp.float32
    ) * HEAD_DIM ** (-0.5)
    stacked = jnp.stack([grad_queries, grad_keys, grad_values], axis=3)
    return stacked.reshape(-1, 3 * shape_info[3])


def block_forward(token_rows, weights, norm_pair, mixer_forward):
    w_qkv, w_out, w_up, w_down = weights
    normed_full, norm_back_first = jax.vjp(norm_apply, token_rows, norm_pair[0, 0], norm_pair[0, 1])
    normed = normed_full.astype(jnp.bfloat16)
    packed = matmul(normed, w_qkv).astype(jnp.bfloat16)
    mixture, attn_saved = mixer_forward(packed)
    rows_middle = token_rows + matmul(mixture, w_out)
    second_full, norm_back_second = jax.vjp(
        norm_apply, rows_middle, norm_pair[1, 0], norm_pair[1, 1]
    )
    second = second_full.astype(jnp.bfloat16)
    hidden_pre = matmul(second, w_up)
    active_full, gelu_back = jax.vjp(partial(jax.nn.gelu, approximate=False), hidden_pre)
    active = active_full.astype(jnp.bfloat16)
    rows_after = rows_middle + matmul(active, w_down)
    return (
        rows_after,
        (
            norm_back_first,
            normed,
            packed,
            mixture,
            attn_saved,
            norm_back_second,
            second,
            gelu_back,
            active,
        ),
    )


def block_backward(grad_after, weights, kept_values, mixer_backward):
    w_qkv, w_out, w_up, w_down = weights
    (
        norm_back_first,
        normed,
        packed,
        mixture,
        attn_saved,
        norm_back_second,
        second,
        gelu_back,
        active,
    ) = kept_values
    grad_branch = grad_after.astype(jnp.bfloat16)
    grad_down = weight_grad(active, grad_branch)
    grad_active = input_grad(grad_branch, w_down)
    grad_hidden = gelu_back(grad_active)[0].astype(jnp.bfloat16)
    grad_up = weight_grad(second, grad_hidden)
    grad_second = input_grad(grad_hidden, w_up)
    grad_middle, gain_second, shift_second = norm_back_second(grad_second)
    grad_middle = grad_middle + grad_after
    grad_attn = grad_middle.astype(jnp.bfloat16)
    grad_outproj = weight_grad(mixture, grad_attn)
    grad_mix = input_grad(grad_attn, w_out).astype(jnp.bfloat16)
    grad_packed = mixer_backward(packed, attn_saved, grad_mix).astype(jnp.bfloat16)
    grad_qkv = weight_grad(normed, grad_packed)
    grad_normed = input_grad(grad_packed, w_qkv)
    grad_before, gain_first, shift_first = norm_back_first(grad_normed)
    grad_before = grad_before + grad_middle
    flat_grad = jnp.concatenate(
        [grad_qkv.reshape(-1), grad_outproj.reshape(-1), grad_up.reshape(-1), grad_down.reshape(-1)]
    )
    norm_grad = jnp.stack(
        [jnp.stack([gain_first, shift_first]), jnp.stack([gain_second, shift_second])]
    )
    return (grad_before, flat_grad, norm_grad)


def adamw(param_value, moment, second, grad_total, step_value, rate, decay_rate):
    moment_next = beta_first * moment + (1.0 - beta_first) * grad_total
    second_next = beta_second * second + (1.0 - beta_second) * grad_total * grad_total
    moment_hat = moment_next / (1.0 - beta_first**step_value)
    second_hat = second_next / (1.0 - beta_second**step_value)
    param_next = param_value - rate * (
        moment_hat / (jnp.sqrt(second_hat) + adam_floor) + decay_rate * param_value
    )
    return (param_next, moment_next, second_next)


def on_device(
    clip_tokens,
    cotangent,
    lengths,
    params,
    param_moment,
    param_second,
    norm_par,
    norm_moment,
    norm_second,
):
    clip_count, step_slots, patch_count, model_width = clip_tokens.shape
    frame_count = clip_count * step_slots
    gathered, norm_whole = (
        lax.all_gather(params.astype(jnp.bfloat16), "dp", axis=1, tiled=True),
        lax.all_gather(norm_par.astype(jnp.bfloat16), "dp", axis=0, tiled=True),
    )
    spatial_flat = gathered[0]
    temporal_flat = gathered[1]
    norm_table = norm_whole.astype(jnp.float32).reshape(2, 2, 2, model_width)
    spatial_weights = unpack(spatial_flat, model_width, FF)
    slot_index = jnp.arange(step_slots)
    causal = slot_index[None, :] <= slot_index[:, None]
    present = slot_index[None, :] < lengths[:, None]
    allowed = (causal[None, :, :] & present[:, None, :])[:, None, :, :, None]
    token_rows = clip_tokens.reshape(-1, model_width).astype(jnp.float32)
    spatial_mixer = partial(spatial_forward, frame_count=frame_count)
    middle, spatial_kept = block_forward(token_rows, spatial_weights, norm_table[0], spatial_mixer)
    temporal_weights = unpack(temporal_flat, model_width, FF)
    temporal_mixer = partial(temporal_forward, allowed=allowed, shape_info=clip_tokens.shape)
    result, temporal_kept = block_forward(middle, temporal_weights, norm_table[1], temporal_mixer)
    live_mask = (slot_index[None, :] < lengths[:, None]).astype(jnp.float32)
    grad_rows = (cotangent.astype(jnp.float32) * live_mask[:, :, None, None]).reshape(
        -1, model_width
    )
    temporal_undo = partial(temporal_backward, allowed=allowed, shape_info=clip_tokens.shape)
    grad_middle, temporal_grad, temporal_norm = block_backward(
        grad_rows, temporal_weights, temporal_kept, temporal_undo
    )
    spatial_undo = partial(spatial_backward, frame_count=frame_count)
    grad_before, spatial_grad, spatial_norm = block_backward(
        grad_middle, spatial_weights, spatial_kept, spatial_undo
    )
    norm_grad = jnp.concatenate([spatial_norm.reshape(-1), temporal_norm.reshape(-1)])
    spatial_sum, temporal_sum, norm_sum = (
        lax.psum_scatter(spatial_grad, "dp", scatter_dimension=0, tiled=True),
        lax.psum_scatter(temporal_grad, "dp", scatter_dimension=0, tiled=True),
        lax.psum_scatter(norm_grad, "dp", scatter_dimension=0, tiled=True),
    )
    weight_sum = jnp.stack([spatial_sum, temporal_sum])
    step_value = float(STEP)
    new_params, new_moment, new_second = adamw(
        params, param_moment, param_second, weight_sum, step_value, learn_rate, weight_decay
    )
    new_norm, new_norm_moment, new_norm_second = adamw(
        norm_par, norm_moment, norm_second, norm_sum, step_value, norm_rate, 0.0
    )
    output = result.reshape(clip_tokens.shape)
    grad_input = grad_before.reshape(clip_tokens.shape)
    return (
        output,
        grad_input,
        new_params,
        new_moment,
        new_second,
        new_params.astype(jnp.bfloat16),
        new_norm,
        new_norm_moment,
        new_norm_second,
    )


def solution(mesh):
    placed = (
        P("dp", None, None, None),
        P("dp", None, None, None),
        P("dp"),
        P(None, "dp"),
        P(None, "dp"),
        P(None, "dp"),
        P("dp"),
        P("dp"),
        P("dp"),
    )
    return jax.shard_map(
        on_device,
        mesh=mesh,
        in_specs=placed,
        out_specs=(
            P("dp", None, None, None),
            P("dp", None, None, None),
            P(None, "dp"),
            P(None, "dp"),
            P(None, "dp"),
            P(None, "dp"),
            P("dp"),
            P("dp"),
            P("dp"),
        ),
        check_vma=False,
    )
```

profile of v0, /device:TPU:0, one launch (start us, length us, event | category | flops | bytes accessed | tf_op | source)
XLA Modules:
  0.0 1222.5 jit_solution(6003756872495330213)
XLA Ops:
  10.3 43.1 %all-gather = bf16[32,1,128]{2,1,0:T(2,128)(2,1)S(1)} all-gather(bf16[1,1,128]{2,1,0:T(2,128)(2,1)S(1)} %convert_bitcast_fusion.1), channel_id=1, replica_groups=mesh['dp'=32] {'dp'}, dimensions={0}, use_global_device_ids=true | all-gather | bytes 8448 | tf_op jit(solution)/shard_map/all_gather | solution.py:267
  67.3 42.9 %all-gather.3.cloned.1.call-done = bf16[2,3145728]{1,0:T(2,128)(2,1)} async-done(((bf16[2,98304]{1,0:T(2,128)(2,1)}), bf16[2,3145728]{1,0:T(2,128)(2,1)}) %all-gather.3.cloned.1.call-update) | async-done | bytes 12582928 | tf_op jit(solution)/shard_map/all_gather | solution.py:266
  110.2 36.1 %slice_reduce_fusion.4 = (bf16[786432]{0:T(1024)(128)(2,1)}, bf16[786432]{0:T(1024)(128)(2,1)}) fusion(bf16[2,3145728]{1,0:T(2,128)(2,1)} %all-gather.3.cloned.1.call-done), kind=kLoop, calls=%fused_computation.109 | loop fusion | bytes 6291456 | tf_op jit(solution)/shard_map/slice | solution.py:35
  179.2 13.2 %slice_reduce_fusion.6 = (bf16[262144]{0:T(1024)(128)(2,1)}, bf16[262144]{0:T(1024)(128)(2,1)S(1)}) fusion(bf16[2,3145728]{1,0:T(2,128)(2,1)} %all-gather.3.cloned.1.call-done), kind=kLoop, calls=%fused_computation.250 | loop fusion | bytes 2097152 | tf_op jit(solution)/shard_map/slice | solution.py:36
  199.4 50.2 %slice_reduce_fusion = (bf16[1048576]{0:T(1024)(128)(2,1)}, bf16[1048576]{0:T(1024)(128)(2,1)}, bf16[1048576]{0:T(1024)(128)(2,1)S(1)}, bf16[1048576]{0:T(1024)(128)(2,1)}) fusion(bf16[2,3145728]{1,0:T(2,128)(2,1)} %all-gather.3.cloned.1.call-done), kind=kLoop, calls=%fused_computation.55 | loop fusion | bytes 16777216 | tf_op jit(solution)/shard_map/slice | solution.py:38
  256.4 44.1 %multiply_convert_fusion.1 = (bf16[2048,2048]{1,0:T(8,128)(2,1)S(1)}, f32[2048,2048]{1,0:T(8,128)}, f32[2048,2048]{1,0:T(8,128)}) fusion(bf16[512,2048]{1,0:T(8,128)(2,1)} %reshape.666, f32[2048,512]{1,0:T(8,128)} %copy-done.29, f32[512]{0:T(512)S(1)} %bitcast.472, f32[512]{0:T(512)S(1)} %bitcast.458, f32[2048]{0:T(1024)S(1)} %fusion.208, ...), kind=kOutput, calls=%fused_computation.19 | convolution fusion | flops 4572839936 | bytes 48254976 | tf_op jit(solution)/shard_map/dot_general | solution.py:43
  310.6 9.0 convolution_convert_fusion
  362.4 9.2 copy.473
  404.8 44.3 %multiply_convert_fusion = (bf16[2048,2048]{1,0:T(8,128)(2,1)}, f32[2048,2048]{1,0:T(8,128)}, f32[2048,2048]{1,0:T(8,128)}) fusion(bf16[512,2048]{1,0:T(8,128)(2,1)} %reshape.676, f32[2048,512]{1,0:T(8,128)} %copy-done.21, f32[512]{0:T(512)S(1)} %bitcast.468, f32[512]{0:T(512)S(1)} %bitcast.450, f32[2048]{0:T(1024)S(1)} %fusion.210, ...), kind=kOutput, calls=%fused_computation.6 | convolution fusion | flops 4572839936 | bytes 48254976 | tf_op jit(solution)/shard_map/dot_general | solution.py:43
  449.1 18.4 %add_convert_fusion.1 = bf16[2048,2048]{1,0:T(8,128)(2,1)} fusion(f32[2048,2048]{1,0:T(8,128)} %get-tuple-element.47, f32[2048,2048]{1,0:T(8,128)} %get-tuple-element.97, bf16[2048,512]{1,0:T(8,128)(2,1)} %bitcast.410, bf16[2048,512]{1,0:T(8,128)(2,1)S(1)} %copy-done.66), kind=kOutput, calls=%fused_computation.5 | convolution fusion | flops 4353687552 | bytes 46137344 | tf_op jit(solution)/shard_map/dot_general | solution.py:53
  467.5 11.9 multiply_reduce_fusion
  516.0 9.2 fusion.12
  557.0 9.0 fusion.36
  577.9 9.2 fusion.40
  617.4 18.7 %add_convert_fusion = bf16[2048,2048]{1,0:T(8,128)(2,1)} fusion(f32[2048,2048]{1,0:T(8,128)} %get-tuple-element.49, f32[2048,2048]{1,0:T(8,128)} %get-tuple-element.90, bf16[2048,512]{1,0:T(8,128)(2,1)S(1)} %copy-done.69, f32[2048,512]{1,0:T(8,128)} %add_add_fusion.6), kind=kOutput, calls=%fused_computation.4 | convolution fusion | flops 4354736128 | bytes 48234496 | tf_op jit(solution)/shard_map/dot_general | solution.py:53
  636.1 12.0 multiply_reduce_fusion.2
  711.1 10.0 convolution_bitcast_fusion.2
  729.6 10.3 convolution_bitcast_fusion.1
  772.8 9.8 convolution_bitcast_fusion
  787.3 15.6 %pad_maximum_fusion = f32[3145728]{0:T(1024)} fusion(f32[1048576]{0:T(1024)S(1)} %bitcast.395, f32[1048576]{0:T(1024)S(1)} %bitcast.394, f32[262144]{0:T(1024)S(1)} %bitcast.405, f32[786432]{0:T(1024)S(1)} %reshape.684), kind=kLoop, calls=%fused_computation.35 | loop fusion | flops 9437184 | bytes 25165824 | tf_op jit(solution)/shard_map/concatenate | solution.py:232
  803.0 15.5 %pad_maximum_fusion.1 = f32[3145728]{0:T(1024)} fusion(f32[1048576]{0:T(1024)S(1)} %bitcast.397, f32[1048576]{0:T(1024)S(1)} %bitcast.396, f32[262144]{0:T(1024)S(1)} %bitcast.406, f32[786432]{0:T(1024)S(1)} %copy-done.48), kind=kLoop, calls=%fused_computation.36 | loop fusion | flops 9437184 | bytes 25165824 | tf_op jit(solution)/shard_map/concatenate | solution.py:232
  831.4 40.5 %all-reduce.2 = f32[4096]{0:T(1024)S(1)} all-reduce(f32[4096]{0:T(1024)S(1)} %pad_maximum_fusion.3), channel_id=4, replica_groups=mesh['dp'=32] {'dp'}, use_global_device_ids=true, to_apply=%region_53.54.clone | all-reduce | flops 4096 | bytes 32768
  879.5 10.1 convolution_add_fusion.1
  889.6 319.3 %all-reduce.6.cloned.1.call-done = (f32[3145728]{0:T(1024)}, f32[3145728]{0:T(1024)}) async-done(((f32[3145728]{0:T(1024)}, f32[3145728]{0:T(1024)}), (f32[3145728]{0:T(1024)}, f32[3145728]{0:T(1024)})) %all-reduce.6.cloned.1.call-update) | async-done | bytes 25165840
  (556 shorter events, 393.6 us)
Async XLA Ops:
  7.2 51.0 %copy-start.2 = (bf16[1,8,256,512]{3,2,1,0:T(8,128)(2,1)S(1)}, bf16[1,8,256,512]{3,2,1,0:T(8,128)(2,1)}, u32[]{:S(2)}) copy-start(bf16[1,8,256,512]{3,2,1,0:T(8,128)(2,1)} %param.9) | copy-start | bytes 6291460
  7.2 103.0 %all-gather.3.cloned.1.call-start = ((), (), s32[]{:S(2)}) async-start(), calls=%async_computation | async-start | bytes 12976128 | tf_op jit(solution)/shard_map/all_gather | solution.py:266
  9.5 1199.4 %all-reduce.6.cloned.1.call-start = ((), (), s32[]{:S(2)}) async-start(), calls=%async_computation.1 | async-start | bytes 50331648
  56.9 199.4 %copy-start.133 = (f32[1,1,512]{2,1,0:T(1,128)}, f32[1,1,512]{2,1,0:T(1,128)S(1)}, u32[]{:S(2)}) copy-start(f32[1,1,512]{2,1,0:T(1,128)S(1)} %get-tuple-element.68) | copy-start | bytes 6148
  57.0 199.4 %copy-start.145 = (f32[1,1,512]{2,1,0:T(1,128)}, f32[1,1,512]{2,1,0:T(1,128)S(1)}, u32[]{:S(2)}) copy-start(f32[1,1,512]{2,1,0:T(1,128)S(1)} %get-tuple-element.69) | copy-start | bytes 6148
  195.9 60.5 %copy-start.110 = (f32[2048]{0:T(1024)}, f32[2048]{0:T(1024)S(1)}, u32[]{:S(2)}) copy-start(f32[2048]{0:T(1024)S(1)} %broadcast_multiply_fusion.2) | copy-start | bytes 24580
  199.4 57.0 %copy-start.120 = (f32[2048]{0:T(1024)}, f32[2048]{0:T(1024)S(1)}, u32[]{:S(2)}) copy-start(f32[2048]{0:T(1024)S(1)} %fusion.208) | copy-start | bytes 24580
  256.4 44.1 %copy-start.30 = (f32[2048,512]{1,0:T(8,128)S(1)}, f32[2048,512]{1,0:T(8,128)}, u32[]{:S(2)}) copy-start(f32[2048,512]{1,0:T(8,128)} %copy-done.29) | copy-start | bytes 12582916
  256.4 44.1 %copy-start.68 = (bf16[2048,512]{1,0:T(8,128)(2,1)S(1)}, bf16[2048,512]{1,0:T(8,128)(2,1)}, u32[]{:S(2)}) copy-start(bf16[2048,512]{1,0:T(8,128)(2,1)} %reshape.667) | copy-start | bytes 6291460
  362.4 18.0 %copy-start.39 = (f32[8,8,256]{1,2,0:T(8,128)}, f32[8,8,256]{1,2,0:T(8,128)S(1)}, u32[]{:S(2)}) copy-start(f32[8,8,256]{1,2,0:T(8,128)S(1)} %log_add_fusion) | copy-start | bytes 196612
  394.7 84.8 %copy-start.114 = (f32[2048]{0:T(1024)}, f32[2048]{0:T(1024)S(1)}, u32[]{:S(2)}) copy-start(f32[2048]{0:T(1024)S(1)} %broadcast_multiply_fusion) | copy-start | bytes 24580
  398.1 81.4 %copy-start.124 = (f32[2048]{0:T(1024)}, f32[2048]{0:T(1024)S(1)}, u32[]{:S(2)}) copy-start(f32[2048]{0:T(1024)S(1)} %fusion.210) | copy-start | bytes 24580
  404.8 44.3 %copy-start.66 = (bf16[2048,512]{1,0:T(8,128)(2,1)S(1)}, bf16[2048,512]{1,0:T(8,128)(2,1)}, u32[]{:S(2)}) copy-start(bf16[2048,512]{1,0:T(8,128)(2,1)} %reshape.677) | copy-start | bytes 6291460
  617.4 18.7 %copy-start.111 = (f32[2048]{0:T(1024)S(1)}, f32[2048]{0:T(1024)}, u32[]{:S(2)}) copy-start(f32[2048]{0:T(1024)} %copy-done.110) | copy-start | bytes 24580
  617.4 18.7 %copy-start.121 = (f32[2048]{0:T(1024)S(1)}, f32[2048]{0:T(1024)}, u32[]{:S(2)}) copy-start(f32[2048]{0:T(1024)} %copy-done.120) | copy-start | bytes 24580
  617.4 18.7 %copy-start.134 = (f32[1,1,512]{2,1,0:T(1,128)S(1)}, f32[1,1,512]{2,1,0:T(1,128)}, u32[]{:S(2)}) copy-start(f32[1,1,512]{2,1,0:T(1,128)} %copy-done.133) | copy-start | bytes 6148
  651.6 69.5 %copy-start.20 = (f32[2048,512]{1,0:T(8,128)}, f32[2048,512]{1,0:T(8,128)S(1)}, u32[]{:S(2)}) copy-start(f32[2048,512]{1,0:T(8,128)S(1)} %add_add_fusion.5) | copy-start | bytes 12582916
  703.8 19.6 %slice-start.2 = ((s8[6291456]{0:T(1024)(128)(4,1)}), s8[2097152]{0:T(1024)(128)(4,1)S(1)}, s32[]{:S(2)}) async-start(s8[6291456]{0:T(1024)(128)(4,1)} %bitcast.402), calls=%async_computation.4 | async-start | bytes 4194304
  827.0 44.9 %copy-start.147 = (f32[128]{0:T(128)S(1)}, f32[128]{0:T(128)}, u32[]{:S(2)}) copy-start(f32[128]{0:T(128)} %param.15) | copy-start | bytes 1540
  827.1 44.9 %copy-start.148 = (f32[128]{0:T(128)S(1)}, f32[128]{0:T(128)}, u32[]{:S(2)}) copy-start(f32[128]{0:T(128)} %param.16) | copy-start | bytes 1540
  827.1 44.9 %copy-start.149 = (f32[128]{0:T(128)S(1)}, f32[128]{0:T(128)}, u32[]{:S(2)}) copy-start(f32[128]{0:T(128)} %param.17) | copy-start | bytes 1540
  879.5 331.5 %copy-start.63 = (f32[2,98304]{1,0:T(2,128)S(1)}, f32[2,98304]{1,0:T(2,128)}, u32[]{:S(2)}) copy-start(f32[2,98304]{1,0:T(2,128)} %param.12) | copy-start | bytes 2359300
  879.5 331.5 %copy-start.86 = (f32[2,98304]{1,0:T(2,128)S(1)}, f32[2,98304]{1,0:T(2,128)}, u32[]{:S(2)}) copy-start(f32[2,98304]{1,0:T(2,128)} %param.13) | copy-start | bytes 2359300
  879.5 331.5 %copy-start.87 = (f32[2,98304]{1,0:T(2,128)S(1)}, f32[2,98304]{1,0:T(2,128)}, u32[]{:S(2)}) copy-start(f32[2,98304]{1,0:T(2,128)} %param.14) | copy-start | bytes 2359300
  (135 other events, 667.3 us)
Sparse Core Ops, SparseCore 0:
  11.5 98.6 all-gather.2
  818.6 390.3 all-reduce.5
where the time goes:
time: 1230 us; the launch traced here: 1220 us
  waiting for transfers between devices  362 us (29%)
  matrix products  356 us (29%)
  local copies, waits for them, and re-layouts  296 us (24%)
  other arithmetic  108 us (9%)
  blocking collectives  83.7 us (7%)
  between operations  17.3 us (1%)
    unnamed x3, waiting for transfers between devices  319 us
    dot_general x8, matrix products, matmul(): return jnp.dot(left_side, right_side, preferred_element_type=jnp.float32)  125 us
    unnamed x356, local copies, waits for them, and re-layouts  81.1 us
    dot_general x8, matrix products, input_grad(): lax.dot_general(grad_rows, weights, (((1,), (1,)), ((), ())), preferred_e...  79.3 us
    dot_general x8, matrix products, weight_grad(): lax.dot_general(inputs, grad_rows, (((0,), (0,)), ((), ())), preferred_el...  53.5 us
    slice x1, local copies, waits for them, and re-layouts, unpack(): flat_weights[cut_up:].reshape(hidden_width, model_width)  50.2 us
    all_gather x1, blocking collectives, on_device(): lax.all_gather(norm_par.astype(jnp.bfloat16), 'dp', axis=0, tiled=True)  43.1 us
    all_gather x1, waiting for transfers between devices, on_device(): lax.all_gather(params.astype(jnp.bfloat16), 'dp', axis=1, tiled=True)  42.9 us
  transfers between devices with their start and end apart: 2, of which 2 were waited for; matrix products, arithmetic and copies ran while one was open for 3% of the time, Pallas kernels for 0%

commit v1 on v0

v1 whole, which is shorter than its diff:
```python
from functools import partial

import jax
import jax.numpy as jnp
from jax import lax
from jax.experimental import pallas as pl
from jax.experimental.pallas import tpu as pltpu
from jax.sharding import PartitionSpec as P

HEADS = 8
HEAD_DIM = 64
FF = 2048
STEP = 7

norm_epsilon = 1e-05
beta_first = 0.9
beta_second = 0.999
learn_rate = 0.05
norm_rate = 0.5
weight_decay = 0.1
adam_floor = 1e-08
masked_score = -1e30

bf16 = jnp.bfloat16
f32 = jnp.float32
MIB = 2**20

SPATIAL_TILE = 256
TEMPORAL_TILE = 256
PATCH_GROUP = 16


def dot_nn(left, right):
    return lax.dot_general(left, right, (((1,), (0,)), ((), ())), preferred_element_type=f32)


def dot_nt(left, right):
    return lax.dot_general(left, right, (((1,), (1,)), ((), ())), preferred_element_type=f32)


def dot_tn(left, right):
    return lax.dot_general(left, right, (((0,), (0,)), ((), ())), preferred_element_type=f32)


def normalise(rows):
    center = rows - jnp.mean(rows, axis=-1, keepdims=True)
    spread = jnp.mean(center * center, axis=-1, keepdims=True)
    scale = lax.rsqrt(spread + norm_epsilon)
    return center * scale, scale


def fold_rows(rows):
    return jnp.sum(rows.reshape(-1, 8, rows.shape[-1]), axis=0)


def norm_backward(hat, scale, gain, grad):
    weighted = grad * gain
    mean_first = jnp.mean(weighted, axis=-1, keepdims=True)
    mean_second = jnp.mean(weighted * hat, axis=-1, keepdims=True)
    grad_rows = scale * (weighted - mean_first - hat * mean_second)
    return grad_rows, fold_rows(grad * hat), fold_rows(grad)


def gelu_pair(value):
    cumulative = 0.5 + 0.5 * lax.erf(value * 0.7071067811865476)
    density = jnp.exp(-0.5 * value * value) * 0.3989422804014327
    return value * cumulative, cumulative + value * density


def lane_halves(count):
    lane = lax.broadcasted_iota(jnp.int32, (count, 2 * HEAD_DIM), 1)
    return lane < HEAD_DIM


def only_head(pair, low_half, which):
    keep = low_half if which == 0 else jnp.logical_not(low_half)
    return jnp.where(keep, pair, jnp.zeros_like(pair))


def softmax(scores):
    top = jnp.max(scores, axis=-1, keepdims=True)
    powers = jnp.exp(scores - top)
    return powers * (1.0 / jnp.sum(powers, axis=-1, keepdims=True))


def attend(query, key, value, low_half, bias):
    query = query * jnp.asarray(HEAD_DIM**-0.5, bf16)
    weights = []
    mixture = None
    for which in range(2):
        scores = dot_nt(query, only_head(key, low_half, which))
        if bias is not None:
            scores = scores + bias
        soft = softmax(scores).astype(bf16)
        weights.append(soft)
        part = dot_nn(soft, only_head(value, low_half, which))
        mixture = part if mixture is None else mixture + part
    return weights, mixture.astype(bf16)


def attend_backward(query, key, value, grad, weights, low_half):
    scale = jnp.asarray(HEAD_DIM**-0.5, bf16)
    query = query * scale
    scaled_key = key * scale
    totals = [None, None, None]
    for which in range(2):
        soft = weights[which]
        grad_soft = dot_nt(grad, only_head(value, low_half, which))
        wide = soft.astype(f32)
        product = grad_soft * wide
        inner = jnp.sum(product, axis=-1, keepdims=True)
        grad_scores = (product - wide * inner).astype(bf16)
        parts = (
            dot_nn(grad_scores, only_head(scaled_key, low_half, which)),
            dot_tn(grad_scores, only_head(query, low_half, which)),
            dot_tn(soft, only_head(grad, low_half, which)),
        )
        totals = [p if t is None else t + p for t, p in zip(totals, parts)]
    return [t.astype(bf16) for t in totals]


def feed_forward(second, w_up, w_down, active_ref, slope_ref, chunk=512):
    hidden = w_up.shape[1]
    for start in range(0, hidden, chunk):
        active, slope = gelu_pair(dot_nn(second, w_up[:, start : start + chunk]))
        active_ref[:, start : start + chunk] = active.astype(bf16)
        slope_ref[:, start : start + chunk] = slope.astype(bf16)
    return dot_nn(active_ref[...], w_down[...])


def hidden_backward(branch, w_down, slope_ref, hidden_ref, chunk=512):
    hidden = w_down.shape[0]
    for start in range(0, hidden, chunk):
        grad = dot_nt(branch, w_down[start : start + chunk, :])
        slope = slope_ref[:, start : start + chunk].astype(f32)
        hidden_ref[:, start : start + chunk] = (grad * slope).astype(bf16)


def spatial_forward_kernel(
    x_ref, w_qkv, w_out, w_up, w_down, norm_ref,
    packed_ref, weights_ref, mixture_ref, middle_ref, active_ref, slope_ref, after_ref,
):
    width = x_ref.shape[1]
    rows = x_ref[...].astype(f32)
    hat, _ = normalise(rows)
    first = (hat * norm_ref[0:1] + norm_ref[1:2]).astype(bf16)
    packed_ref[...] = dot_nn(first, w_qkv[...]).astype(bf16)
    frame = weights_ref.shape[2]
    low_half = lane_halves(frame)
    for item in range(weights_ref.shape[0]):
        span = slice(item * frame, (item + 1) * frame)
        for pair in range(HEADS // 2):
            cut = [
                packed_ref[span, part * width + 128 * pair : part * width + 128 * (pair + 1)]
                for part in range(3)
            ]
            weights, mixture = attend(*cut, low_half, None)
            weights_ref[item, 2 * pair] = weights[0]
            weights_ref[item, 2 * pair + 1] = weights[1]
            mixture_ref[span, 128 * pair : 128 * (pair + 1)] = mixture
    middle = rows + dot_nn(mixture_ref[...], w_out[...])
    middle_ref[...] = middle
    hat, _ = normalise(middle)
    second = (hat * norm_ref[2:3] + norm_ref[3:4]).astype(bf16)
    after_ref[...] = middle + feed_forward(second, w_up, w_down, active_ref, slope_ref)


def whole(shape):
    return pl.BlockSpec(shape, lambda *_: (0,) * len(shape), pipeline_mode=pl.Buffered(1))


def tiles(tile, *rest):
    return pl.BlockSpec((tile, *rest), lambda i: (i,) + (0,) * len(rest))


def spatial_forward(x, weights, norms, frame):
    tokens, width = x.shape
    hidden = weights[2].shape[1]
    tile = SPATIAL_TILE
    frames = tile // frame
    return pl.pallas_call(
        spatial_forward_kernel,
        grid=(tokens // tile,),
        in_specs=[tiles(tile, width)] + [whole(w.shape) for w in weights] + [whole(norms.shape)],
        out_specs=[
            tiles(tile, 3 * width),
            tiles(frames, HEADS, frame, frame),
            tiles(tile, width),
            tiles(tile, width),
            tiles(tile, hidden),
            tiles(tile, hidden),
            tiles(tile, width),
        ],
        out_shape=[
            jax.ShapeDtypeStruct((tokens, 3 * width), bf16),
            jax.ShapeDtypeStruct((tokens // frame, HEADS, frame, frame), bf16),
            jax.ShapeDtypeStruct((tokens, width), bf16),
            jax.ShapeDtypeStruct((tokens, width), f32),
            jax.ShapeDtypeStruct((tokens, hidden), bf16),
            jax.ShapeDtypeStruct((tokens, hidden), bf16),
            jax.ShapeDtypeStruct((tokens, width), f32),
        ],
        compiler_params=pltpu.CompilerParams(vmem_limit_bytes=56 * MIB),
    )(x, *weights, norms)


def weight_grads(first, grad_packed, mixture, attn, second, grad_hidden, active, branch, outs, chunk=512):
    sides = ((first, grad_packed), (mixture, attn), (second, grad_hidden), (active, branch))
    for (left, right), out in zip(sides, outs):
        for start in range(0, out.shape[1], chunk):
            out[:, start : start + chunk] = dot_tn(
                left[...], right[:, start : start + chunk]
            ).astype(out.dtype)


def temporal_kernel(
    length_ref, rows_ref, cotangent_ref, w_qkv, w_out, w_up, w_down, norm_ref,
    result_ref, before_ref, g_qkv, g_out, g_up, g_down, g_norm,
    packed, slope, weights_buf, grad_mix,
    first_all, packed_all, mixture_all, attn_all, second_all, hidden_all, active_all, branch_all,
):
    step = pl.program_id(0)
    steps, patches, width = rows_ref.shape
    tile = steps * patches
    here = pl.ds(pl.multiple_of(step * tile, tile), tile)
    length = length_ref[0]
    group = PATCH_GROUP
    count = steps * group

    @pl.when(step == 0)
    def _():
        g_norm[...] = jnp.zeros_like(g_norm)

    row = lax.broadcasted_iota(jnp.int32, (count, count), 0)
    column = lax.broadcasted_iota(jnp.int32, (count, count), 1)
    seen = (row % group == column % group) & (column // group <= row // group)
    seen = seen & (column // group < length)
    bias = jnp.where(seen, 0.0, masked_score)
    low_half = lane_halves(count)

    rows = rows_ref[...].reshape(tile, width)
    hat, _ = normalise(rows)
    first = (hat * norm_ref[0:1] + norm_ref[1:2]).astype(bf16)
    first_all[here, :] = first
    packed[...] = dot_nn(first, w_qkv[...]).astype(bf16).reshape(packed.shape)

    mixture_view = mixture_all.at[here, :]

    def cut(source, part, place, pair):
        start = part * width + 128 * pair
        return source[:, place : place + group, start : start + 128].reshape(count, 128)

    for place in range(0, patches, group):
        for pair in range(HEADS // 2):
            weights, mixture = attend(
                *[cut(packed, part, place, pair) for part in range(3)], low_half, bias
            )
            for which in range(2):
                weights_buf[place // group, 2 * pair + which] = weights[which]
            grad_mix[:, place : place + group, 128 * pair : 128 * (pair + 1)] = mixture.reshape(
                steps, group, 128
            )
    mixture = grad_mix[...].reshape(tile, width)
    mixture_all[here, :] = mixture
    middle = rows + dot_nn(mixture, w_out[...])
    hat, scale = normalise(middle)
    second = (hat * norm_ref[2:3] + norm_ref[3:4]).astype(bf16)
    second_all[here, :] = second
    after = middle + feed_forward(second, w_up, w_down, active_all.at[here, :], slope)
    result_ref[...] = after.reshape(result_ref.shape)

    slot = lax.broadcasted_iota(jnp.int32, rows_ref.shape, 0)
    live = (slot < length).astype(f32)
    grad_after = (cotangent_ref[...].astype(f32) * live).reshape(tile, width)
    branch = grad_after.astype(bf16)
    branch_all[here, :] = branch
    hidden_backward(branch, w_down, slope, hidden_all.at[here, :])
    grad_second = dot_nt(hidden_all[here, :], w_up[...])
    hat, scale = normalise(middle)
    grad_rows, gain, shift = norm_backward(hat, scale, norm_ref[2:3], grad_second)
    g_norm[2] += gain
    g_norm[3] += shift
    grad_middle = grad_after + grad_rows
    attn = grad_middle.astype(bf16)
    attn_all[here, :] = attn
    grad_mix[...] = dot_nt(attn, w_out[...]).astype(bf16).reshape(grad_mix.shape)
    for place in range(0, patches, group):
        for pair in range(HEADS // 2):
            grads = attend_backward(
                *[cut(packed, part, place, pair) for part in range(3)],
                cut(grad_mix, 0, place, pair),
                [weights_buf[place // group, 2 * pair + which] for which in range(2)],
                low_half,
            )
            for part in range(3):
                start = part * width + 128 * pair
                packed[:, place : place + group, start : start + 128] = grads[part].reshape(
                    steps, group, 128
                )
    grad_packed = packed[...].reshape(tile, 3 * width)
    packed_all[here, :] = grad_packed
    grad_first = dot_nt(grad_packed, w_qkv[...])
    hat, scale = normalise(rows)
    grad_rows, gain, shift = norm_backward(hat, scale, norm_ref[0:1], grad_first)
    g_norm[0] += gain
    g_norm[1] += shift
    before_ref[...] = (grad_middle + grad_rows).reshape(before_ref.shape)

    @pl.when(step == pl.num_programs(0) - 1)
    def _():
        weight_grads(
            first_all, packed_all, mixture_all, attn_all, second_all, hidden_all, active_all,
            branch_all, (g_qkv, g_out, g_up, g_down),
        )


def temporal_block(length, rows, cotangent, weights, norms):
    steps, patches, width = rows.shape
    tokens = steps * patches
    hidden = weights[2].shape[1]
    part = TEMPORAL_TILE // steps
    slab = pl.BlockSpec((steps, part, width), lambda i: (0, i, 0))
    return pl.pallas_call(
        temporal_kernel,
        grid=(patches // part,),
        in_specs=[pl.BlockSpec(memory_space=pltpu.SMEM), slab, slab]
        + [whole(w.shape) for w in weights]
        + [whole(norms.shape)],
        out_specs=[slab, slab] + [whole(w.shape) for w in weights] + [whole((4, 8, width))],
        out_shape=[
            jax.ShapeDtypeStruct(rows.shape, f32),
            jax.ShapeDtypeStruct(rows.shape, f32),
        ]
        + [jax.ShapeDtypeStruct(w.shape, bf16) for w in weights]
        + [jax.ShapeDtypeStruct((4, 8, width), f32)],
        scratch_shapes=[
            pltpu.VMEM((steps, part, 3 * width), bf16),
            pltpu.VMEM((TEMPORAL_TILE, hidden), bf16),
            pltpu.VMEM((part // PATCH_GROUP, HEADS, steps * PATCH_GROUP, steps * PATCH_GROUP), bf16),
            pltpu.VMEM((steps, part, width), bf16),
            pltpu.VMEM((tokens, width), bf16),
            pltpu.VMEM((tokens, 3 * width), bf16),
            pltpu.VMEM((tokens, width), bf16),
            pltpu.VMEM((tokens, width), bf16),
            pltpu.VMEM((tokens, width), bf16),
            pltpu.VMEM((tokens, hidden), bf16),
            pltpu.VMEM((tokens, hidden), bf16),
            pltpu.VMEM((tokens, width), bf16),
        ],
        compiler_params=pltpu.CompilerParams(vmem_limit_bytes=62 * MIB),
    )(length, rows, cotangent, *weights, norms)


def spatial_backward_kernel(
    x_ref, grad_ref, packed_ref, weights_ref, middle_ref, slope_ref, mixture_all, active_all,
    w_qkv, w_out, w_up, w_down, norm_ref,
    before_ref, g_qkv, g_out, g_up, g_down, g_norm,
    grad_mix, first_all, packed_all, attn_all, second_all, hidden_all, branch_all,
):
    step = pl.program_id(0)
    tile, width = x_ref.shape
    here = pl.ds(pl.multiple_of(step * tile, tile), tile)

    @pl.when(step == 0)
    def _():
        g_norm[...] = jnp.zeros_like(g_norm)

    grad_after = grad_ref[...]
    branch = grad_after.astype(bf16)
    branch_all[here, :] = branch
    hidden_backward(branch, w_down, slope_ref, hidden_all.at[here, :])
    grad_second = dot_nt(hidden_all[here, :], w_up[...])
    hat, scale = normalise(middle_ref[...])
    second_all[here, :] = (hat * norm_ref[2:3] + norm_ref[3:4]).astype(bf16)
    grad_rows, gain, shift = norm_backward(hat, scale, norm_ref[2:3], grad_second)
    g_norm[2] += gain
    g_norm[3] += shift
    grad_middle = grad_after + grad_rows
    attn = grad_middle.astype(bf16)
    attn_all[here, :] = attn
    grad_mix[...] = dot_nt(attn, w_out[...]).astype(bf16)
    frame = weights_ref.shape[2]
    low_half = lane_halves(frame)
    for item in range(weights_ref.shape[0]):
        span = slice(item * frame, (item + 1) * frame)
        there = pl.ds(pl.multiple_of(step * tile + item * frame, frame), frame)
        for pair in range(HEADS // 2):
            grads = attend_backward(
                *[
                    packed_ref[span, part * width + 128 * pair : part * width + 128 * (pair + 1)]
                    for part in range(3)
                ],
                grad_mix[span, 128 * pair : 128 * (pair + 1)],
                [weights_ref[item, 2 * pair + which] for which in range(2)],
                low_half,
            )
            for part in range(3):
                start = part * width + 128 * pair
                packed_all[there, start : start + 128] = grads[part]
    grad_first = dot_nt(packed_all[here, :], w_qkv[...])
    hat, scale = normalise(x_ref[...].astype(f32))
    first_all[here, :] = (hat * norm_ref[0:1] + norm_ref[1:2]).astype(bf16)
    grad_rows, gain, shift = norm_backward(hat, scale, norm_ref[0:1], grad_first)
    g_norm[0] += gain
    g_norm[1] += shift
    before_ref[...] = grad_middle + grad_rows

    @pl.when(step == pl.num_programs(0) - 1)
    def _():
        weight_grads(
            first_all, packed_all, mixture_all, attn_all, second_all, hidden_all, active_all,
            branch_all, (g_qkv, g_out, g_up, g_down),
        )


def spatial_backward(x, grad, kept, weights, norms):
    packed, soft, mixture, middle, active, slope = kept
    tokens, width = x.shape
    hidden = weights[2].shape[1]
    frame = soft.shape[2]
    tile = SPATIAL_TILE
    return pl.pallas_call(
        spatial_backward_kernel,
        grid=(tokens // tile,),
        in_specs=[
            tiles(tile, width),
            tiles(tile, width),
            tiles(tile, 3 * width),
            tiles(tile // frame, HEADS, frame, frame),
            tiles(tile, width),
            tiles(tile, hidden),
            whole(mixture.shape),
            whole(active.shape),
        ]
        + [whole(w.shape) for w in weights]
        + [whole(norms.shape)],
        out_specs=[tiles(tile, width)]
        + [whole(w.shape) for w in weights]
        + [whole((4, 8, width))],
        out_shape=[jax.ShapeDtypeStruct((tokens, width), f32)]
        + [jax.ShapeDtypeStruct(w.shape, bf16) for w in weights]
        + [jax.ShapeDtypeStruct((4, 8, width), f32)],
        scratch_shapes=[
            pltpu.VMEM((tile, width), bf16),
            pltpu.VMEM((tokens, width), bf16),
            pltpu.VMEM((tokens, 3 * width), bf16),
            pltpu.VMEM((tokens, width), bf16),
            pltpu.VMEM((tokens, width), bf16),
            pltpu.VMEM((tokens, hidden), bf16),
            pltpu.VMEM((tokens, width), bf16),
        ],
        compiler_params=pltpu.CompilerParams(vmem_limit_bytes=62 * MIB),
    )(x, grad, packed, soft, middle, slope, mixture, active, *weights, norms)


def unpack(flat_weights, model_width, hidden_width):
    cut_qkv = 3 * model_width * model_width
    cut_out = 4 * model_width * model_width
    cut_up = cut_out + model_width * hidden_width
    return (
        flat_weights[:cut_qkv].reshape(model_width, 3 * model_width),
        flat_weights[cut_qkv:cut_out].reshape(model_width, model_width),
        flat_weights[cut_out:cut_up].reshape(model_width, hidden_width),
        flat_weights[cut_up:].reshape(hidden_width, model_width),
    )


def adamw(param_value, moment, second, grad_total, step_value, rate, decay_rate):
    moment_next = beta_first * moment + (1.0 - beta_first) * grad_total
    second_next = beta_second * second + (1.0 - beta_second) * grad_total * grad_total
    moment_hat = moment_next / (1.0 - beta_first**step_value)
    second_hat = second_next / (1.0 - beta_second**step_value)
    param_next = param_value - rate * (
        moment_hat / (jnp.sqrt(second_hat) + adam_floor) + decay_rate * param_value
    )
    return (param_next, moment_next, second_next)


def on_device(
    clip_tokens,
    cotangent,
    lengths,
    params,
    param_moment,
    param_second,
    norm_par,
    norm_moment,
    norm_second,
):
    clip_count, step_slots, patch_count, model_width = clip_tokens.shape
    shards = lax.axis_size("dp")
    gathered = lax.all_gather(params.astype(bf16), "dp", axis=1, tiled=True)
    norm_whole = lax.all_gather(norm_par.astype(bf16), "dp", axis=0, tiled=True)
    norm_table = norm_whole.astype(f32).reshape(2, 4, model_width)
    spatial_weights = unpack(gathered[0], model_width, FF)
    temporal_weights = unpack(gathered[1], model_width, FF)
    x = clip_tokens.reshape(-1, model_width)
    *kept, after = spatial_forward(x, spatial_weights, norm_table[0], patch_count)
    result, grad_after, *temporal_grads, temporal_norm = temporal_block(
        lengths,
        after.reshape(step_slots, patch_count, model_width),
        cotangent.reshape(step_slots, patch_count, model_width),
        temporal_weights,
        norm_table[1],
    )
    grad_before, *spatial_grads, spatial_norm = spatial_backward(
        x, grad_after.reshape(-1, model_width), kept, spatial_weights, norm_table[0]
    )

    def scatter(grads):
        flat = jnp.concatenate([g.reshape(-1) for g in grads])
        return lax.psum_scatter(flat, "dp", scatter_dimension=0, tiled=True).astype(f32)

    weight_sum = jnp.stack([scatter(spatial_grads), scatter(temporal_grads)])
    norm_grad = jnp.stack([spatial_norm, temporal_norm]).sum(axis=2).reshape(-1)
    norm_sum = lax.psum_scatter(norm_grad, "dp", scatter_dimension=0, tiled=True)
    step_value = float(STEP)
    new_params, new_moment, new_second = adamw(
        params, param_moment, param_second, weight_sum, step_value, learn_rate, weight_decay
    )
    new_norm, new_norm_moment, new_norm_second = adamw(
        norm_par, norm_moment, norm_second, norm_sum, step_value, norm_rate, 0.0
    )
    return (
        result.reshape(clip_tokens.shape),
        grad_before.reshape(clip_tokens.shape),
        new_params,
        new_moment,
        new_second,
        new_params.astype(bf16),
        new_norm,
        new_norm_moment,
        new_norm_second,
    )


def solution(mesh):
    placed = (
        P("dp", None, None, None),
        P("dp", None, None, None),
        P("dp"),
        P(None, "dp"),
        P(None, "dp"),
        P(None, "dp"),
        P("dp"),
        P("dp"),
        P("dp"),
    )
    return jax.shard_map(
        on_device,
        mesh=mesh,
        in_specs=placed,
        out_specs=(
            P("dp", None, None, None),
            P("dp", None, None, None),
            P(None, "dp"),
            P(None, "dp"),
            P(None, "dp"),
            P(None, "dp"),
            P("dp"),
            P("dp"),
            P("dp"),
        ),
        check_vma=False,
    )
```

time: 1230 us -> 746 us (0.61)
  matrix products: 356 us -> 0 us
  Pallas kernels: 0 us -> 216 us
  local copies, waits for them, and re-layouts: 296 us -> 149 us
  waiting for transfers between devices: 362 us -> 244 us
  other arithmetic: 108 us -> 30.4 us
    dot_general x78 -> x0, matrix products: 356 us -> none  [the longest x8 125 us: matmul(): return jnp.dot(left_side, right_side, preferred_element_type=jnp.float32)]
    pallas_call x0 -> x3, Pallas kernels: none -> 216 us  [the longest x1 114 us: temporal_block(): pl.pallas_call(temporal_kernel, grid=(patches // part,), in_specs=[pl.Blo...]
    unnamed x3, waiting for transfers between devices: 319 us -> 189 us
    unnamed x356 -> x33, local copies, waits for them, and re-layouts: 81.1 us -> 14 us
    another operation x6 -> x2, local copies, waits for them, and re-layouts: 37.5 us -> 0.41 us  [on_device(): weight_sum = jnp.stack([scatter(spatial_grads), scatter(temporal_grads)])]
    convert_element_type x4 -> x0, local copies, waits for them, and re-layouts: 23.1 us -> none  [the longest x1 8.73 us: block_forward(): packed = matmul(normed, w_qkv).astype(jnp.bfloat16)]
    convert_element_type x15 -> x3, other arithmetic: 28.9 us -> 6.6 us  [the longest x1 4.43 us: on_device(): new_params.astype(bf16)]
    dot_general x3 -> x0, local copies, waits for them, and re-layouts: 21.9 us -> none  [the longest x1 7.74 us: temporal_backward(): jnp.einsum('chtup,cuphe->ctphe', grad_scores, keys, preferred_element_typ...]
  transfers between devices with their start and end apart: 2 -> 2, of which waited for: 2 -> 2; matrix products, arithmetic and copies ran while one was open for 3% -> 0% of each run, Pallas kernels for 0% -> 0%
where the time goes in v1:
time: 746 us; the launch traced here: 737 us
  waiting for transfers between devices  244 us (33%)
  Pallas kernels  216 us (29%)
  local copies, waits for them, and re-layouts  149 us (20%)
  blocking collectives  83.7 us (11%)
  other arithmetic  30.4 us (4%)
  between operations  15.1 us (2%)
    unnamed x3, waiting for transfers between devices  189 us
    pallas_call x1, Pallas kernels, temporal_block(): pl.pallas_call(temporal_kernel, grid=(patches // part,), in_specs=[pl.Blo...  114 us
    pallas_call x1, Pallas kernels, spatial_backward(): pl.pallas_call(spatial_backward_kernel, grid=(tokens // tile,), in_specs=...  60.4 us
    all_gather x1, waiting for transfers between devices, on_device(): gathered = lax.all_gather(params.astype(bf16), 'dp', axis=1, tiled=True)  55 us
    slice x1, local copies, waits for them, and re-layouts, unpack(): flat_weights[cut_up:].reshape(hidden_width, model_width)  50 us
    all_gather x1, blocking collectives, on_device(): norm_whole = lax.all_gather(norm_par.astype(bf16), 'dp', axis=0, tiled=True)  43.1 us
    pallas_call x1, Pallas kernels, spatial_forward(): pl.pallas_call(spatial_forward_kernel, grid=(tokens // tile,), in_specs=[...  41 us
    unnamed x1, blocking collectives  40.5 us
  transfers between devices with their start and end apart: 2, of which 2 were waited for; matrix products, arithmetic and copies ran while one was open for 0% of the time, Pallas kernels for 0%

profile of v1, /device:TPU:0, one launch (start us, length us, event | category | flops | bytes accessed | tf_op | source)
XLA Modules:
  0.0 737.4 jit_solution(15790213130542090)
XLA Ops:
  10.1 43.1 %all-gather = bf16[32,1,128]{2,1,0:T(2,128)(2,1)S(1)} all-gather(bf16[1,1,128]{2,1,0:T(2,128)(2,1)S(1)} %convert_bitcast_fusion), channel_id=1, replica_groups=mesh['dp'=32] {'dp'}, dimensions={0}, use_global_device_ids=true | all-gather | bytes 8448 | tf_op jit(solution)/shard_map/all_gather | solution.py:493
  55.2 55.0 %all-gather.3.cloned.1.call-done = bf16[2,3145728]{1,0:T(2,128)(2,1)} async-done(((bf16[2,98304]{1,0:T(2,128)(2,1)}), bf16[2,3145728]{1,0:T(2,128)(2,1)}) %all-gather.3.cloned.1.call-update) | async-done | bytes 12582928 | tf_op jit(solution)/shard_map/all_gather | solution.py:492
  110.2 50.0 %slice_reduce_fusion = (bf16[1048576]{0:T(1024)(128)(2,1)S(1)}, bf16[1048576]{0:T(1024)(128)(2,1)}, bf16[1048576]{0:T(1024)(128)(2,1)}, bf16[1048576]{0:T(1024)(128)(2,1)}) fusion(bf16[2,3145728]{1,0:T(2,128)(2,1)} %all-gather.3.cloned.1.call-done), kind=kLoop, calls=%fused_computation.2 | loop fusion | bytes 16777216 | tf_op jit(solution)/shard_map/slice | solution.py:464
  160.1 4.2 reshape.127.w_up
  164.3 4.4 reshape.128.w_down
  168.7 36.2 %slice_reduce_fusion.4 = (bf16[786432]{0:T(1024)(128)(2,1)}, bf16[786432]{0:T(1024)(128)(2,1)}) fusion(bf16[2,3145728]{1,0:T(2,128)(2,1)} %all-gather.3.cloned.1.call-done), kind=kLoop, calls=%fused_computation.6 | loop fusion | bytes 6291456 | tf_op jit(solution)/shard_map/slice | solution.py:461
  204.9 4.3 reshape.125.w_qkv
  209.2 12.5 %slice_reduce_fusion.6 = (bf16[262144]{0:T(1024)(128)(2,1)S(1)}, bf16[262144]{0:T(1024)(128)(2,1)S(1)}) fusion(bf16[2,3145728]{1,0:T(2,128)(2,1)} %all-gather.3.cloned.1.call-done), kind=kLoop, calls=%fused_computation.9 | loop fusion | bytes 2097152 | tf_op jit(solution)/shard_map/slice | solution.py:462
  222.8 4.2 reshape.133.w_up
  226.9 2.6 reshape.134.w_down
  229.5 4.3 reshape.131.w_qkv
  234.9 41.0 %shard_map.160 = (bf16[2048,1536]{1,0:T(8,128)(2,1)}, bf16[8,8,256,256]{3,2,1,0:T(8,128)(2,1)}, bf16[2048,512]{1,0:T(8,128)(2,1)}, f32[2048,512]{1,0:T(8,128)}, ...) custom-call(bf16[2048,512]{1,0:T(8,128)(2,1)} %bitcast.28, ...), custom_call_target="tpu_custom_call" | custom-call | tf_op jit(solution)/shard_map/pallas_call | solution.py:181
  275.9 114.2 %shard_map.161 = (f32[8,256,512]{2,1,0:T(8,128)}, f32[8,256,512]{2,1,0:T(8,128)}, bf16[512,1536]{1,0:T(8,128)(2,1)}, bf16[512,512]{1,0:T(8,128)(2,1)}, bf16[512,...) custom-call(s32[1]{0:T(128)S(6)} %copy.27.length_ref, f32[8,256,512]{2,1,0:T(8,128)} %bitcast.30, ...), custom_call_target="tpu_custom_call" | custom-call | tf_op jit(solution)/shard_map/pallas_call | solution.py:323
  390.2 60.4 %shard_map.162 = (f32[2048,512]{1,0:T(8,128)}, bf16[512,1536]{1,0:T(8,128)(2,1)}, bf16[512,512]{1,0:T(8,128)(2,1)}, bf16[512,2048]{1,0:T(8,128)(2,1)}, bf16[2048,512]{1,0:T(8,128)(2,1)}, /*index=5*/f32[4,8,512]{2,1,0:T(8,128)}) custom-call(bf16[2048,512]{1,0:T(8,128)(2,1)} %bitcast.29, f32[2048,512]{1,0:T(8,128)} %bitcast.31, ...), custom_call_target="tpu_custom_call" | custom-call | tf_op jit(solution)/shard_map/pallas_call | solution.py:422
  450.6 2.3 copy.19
  453.0 2.4 copy.20
  455.4 4.3 reshape.138
  459.9 3.7 copy.22
  463.6 2.4 copy.23
  466.0 4.3 reshape.142
  470.5 22.5 %pad_maximum_fusion = (bf16[3145728]{0:T(1024)(128)(2,1)}, bf16[3145728]{0:T(1024)(128)(2,1)}) fusion(bf16[1048576]{0:T(1024)(128)(2,1)} %bitcast.25, bf16[1048576]{0:T(1024)(128)(2,1)S(1)} %bitcast.24, bf16[262144]{0:T(1024)(128)(2,1)S(1)} %bitcast.32, bf16[786432]{0:T(1024)(128)(2,1)} %reshape.138, bf16[1048576]{0:T(1024)(128)(2,1)} %bitcast.27, ...), kind=kLoop, calls=%fused_computation | loop fusion | flops 50331648 | bytes 25165824 | tf_op jit(solution)/shard_map/concatenate | solution.py:511
  493.9 40.5 %all-reduce.2 = f32[4096]{0:T(1024)S(1)} all-reduce(f32[4096]{0:T(1024)S(1)} %bitcast.44), channel_id=4, replica_groups=mesh['dp'=32] {'dp'}, use_global_device_ids=true, to_apply=%region_3.0.clone | all-reduce | flops 4096 | bytes 32768
  535.1 188.5 %all-reduce.6.cloned.1.call-done = (bf16[3145728]{0:T(1024)(128)(2,1)}, bf16[3145728]{0:T(1024)(128)(2,1)}) async-done(((bf16[3145728]{0:T(1024)(128)(2,1)}, bf16[3145728]{0:T(1024)(128)(2,1)}), (bf16[3145728]{0:T(1024)(128)(2,1)}, bf16[3145728]{0:T(1024)(128)(2,1)})) %all-reduce.6.cloned.1.call-update) | async-done | bytes 12582928
  725.9 4.4 fusion.4
  (45 shorter events, 10.6 us)
Async XLA Ops:
  7.2 103.0 %all-gather.3.cloned.1.call-start = ((), (), s32[]{:S(2)}) async-start(), calls=%async_computation | async-start | bytes 12976128 | tf_op jit(solution)/shard_map/all_gather | solution.py:492
  9.4 714.2 %all-reduce.6.cloned.1.call-start = ((), (), s32[]{:S(2)}) async-start(), calls=%async_computation.1 | async-start | bytes 25165824
  450.6 2.4 copy-start.2
  452.9 6.8 copy-start.6
  459.7 3.9 copy-start.1
  463.6 6.7 copy-start.5
  493.0 0.8 copy-start.7
  493.0 0.9 copy-start.8
  493.0 41.4 %copy-start.9 = (f32[128]{0:T(128)S(1)}, f32[128]{0:T(128)}, u32[]{:S(2)}) copy-start(f32[128]{0:T(128)} %param.15) | copy-start | bytes 1540
  493.0 41.4 %copy-start.10 = (f32[128]{0:T(128)S(1)}, f32[128]{0:T(128)}, u32[]{:S(2)}) copy-start(f32[128]{0:T(128)} %param.16) | copy-start | bytes 1540
  493.1 41.4 %copy-start.11 = (f32[128]{0:T(128)S(1)}, f32[128]{0:T(128)}, u32[]{:S(2)}) copy-start(f32[128]{0:T(128)} %param.17) | copy-start | bytes 1540
  493.1 232.8 %copy-start = (f32[2,98304]{1,0:T(2,128)S(1)}, f32[2,98304]{1,0:T(2,128)}, u32[]{:S(2)}) copy-start(f32[2,98304]{1,0:T(2,128)} %param.12) | copy-start | bytes 2359300
  493.1 232.8 %copy-start.3 = (f32[2,98304]{1,0:T(2,128)S(1)}, f32[2,98304]{1,0:T(2,128)}, u32[]{:S(2)}) copy-start(f32[2,98304]{1,0:T(2,128)} %param.13) | copy-start | bytes 2359300
  493.1 232.8 %copy-start.4 = (f32[2,98304]{1,0:T(2,128)S(1)}, f32[2,98304]{1,0:T(2,128)}, u32[]{:S(2)}) copy-start(f32[2,98304]{1,0:T(2,128)} %param.14) | copy-start | bytes 2359300
Sparse Core Ops, SparseCore 0:
  11.5 98.6 all-gather.2
  493.2 230.2 all-reduce.5

commit v2 on v1

--- a/solution.py
+++ b/solution.py
@@ -204,21 +204,503 @@
     )(x, *weights, norms)
 
 
-def weight_grads(first, grad_packed, mixture, attn, second, grad_hidden, active, branch, outs, chunk=512):
+MESH_IDS = pl.DeviceIdType.MESH
+LANES = 128
+ROW_TILE = 16
+
+
+def matrix_shapes(width, hidden):
+    return ((width, 3 * width), (width, width), (width, hidden), (hidden, width))
+
+
+def shard_plan(shards, width, hidden):
+    plan = []
+    base = 0
+    regions = []
+    for index, (rows, columns) in enumerate(matrix_shapes(width, hidden)):
+        regions.append((index, base, rows, columns))
+        base += rows * columns
+    if base % shards:
+        return None
+    size = base // shards
+    for device in range(shards):
+        low, high = device * size, (device + 1) * size
+        halves = ([], [])
+        for index, start, rows, columns in regions:
+            first, last = max(low, start), min(high, start + rows * columns)
+            if first >= last:
+                continue
+            if (first - start) % columns or (last - start) % columns:
+                return None
+            row, count = (first - start) // columns, (last - first) // columns
+            if row % ROW_TILE or count % ROW_TILE:
+                return None
+            stride = columns // LANES
+            for block in range(stride):
+                halves[2 * block // stride].append(
+                    (index, row, count, block, (first - low) // LANES + block, stride)
+                )
+        place = 0
+        entries = []
+        for item in halves[0] + halves[1]:
+            entries.append(item + (place,))
+            place += item[2]
+        plan.append(entries)
+    return plan
+
+
+def by_pattern(plan):
+    groups = {}
+    for device, entries in enumerate(plan):
+        layout = tuple((e[2], e[4], e[5], e[6]) for e in entries)
+        ranges = groups.setdefault(layout, [])
+        if ranges and ranges[-1][1] == device:
+            ranges[-1][1] = device + 1
+        else:
+            ranges.append([device, device + 1])
+    return list(groups.items())
+
+
+def on_pattern(plan, me, body):
+    for layout, ranges in by_pattern(plan):
+        inside = None
+        for low, high in ranges:
+            test = (me >= low) & (me < high)
+            inside = test if inside is None else inside | test
+
+        @pl.when(inside)
+        def _(layout=layout):
+            body(layout)
+
+
+class Place:
+    def __init__(self, me):
+        self.me = me
+        self.c = lax.rem(me, 2)
+        self.x = lax.rem(me // 2, 2)
+        self.y = lax.rem(me // 4, 2)
+        self.z = me // 8
+
+    def device(self, z, y, x, c):
+        return ((z * 2 + y) * 2 + x) * 2 + c
+
+    @property
+    def sibling(self):
+        return self.device(self.z, self.y, self.x, 1 - self.c)
+
+    @property
+    def across_x(self):
+        return self.device(self.z, self.y, 1 - self.x, self.c)
+
+    @property
+    def across_y(self):
+        return self.device(self.z, 1 - self.y, self.x, self.c)
+
+    def plane(self, z):
+        return self.device(z, self.y, self.x, self.c)
+
+
+def remote(src, dst, send, recv, device):
+    return pltpu.make_async_remote_copy(
+        src_ref=src, dst_ref=dst, send_sem=send, recv_sem=recv, device_id=(device,), device_id_type=MESH_IDS
+    )
+
+
+def enter(place):
+    barrier = pltpu.get_barrier_semaphore()
+    partners = [place.sibling, place.across_x, place.across_y]
+    partners += [place.plane(lax.rem(place.z + k, 4)) for k in range(1, 4)]
+    for device in partners:
+        pl.semaphore_signal(barrier, inc=1, device_id=(device,), device_id_type=MESH_IDS)
+    pl.semaphore_wait(barrier, len(partners))
+
+
+HALF = 384
+SHARD = 784
+
+
+class Gather:
+    SEMS = 9
+
+    def __init__(self, place, held, send, recv):
+        self.p, self.held, self.send, self.recv = place, held, send, recv
+
+    def along_z(self, k):
+        p = self.p
+        here = self.held.at[p.z, p.y, p.x, p.c]
+        return remote(here, here, self.send.at[0, k - 1], self.recv.at[0, p.z], p.plane(lax.rem(p.z + k, 4)))
+
+    def start_z(self):
+        for k in range(1, 4):
+            self.along_z(k).start()
+
+    def wait_z(self, q):
+        p = self.p
+
+        @pl.when(q != p.z)
+        def _():
+            there = self.held.at[q, p.y, p.x, p.c]
+            remote(there, there, self.send.at[0, 0], self.recv.at[0, q], p.me).wait_recv()
+
+    def first(self, q):
+        p, h = self.p, self.held
+        a = h.at[q, p.y, p.x, p.c, pl.ds(0, HALF)]
+        b = h.at[q, p.y, p.x, p.c, pl.ds(HALF, SHARD - HALF)]
+        return (
+            remote(a, a, self.send.at[1, q], self.recv.at[1, q], p.across_x),
+            remote(b, b, self.send.at[2, q], self.recv.at[2, q], p.across_y),
+        )
+
+    def second(self, q):
+        p, h = self.p, self.held
+        a = h.at[q, p.y, :, p.c, pl.ds(0, HALF)]
+        b = h.at[q, :, p.x, p.c, pl.ds(HALF, SHARD - HALF)]
+        return (
+            remote(a, a, self.send.at[3, q], self.recv.at[3, q], p.across_y),
+            remote(b, b, self.send.at[4, q], self.recv.at[4, q], p.across_x),
+        )
+
+    def third(self, q):
+        p, h = self.p, self.held
+        a = h.at[q, :, :, p.c]
+        return (remote(a, a, self.send.at[5, q], self.recv.at[5, q], p.sibling),)
+
+    def begin_first(self, q):
+        self.wait_z(q)
+        for copy in self.first(q):
+            copy.start()
+
+    def begin_second(self, q):
+        for copy in self.first(q):
+            copy.wait_recv()
+        for copy in self.second(q):
+            copy.start()
+
+    def begin_third(self, q):
+        for copy in self.second(q):
+            copy.wait_recv()
+        for copy in self.third(q):
+            copy.start()
+
+    def finish(self, q):
+        for copy in self.third(q):
+            copy.wait_recv()
+
+    def drain(self):
+        for k in range(1, 4):
+            self.along_z(k).wait_send()
+        for q in range(4):
+            for copy in self.first(q) + self.second(q) + self.third(q):
+                copy.wait_send()
+
+
+def load_shard(plan, me, shard_ref, norm_ref, held_here):
+    def body(layout):
+        for count, flat, stride, place in layout:
+            held_here[pl.ds(place, count), :] = shard_ref[pl.ds(flat, count, stride), :].astype(bf16)
+
+    on_pattern(plan, me, body)
+    held_here[SHARD - ROW_TILE :, :] = jnp.broadcast_to(norm_ref[...], (ROW_TILE, LANES)).astype(bf16)
+
+
+def coordinates(device):
+    return device // 8, device // 4 % 2, device // 2 % 2, device % 2
+
+
+def assemble(plan, held, outs, planes):
+    for device, entries in enumerate(plan):
+        z, y, x, c = coordinates(device)
+        if z not in planes:
+            continue
+        for index, row, count, block, _, _, place in entries:
+            outs[index][row : row + count, LANES * block : LANES * (block + 1)] = held[
+                z, y, x, c, place : place + count, :
+            ]
+
+
+def assemble_norms(shards, held, norm_out):
+    per_row = norm_out.shape[1] // LANES
+    for device in range(shards):
+        z, y, x, c = coordinates(device)
+        row, column = device // per_row, device % per_row
+        norm_out[row : row + 1, LANES * column : LANES * (column + 1)] = held[
+            z, y, x, c, SHARD - ROW_TILE : SHARD, :
+        ].astype(f32)[0:1]
+
+
+def gather_kernel(plan, shard_ref, norm_ref, *refs):
+    outs, norm_out, (held, send, recv) = refs[:8], refs[8], refs[9:]
+    place = Place(lax.axis_index("dp"))
+    enter(place)
+    gathers = [Gather(place, held.at[b], send.at[b], recv.at[b]) for b in range(2)]
+    for b in range(2):
+        load_shard(
+            plan, place.me, shard_ref.at[b], norm_ref, held.at[b, place.z, place.y, place.x, place.c]
+        )
+        gathers[b].start_z()
+    for b in range(2):
+        g = gathers[b]
+        for stage in (g.begin_first, g.begin_second, g.begin_third):
+            for q in range(4):
+                stage(q)
+        for q in range(4):
+            g.finish(q)
+        assemble(plan, held.at[b], outs[4 * b : 4 * b + 4], range(4))
+        if b == 0:
+            assemble_norms(len(plan), held.at[b], norm_out)
+    for g in gathers:
+        g.drain()
+
+
+def gather_weights(plan, params, norm_par, width, hidden):
+    size = params.shape[1]
+    vmem = pl.BlockSpec(memory_space=pltpu.VMEM)
+    shapes = matrix_shapes(width, hidden)
+    outs = pl.pallas_call(
+        partial(gather_kernel, plan),
+        in_specs=[vmem, vmem],
+        out_specs=[vmem] * 9,
+        out_shape=[jax.ShapeDtypeStruct(s, bf16) for s in shapes * 2]
+        + [jax.ShapeDtypeStruct((8, width), f32)],
+        scratch_shapes=[
+            pltpu.VMEM((2, 4, 2, 2, 2, SHARD, LANES), bf16),
+            pltpu.SemaphoreType.DMA((2, 6, 4)),
+            pltpu.SemaphoreType.DMA((2, 6, 4)),
+        ],
+        compiler_params=pltpu.CompilerParams(
+            collective_id=0, has_side_effects=True, vmem_limit_bytes=48 * MIB
+        ),
+    )(params.reshape(2, size // LANES, LANES), norm_par.reshape(1, LANES))
+    return outs[:4], outs[4:8], outs[8].reshape(2, 4, width)
+
+
+class Scatter:
+    def __init__(self, place, own, r1, r2a, r2b, r3, r4, send, recv):
+        self.p, self.own = place, own
+        self.r1, self.r2a, self.r2b, self.r3, self.r4 = r1, r2a, r2b, r3, r4
+        self.send, self.recv = send, recv
+
+    def first(self, q):
+        p = self.p
+        return (
+            remote(
+                self.own.at[q, :, :, 1 - p.c], self.r1.at[q], self.send.at[0, q], self.recv.at[0, q], p.sibling
+            ),
+        )
+
+    def second(self, q):
+        p = self.p
+        low, high = pl.ds(0, HALF), pl.ds(HALF, SHARD - HALF)
+        return (
+            remote(
+                self.r1.at[q, :, 1 - p.x, low], self.r2a.at[q], self.send.at[1, q], self.recv.at[1, q], p.across_x
+            ),
+            remote(
+                self.r1.at[q, 1 - p.y, :, high], self.r2b.at[q], self.send.at[2, q], self.recv.at[2, q], p.across_y
+            ),
+        )
+
+    def third(self, q):
+        p = self.p
+        low, high = pl.ds(0, HALF), pl.ds(HALF, SHARD - HALF)
+        return (
+            remote(
+                self.r2a.at[q, 1 - p.y], self.r3.at[q, low], self.send.at[3, q], self.recv.at[3, q], p.across_y
+            ),
+            remote(
+                self.r2b.at[q, 1 - p.x], self.r3.at[q, high], self.send.at[4, q], self.recv.at[4, q], p.across_x
+            ),
+        )
+
+    def along_z(self, q):
+        p = self.p
+        return remote(self.r3.at[q], self.r4.at[p.z], self.send.at[5, q], self.recv.at[5, p.z], p.plane(q))
+
+    def begin_first(self, q):
+        for copy in self.first(q):
+            copy.start()
+
+    def begin_second(self, q, mine):
+        for copy in self.first(q):
+            copy.wait_recv()
+        for y in range(2):
+            for x in range(2):
+                self.r1[q, y, x] = (self.r1[q, y, x].astype(f32) + mine[y, x].astype(f32)).astype(bf16)
+        for copy in self.second(q):
+            copy.start()
+
+    def begin_third(self, q):
+        p = self.p
+        for copy in self.second(q):
+            copy.wait_recv()
+        low, high = pl.ds(0, HALF), pl.ds(HALF, SHARD - HALF)
+        for k in range(2):
+            self.r2a[q, k] = (self.r2a[q, k].astype(f32) + self.r1[q, k, p.x, low].astype(f32)).astype(bf16)
+            self.r2b[q, k] = (self.r2b[q, k].astype(f32) + self.r1[q, p.y, k, high].astype(f32)).astype(bf16)
+        for copy in self.third(q):
+            copy.start()
+
+    def begin_z(self, q):
+        p = self.p
+        for copy in self.third(q):
+            copy.wait_recv()
+        low, high = pl.ds(0, HALF), pl.ds(HALF, SHARD - HALF)
+        self.r3[q, low] = (self.r3[q, low].astype(f32) + self.r2a[q, p.y].astype(f32)).astype(bf16)
+        self.r3[q, high] = (self.r3[q, high].astype(f32) + self.r2b[q, p.x].astype(f32)).astype(bf16)
+
+        @pl.when(q != p.z)
+        def _():
+            self.along_z(q).start()
+
+    def finish(self, total):
+        p = self.p
+        for k in range(1, 4):
+            z = lax.rem(p.z + k, 4)
+            remote(self.r3.at[0], self.r4.at[z], self.send.at[5, 0], self.recv.at[5, z], p.me).wait_recv()
+        total[...] = self.r3[p.z].astype(f32)
+        for k in range(1, 4):
+            total[...] += self.r4[lax.rem(p.z + k, 4)].astype(f32)
+
+    def drain(self):
+        for q in range(4):
+            for copy in self.first(q) + self.second(q) + self.third(q):
+                copy.wait_send()
+
+            @pl.when(q != self.p.z)
+            def _(q=q):
+                self.along_z(q).wait_send()
+
+
+SCATTER_SCRATCH = [
+    pltpu.VMEM((4, 2, 2, SHARD, LANES), bf16),
+    pltpu.VMEM((4, 2, HALF, LANES), bf16),
+    pltpu.VMEM((4, 2, SHARD - HALF, LANES), bf16),
+    pltpu.VMEM((4, SHARD, LANES), bf16),
+    pltpu.VMEM((4, SHARD, LANES), bf16),
+    pltpu.SemaphoreType.DMA((6, 4)),
+    pltpu.SemaphoreType.DMA((6, 4)),
+]
+
+
+def unload_shard(plan, me, total, flat_ref):
+    def body(layout):
+        for count, flat, stride, place in layout:
+            flat_ref[pl.ds(flat, count, stride), :] = total[pl.ds(place, count), :]
+
+    on_pattern(plan, me, body)
+
+
+def scatter_kernel(plan, g0, g1, flat0, flat1, norm_out, total, mine, load, *rest):
+    place = Place(lax.axis_index("dp"))
+    enter(place)
+    count = len(SCATTER_SCRATCH)
+    scatters = []
+    for b, own in ((1, g1), (0, g0)):
+        s = Scatter(place, own, *rest[b * count : (b + 1) * count])
+        scatters.append((b, s, own))
+    for b, s, own in scatters:
+        for q in range(4):
+            s.begin_first(q)
+    for b, s, own in scatters:
+        for q in range(4):
+            copy = pltpu.make_async_copy(own.at[q, :, :, place.c], mine.at[b, q], load.at[b, q])
+            copy.start()
+        for q in range(4):
+            pltpu.make_async_copy(own.at[q, :, :, place.c], mine.at[b, q], load.at[b, q]).wait()
+            s.begin_second(q, mine.at[b, q])
+        for q in range(4):
+            s.begin_third(q)
+        for q in range(4):
+            s.begin_z(q)
+    for b, s, own in scatters:
+        s.finish(total)
+        unload_shard(plan, place.me, total, (flat0, flat1)[b])
+        if b == 1:
+            norm_out[...] = total[SHARD - ROW_TILE : SHARD - ROW_TILE + 8]
+        else:
+            norm_out[...] += total[SHARD - ROW_TILE : SHARD - ROW_TILE + 8]
+    for b, s, own in scatters:
+        s.drain()
+
+
+def scatter_grads(plan, grads):
+    vmem = pl.BlockSpec(memory_space=pltpu.VMEM)
+    rows = SHARD - ROW_TILE
+    flat0, flat1, norm = pl.pallas_call(
+        partial(scatter_kernel, plan),
+        in_specs=[pl.BlockSpec(memory_space=pl.ANY)] * 2,
+        out_specs=[vmem] * 3,
+        out_shape=[
+            jax.ShapeDtypeStruct((rows, LANES), f32),
+            jax.ShapeDtypeStruct((rows, LANES), f32),
+            jax.ShapeDtypeStruct((8, LANES), f32),
+        ],
+        scratch_shapes=[
+            pltpu.VMEM((SHARD, LANES), f32),
+            pltpu.VMEM((2, 4, 2, 2, SHARD, LANES), bf16),
+            pltpu.SemaphoreType.DMA((2, 4)),
+        ]
+        + SCATTER_SCRATCH * 2,
+        compiler_params=pltpu.CompilerParams(
+            collective_id=1, has_side_effects=True, vmem_limit_bytes=48 * MIB
+        ),
+    )(*grads)
+    return jnp.stack([flat0.reshape(-1), flat1.reshape(-1)]), norm[0] + norm[1]
+
+
+def store_travel(plan, own, index, start, value):
+    for device, entries in enumerate(plan):
+        z, y, x, c = coordinates(device)
+        for entry, row, count, block, _, _, place in entries:
+            column = LANES * block - start
+            if entry == index and 0 <= column < value.shape[1]:
+                own[z, y, x, c, place : place + count, :] = value[row : row + count, column : column + LANES]
+
+
+def store_norms(plan, own, block, sums):
+    width = sums.shape[2]
+    per_row = width // LANES
+    line = lax.broadcasted_iota(jnp.int32, (ROW_TILE, LANES), 0)
+    for device in range(len(plan)):
+        z, y, x, c = coordinates(device)
+        row = device // per_row - 4 * block
+        if 0 <= row < 4:
+            column = LANES * (device % per_row)
+            value = jnp.sum(sums[row, :, column : column + LANES], axis=0, keepdims=True)
+            coarse = value.astype(bf16).astype(f32)
+            rows = jnp.where(line == 0, coarse, jnp.where(line == 1, value - coarse, 0.0))
+        else:
+            rows = jnp.zeros((ROW_TILE, LANES), f32)
+        own[z, y, x, c, SHARD - ROW_TILE : SHARD, :] = rows.astype(bf16)
+
+
+def weight_grads(first, grad_packed, mixture, attn, second, grad_hidden, active, branch, store, chunk=512):
     sides = ((first, grad_packed), (mixture, attn), (second, grad_hidden), (active, branch))
-    for (left, right), out in zip(sides, outs):
-        for start in range(0, out.shape[1], chunk):
-            out[:, start : start + chunk] = dot_tn(
-                left[...], right[:, start : start + chunk]
-            ).astype(out.dtype)
+    for index, (left, right) in enumerate(sides):
+        for start in range(0, right.shape[1], chunk):
+            store(index, start, dot_tn(left[...], right[:, start : start + chunk]).astype(bf16))
+
+
+def grad_outputs(plan, weights):
+    shapes = [w.shape for w in weights] if plan is None else [(4, 2, 2, 2, SHARD, LANES)]
+    return [whole(s) for s in shapes], [jax.ShapeDtypeStruct(s, bf16) for s in shapes]
+
+
+def storing(plan, block, outs, sums):
+    if plan is None:
+        def store(index, start, value):
+            outs[index][:, start : start + value.shape[1]] = value
+        return store
+    store_norms(plan, outs[0], block, sums)
+    return partial(store_travel, plan, outs[0])
 
 
 def temporal_kernel(
-    length_ref, rows_ref, cotangent_ref, w_qkv, w_out, w_up, w_down, norm_ref,
-    result_ref, before_ref, g_qkv, g_out, g_up, g_down, g_norm,
-    packed, slope, weights_buf, grad_mix,
-    first_all, packed_all, mixture_all, attn_all, second_all, hidden_all, active_all, branch_all,
+    plan, length_ref, rows_ref, cotangent_ref, w_qkv, w_out, w_up, w_down, norm_ref, result_ref, before_ref, *refs
 ):
+    outs, g_norm = refs[:-13], refs[-13]
+    packed, slope, weights_buf, grad_mix = refs[-12:-8]
+    first_all, packed_all, mixture_all, attn_all, second_all, hidden_all, active_all, branch_all = refs[-8:]
     step = pl.program_id(0)
     steps, patches, width = rows_ref.shape
     tile = steps * patches
@@ -310,28 +792,29 @@
     def _():
         weight_grads(
             first_all, packed_all, mixture_all, attn_all, second_all, hidden_all, active_all,
-            branch_all, (g_qkv, g_out, g_up, g_down),
+            branch_all, storing(plan, 1, outs, g_norm),
         )
 
 
-def temporal_block(length, rows, cotangent, weights, norms):
+def temporal_block(plan, length, rows, cotangent, weights, norms):
+    grad_specs, grad_shapes = grad_outputs(plan, weights)
     steps, patches, width = rows.shape
     tokens = steps * patches
     hidden = weights[2].shape[1]
     part = TEMPORAL_TILE // steps
     slab = pl.BlockSpec((steps, part, width), lambda i: (0, i, 0))
     return pl.pallas_call(
-        temporal_kernel,
+        partial(temporal_kernel, plan),
         grid=(patches // part,),
         in_specs=[pl.BlockSpec(memory_space=pltpu.SMEM), slab, slab]
         + [whole(w.shape) for w in weights]
         + [whole(norms.shape)],
-        out_specs=[slab, slab] + [whole(w.shape) for w in weights] + [whole((4, 8, width))],
+        out_specs=[slab, slab] + grad_specs + [whole((4, 8, width))],
         out_shape=[
             jax.ShapeDtypeStruct(rows.shape, f32),
             jax.ShapeDtypeStruct(rows.shape, f32),
         ]
-        + [jax.ShapeDtypeStruct(w.shape, bf16) for w in weights]
+        + grad_shapes
         + [jax.ShapeDtypeStruct((4, 8, width), f32)],
         scratch_shapes=[
             pltpu.VMEM((steps, part, 3 * width), bf16),
@@ -352,11 +835,12 @@
 
 
 def spatial_backward_kernel(
-    x_ref, grad_ref, packed_ref, weights_ref, middle_ref, slope_ref, mixture_all, active_all,
+    plan, x_ref, grad_ref, packed_ref, weights_ref, middle_ref, slope_ref, mixture_all, active_all,
     w_qkv, w_out, w_up, w_down, norm_ref,
-    before_ref, g_qkv, g_out, g_up, g_down, g_norm,
-    grad_mix, first_all, packed_all, attn_all, second_all, hidden_all, branch_all,
+    before_ref, *refs,
 ):
+    outs, g_norm = refs[:-8], refs[-8]
+    grad_mix, first_all, packed_all, attn_all, second_all, hidden_all, branch_all = refs[-7:]
     step = pl.program_id(0)
     tile, width = x_ref.shape
     here = pl.ds(pl.multiple_of(step * tile, tile), tile)
@@ -409,18 +893,19 @@
     def _():
         weight_grads(
             first_all, packed_all, mixture_all, attn_all, second_all, hidden_all, active_all,
-            branch_all, (g_qkv, g_out, g_up, g_down),
+            branch_all, storing(plan, 0, outs, g_norm),
         )
 
 
-def spatial_backward(x, grad, kept, weights, norms):
+def spatial_backward(plan, x, grad, kept, weights, norms):
     packed, soft, mixture, middle, active, slope = kept
+    grad_specs, grad_shapes = grad_outputs(plan, weights)
     tokens, width = x.shape
     hidden = weights[2].shape[1]
     frame = soft.shape[2]
     tile = SPATIAL_TILE
     return pl.pallas_call(
-        spatial_backward_kernel,
+        partial(spatial_backward_kernel, plan),
         grid=(tokens // tile,),
         in_specs=[
             tiles(tile, width),
@@ -435,10 +920,10 @@
         + [whole(w.shape) for w in weights]
         + [whole(norms.shape)],
         out_specs=[tiles(tile, width)]
-        + [whole(w.shape) for w in weights]
+        + grad_specs
         + [whole((4, 8, width))],
         out_shape=[jax.ShapeDtypeStruct((tokens, width), f32)]
-        + [jax.ShapeDtypeStruct(w.shape, bf16) for w in weights]
+        + grad_shapes
         + [jax.ShapeDtypeStruct((4, 8, width), f32)],
         scratch_shapes=[
             pltpu.VMEM((tile, width), bf16),
@@ -489,14 +974,21 @@
 ):
     clip_count, step_slots, patch_count, model_width = clip_tokens.shape
     shards = lax.axis_size("dp")
-    gathered = lax.all_gather(params.astype(bf16), "dp", axis=1, tiled=True)
-    norm_whole = lax.all_gather(norm_par.astype(bf16), "dp", axis=0, tiled=True)
-    norm_table = norm_whole.astype(f32).reshape(2, 4, model_width)
-    spatial_weights = unpack(gathered[0], model_width, FF)
-    temporal_weights = unpack(gathered[1], model_width, FF)
+    plan = shard_plan(shards, model_width, FF) if shards == 32 else None
+    if plan is None:
+        gathered = lax.all_gather(params.astype(bf16), "dp", axis=1, tiled=True)
+        norm_whole = lax.all_gather(norm_par.astype(bf16), "dp", axis=0, tiled=True)
+        norm_table = norm_whole.astype(f32).reshape(2, 4, model_width)
+        spatial_weights = unpack(gathered[0], model_width, FF)
+        temporal_weights = unpack(gathered[1], model_width, FF)
+    else:
+        spatial_weights, temporal_weights, norm_table = gather_weights(
+            plan, params, norm_par, model_width, FF
+        )
     x = clip_tokens.reshape(-1, model_width)
     *kept, after = spatial_forward(x, spatial_weights, norm_table[0], patch_count)
     result, grad_after, *temporal_grads, temporal_norm = temporal_block(
+        plan,
         lengths,
         after.reshape(step_slots, patch_count, model_width),
         cotangent.reshape(step_slots, patch_count, model_width),
@@ -504,16 +996,20 @@
         norm_table[1],
     )
     grad_before, *spatial_grads, spatial_norm = spatial_backward(
-        x, grad_after.reshape(-1, model_width), kept, spatial_weights, norm_table[0]
+        plan, x, grad_after.reshape(-1, model_width), kept, spatial_weights, norm_table[0]
     )
 
-    def scatter(grads):
-        flat = jnp.concatenate([g.reshape(-1) for g in grads])
-        return lax.psum_scatter(flat, "dp", scatter_dimension=0, tiled=True).astype(f32)
-
-    weight_sum = jnp.stack([scatter(spatial_grads), scatter(temporal_grads)])
-    norm_grad = jnp.stack([spatial_norm, temporal_norm]).sum(axis=2).reshape(-1)
-    norm_sum = lax.psum_scatter(norm_grad, "dp", scatter_dimension=0, tiled=True)
+    if plan is None:
+
+        def scatter(grads):
+            flat = jnp.concatenate([g.reshape(-1) for g in grads])
+            return lax.psum_scatter(flat, "dp", scatter_dimension=0, tiled=True).astype(f32)
+
+        weight_sum = jnp.stack([scatter(spatial_grads), scatter(temporal_grads)])
+        norm_grad = jnp.stack([spatial_norm, temporal_norm]).sum(axis=2).reshape(-1)
+        norm_sum = lax.psum_scatter(norm_grad, "dp", scatter_dimension=0, tiled=True)
+    else:
+        weight_sum, norm_sum = scatter_grads(plan, (spatial_grads[0], temporal_grads[0]))
     step_value = float(STEP)
     new_params, new_moment, new_second = adamw(
         params, param_moment, param_second, weight_sum, step_value, learn_rate, weight_decay

time: 746 us -> 395 us (0.53)
  waiting for transfers between devices: 244 us -> 0 us
  Pallas kernels: 216 us -> 376 us
  local copies, waits for them, and re-layouts: 149 us -> 6.43 us
  blocking collectives: 83.7 us -> 0 us
  other arithmetic: 30.4 us -> 4.99 us
  between operations: 15.1 us -> 1.64 us
    unnamed x3 -> x0, waiting for transfers between devices: 189 us -> none
    pallas_call x2 -> x4, Pallas kernels: 175 us -> 335 us  [the longest x1 112 us: temporal_block(): pl.pallas_call(partial(temporal_kernel, plan), grid=(patches // part,), i...]
    slice x4 -> x0, local copies, waits for them, and re-layouts: 99.2 us -> none  [the longest x1 50 us: unpack(): flat_weights[cut_up:].reshape(hidden_width, model_width)]
    all_gather x1 -> x0, waiting for transfers between devices: 55 us -> none  [on_device(): gathered = lax.all_gather(params.astype(bf16), 'dp', axis=1, tiled=True)]
    all_gather x1 -> x0, blocking collectives: 43.1 us -> none  [on_device(): norm_whole = lax.all_gather(norm_par.astype(bf16), 'dp', axis=0, tiled=True)]
    unnamed x1 -> x0, blocking collectives: 40.5 us -> none
    reshape x10 -> x0, local copies, waits for them, and re-layouts: 34.7 us -> none  [the longest x2 8.59 us: scatter(): flat = jnp.concatenate([g.reshape(-1) for g in grads])]
    concatenate x1 -> x0, other arithmetic: 22.5 us -> none  [scatter(): flat = jnp.concatenate([g.reshape(-1) for g in grads])]
  transfers between devices with their start and end apart: 2 -> 0, of which waited for: 2 -> 0; matrix products, arithmetic and copies ran while one was open for 0% -> 0% of each run, Pallas kernels for 0% -> 0%
where the time goes in v2:
time: 395 us; the launch traced here: 389 us
  Pallas kernels  376 us (95%)
  local copies, waits for them, and re-layouts  6.43 us (2%)
  other arithmetic  4.99 us (1%)
    pallas_call x1, Pallas kernels, temporal_block(): pl.pallas_call(partial(temporal_kernel, plan), grid=(patches // part,), i...  112 us
    pallas_call x1, Pallas kernels, scatter_grads(): pl.pallas_call(partial(scatter_kernel, plan), in_specs=[pl.BlockSpec(memo...  83.7 us
    pallas_call x1, Pallas kernels, gather_weights(): pl.pallas_call(partial(gather_kernel, plan), in_specs=[vmem, vmem], out_s...  79.5 us
    pallas_call x1, Pallas kernels, spatial_backward(): pl.pallas_call(partial(spatial_backward_kernel, plan), grid=(tokens // ti...  60.3 us
    pallas_call x1, Pallas kernels, spatial_forward(): pl.pallas_call(spatial_forward_kernel, grid=(tokens // tile,), in_specs=[...  41.1 us

profile of v2, /device:TPU:0, one launch (start us, length us, event | category | flops | bytes accessed | tf_op | source)
XLA Modules:
  0.0 389.4 jit_solution(18345466523787457066)
XLA Ops:
  1.3 1.2 copy.20
  2.5 0.0 copy-start.4
  2.5 0.6 copy-done.4
  3.1 79.5 %shard_map.160 = (bf16[512,1536]{1,0:T(8,128)(2,1)S(1)}, bf16[512,512]{1,0:T(8,128)(2,1)S(1)}, bf16[512,2048]{1,0:T(8,128)(2,1)}, bf16[2048,512]{1,0:T(8,128)(2,...) custom-call(f32[2,768,128]{2,1,0:T(8,128)S(1)} %bitcast.20, ...), custom_call_target="tpu_custom_call" | custom-call | tf_op jit(solution)/shard_map/pallas_call | solution.py:459
  82.6 0.0 copy-start
  82.6 1.2 copy-done
  83.8 0.8 copy-done.1
  84.6 1.2 copy-done.2
  85.8 0.8 copy-done.3
  86.6 0.6 fusion.7
  87.2 41.1 %shard_map.161 = (bf16[2048,1536]{1,0:T(8,128)(2,1)}, bf16[8,8,256,256]{3,2,1,0:T(8,128)(2,1)}, bf16[2048,512]{1,0:T(8,128)(2,1)}, f32[2048,512]{1,0:T(8,128)}, ...) custom-call(bf16[2048,512]{1,0:T(8,128)(2,1)} %bitcast.24, bf16[512,1536]{1,0:T(8,128)(2,1)} %copy-done, ...), custom_call_target="tpu_custom_call" | custom-call | tf_op jit(solution)/shard_map/pallas_call | solution.py:181
  128.2 111.8 %shard_map.162 = (f32[8,256,512]{2,1,0:T(8,128)}, f32[8,256,512]{2,1,0:T(8,128)}, bf16[4,2,2,2,784,128]{5,4,3,2,1,0:T(8,128)(2,1)}, f32[4,8,512]{2,1,0:T(8,128)}) custom-call(s32[1]{0:T(128)S(6)} %copy.21.length_ref, f32[8,256,512]{2,1,0:T(8,128)} %bitcast.26, bf16[8,256,512]{2,1,0:T(8,128)(2,1)} %bitcast.29, bf16[512,1536]{1,0:T(8,128)(2,1)} %copy-done.2, ...), custom_call_target="tpu_custom_call" | custom-call | tf_op jit(solution)/shard_map/pallas_call | solution.py:806
  240.1 60.3 %shard_map.163 = (f32[2048,512]{1,0:T(8,128)}, bf16[4,2,2,2,784,128]{5,4,3,2,1,0:T(8,128)(2,1)}, f32[4,8,512]{2,1,0:T(8,128)}) custom-call(bf16[2048,512]{1,0:T(8,128)(2,1)} %bitcast.25, f32[2048,512]{1,0:T(8,128)} %bitcast.27, bf16[2048,1536]{1,0:T(8,128)(2,1)} %get-tuple-element.45.packed_ref, bf16[8,8,256,256]{3,2,1,0:T(8,128)(2,1)} %get-tuple-element.46.weights_ref, ...), custom_call_target="tpu_custom_call" | custom-call | tf_op jit(solution)/shard_map/pallas_call | solution.py:907
  300.4 0.0 copy-start.5
  300.4 0.0 copy-start.9
  300.4 0.0 copy-start.10
  300.4 0.0 copy-start.6
  300.4 0.0 copy-start.7
  300.4 0.0 copy-start.8
  300.4 83.7 %shard_map.164 = (f32[768,128]{1,0:T(8,128)S(1)}, f32[768,128]{1,0:T(8,128)S(1)}, f32[8,128]{1,0:T(8,128)S(1)}) custom-call(bf16[4,2,2,2,784,128]{5,4,3,2,1,0:T(8,128)(2,1)} %get-tuple-element.52.g0, bf16[4,2,2,2,784,128]{5,4,3,2,1,0:T(8,128)(2,1)} %get-tuple-element.53.g1), custom_call_target="tpu_custom_call" | custom-call | tf_op jit(solution)/shard_map/pallas_call | solution.py:629
  384.2 0.0 copy-done.5
  384.2 0.0 copy-done.9
  384.2 0.5 multiply_subtract_fusion.1
  384.8 4.5 %fusion.5 = (bf16[2,98304]{1,0:T(2,128)(2,1)}, f32[2,98304]{1,0:T(2,128)}, f32[2,98304]{1,0:T(2,128)}, f32[2,98304]{1,0:T(2,128)}) fusion(f32[2,98304]{1,0:T(2,128)S(1)} %copy-done.6, f32[1,98304]{1,0:T(1,128)S(1)} %bitcast.22, f32[1,98304]{1,0:T(1,128)S(1)} %bitcast.21, f32[2,98304]{1,0:T(2,128)S(1)} %copy-done.7, f32[2,98304]{1,0:T(2,128)S(1)} %copy-done.8), kind=kLoop, calls=%fused_computation.12 | loop fusion | flops 3342336 | bytes 5898240 | tf_op jit(solution)/shard_map/convert_element_type | solution.py:1026
  (7 shorter events, 0.0 us)
Async XLA Ops:
  2.5 0.7 copy-start.4
  82.6 1.2 copy-start
  83.8 0.8 copy-start.1
  84.6 1.2 copy-start.2
  85.8 0.8 copy-start.3
  300.4 83.8 %copy-start.5 = (f32[128]{0:T(128)S(1)}, f32[128]{0:T(128)}, u32[]{:S(2)}) copy-start(f32[128]{0:T(128)} %param.15) | copy-start | bytes 1540
  300.4 83.8 %copy-start.9 = (f32[128]{0:T(128)S(1)}, f32[128]{0:T(128)}, u32[]{:S(2)}) copy-start(f32[128]{0:T(128)} %param.16) | copy-start | bytes 1540
  300.4 83.8 %copy-start.10 = (f32[128]{0:T(128)S(1)}, f32[128]{0:T(128)}, u32[]{:S(2)}) copy-start(f32[128]{0:T(128)} %param.17) | copy-start | bytes 1540
  300.4 84.4 %copy-start.6 = (f32[2,98304]{1,0:T(2,128)S(1)}, f32[2,98304]{1,0:T(2,128)}, u32[]{:S(2)}) copy-start(f32[2,98304]{1,0:T(2,128)} %param.12) | copy-start | bytes 2359300
  300.4 84.4 %copy-start.7 = (f32[2,98304]{1,0:T(2,128)S(1)}, f32[2,98304]{1,0:T(2,128)}, u32[]{:S(2)}) copy-start(f32[2,98304]{1,0:T(2,128)} %param.13) | copy-start | bytes 2359300
  300.4 84.3 %copy-start.8 = (f32[2,98304]{1,0:T(2,128)S(1)}, f32[2,98304]{1,0:T(2,128)}, u32[]{:S(2)}) copy-start(f32[2,98304]{1,0:T(2,128)} %param.14) | copy-start | bytes 2359300

commit v3 on v2

--- a/solution.py
+++ b/solution.py
@@ -72,51 +72,60 @@
     return lane < HEAD_DIM
 
 
-def only_head(pair, low_half, which):
-    keep = low_half if which == 0 else jnp.logical_not(low_half)
-    return jnp.where(keep, pair, jnp.zeros_like(pair))
-
-
-def softmax(scores):
-    top = jnp.max(scores, axis=-1, keepdims=True)
-    powers = jnp.exp(scores - top)
-    return powers * (1.0 / jnp.sum(powers, axis=-1, keepdims=True))
-
-
-def attend(query, key, value, low_half, bias):
-    query = query * jnp.asarray(HEAD_DIM**-0.5, bf16)
-    weights = []
-    mixture = None
-    for which in range(2):
-        scores = dot_nt(query, only_head(key, low_half, which))
-        if bias is not None:
-            scores = scores + bias
-        soft = softmax(scores).astype(bf16)
-        weights.append(soft)
-        part = dot_nn(soft, only_head(value, low_half, which))
-        mixture = part if mixture is None else mixture + part
-    return weights, mixture.astype(bf16)
-
-
-def attend_backward(query, key, value, grad, weights, low_half):
+def two_heads(pair, low_half):
+    zero = jnp.zeros_like(pair)
+    return jnp.concatenate([jnp.where(low_half, pair, zero), jnp.where(low_half, zero, pair)], axis=0)
+
+
+def own_columns(stacked, low_half):
+    rows = stacked.shape[0] // 2
+    return jnp.where(low_half, stacked[:rows], stacked[rows:]).astype(bf16)
+
+
+ROW_CHUNK = 64
+
+
+def attend(units, scores, soft, low_half, bias):
+    rows, double = scores.shape[1:]
+    keys = double // 2
+    for unit, (query, key, value, put) in enumerate(units):
+        scaled = query() * jnp.asarray(HEAD_DIM**-0.5, bf16)
+        scores[unit] = dot_nt(scaled, two_heads(key(), low_half))
+    for unit in range(len(units)):
+        for start in range(0, rows, ROW_CHUNK):
+            span = slice(start, start + ROW_CHUNK)
+            for half in range(2):
+                columns = slice(half * keys, (half + 1) * keys)
+                part = scores[unit, span, columns]
+                if bias is not None:
+                    part = part + bias[span]
+                powers = jnp.exp(part - jnp.max(part, axis=-1, keepdims=True))
+                part = powers * (1.0 / jnp.sum(powers, axis=-1, keepdims=True))
+                soft[unit, span, columns] = part.astype(bf16)
+    for unit, (query, key, value, put) in enumerate(units):
+        put(dot_nn(soft[unit], two_heads(value(), low_half)).astype(bf16))
+
+
+def attend_backward(units, scores, soft, grad_scores, low_half):
+    rows, double = scores.shape[1:]
+    keys = double // 2
     scale = jnp.asarray(HEAD_DIM**-0.5, bf16)
-    query = query * scale
-    scaled_key = key * scale
-    totals = [None, None, None]
-    for which in range(2):
-        soft = weights[which]
-        grad_soft = dot_nt(grad, only_head(value, low_half, which))
-        wide = soft.astype(f32)
-        product = grad_soft * wide
-        inner = jnp.sum(product, axis=-1, keepdims=True)
-        grad_scores = (product - wide * inner).astype(bf16)
-        parts = (
-            dot_nn(grad_scores, only_head(scaled_key, low_half, which)),
-            dot_tn(grad_scores, only_head(query, low_half, which)),
-            dot_tn(soft, only_head(grad, low_half, which)),
-        )
-        totals = [p if t is None else t + p for t, p in zip(totals, parts)]
-    return [t.astype(bf16) for t in totals]
+    for unit, (query, key, value, grad, put) in enumerate(units):
+        scores[unit] = dot_nt(grad(), two_heads(value(), low_half))
+    for unit in range(len(units)):
+        for start in range(0, rows, ROW_CHUNK):
+            span = slice(start, start + ROW_CHUNK)
+            for half in range(2):
+                columns = slice(half * keys, (half + 1) * keys)
+                wide = soft[unit, span, columns].astype(f32)
+                product = scores[unit, span, columns] * wide
+                inner = jnp.sum(product, axis=-1, keepdims=True)
+                grad_scores[unit, span, columns] = (product - wide * inner).astype(bf16)
+    for unit, (query, key, value, grad, put) in enumerate(units):
+        grad_value = own_columns(dot_tn(soft[unit], grad()), low_half)
+        grad_query = dot_nn(grad_scores[unit], two_heads(key() * scale, low_half)).astype(bf16)
+        grad_key = own_columns(dot_tn(grad_scores[unit], query() * scale), low_half)
+        put(grad_query, grad_key, grad_value)
 
 
 def feed_forward(second, w_up, w_down, active_ref, slope_ref, chunk=512):
@@ -136,33 +145,133 @@
         hidden_ref[:, start : start + chunk] = (grad * slope).astype(bf16)
 
 
-def spatial_forward_kernel(
-    x_ref, w_qkv, w_out, w_up, w_down, norm_ref,
-    packed_ref, weights_ref, mixture_ref, middle_ref, active_ref, slope_ref, after_ref,
-):
-    width = x_ref.shape[1]
-    rows = x_ref[...].astype(f32)
-    hat, _ = normalise(rows)
-    first = (hat * norm_ref[0:1] + norm_ref[1:2]).astype(bf16)
-    packed_ref[...] = dot_nn(first, w_qkv[...]).astype(bf16)
-    frame = weights_ref.shape[2]
-    low_half = lane_halves(frame)
-    for item in range(weights_ref.shape[0]):
-        span = slice(item * frame, (item + 1) * frame)
-        for pair in range(HEADS // 2):
-            cut = [
-                packed_ref[span, part * width + 128 * pair : part * width + 128 * (pair + 1)]
-                for part in range(3)
-            ]
-            weights, mixture = attend(*cut, low_half, None)
-            weights_ref[item, 2 * pair] = weights[0]
-            weights_ref[item, 2 * pair + 1] = weights[1]
-            mixture_ref[span, 128 * pair : 128 * (pair + 1)] = mixture
-    middle = rows + dot_nn(mixture_ref[...], w_out[...])
-    middle_ref[...] = middle
-    hat, _ = normalise(middle)
-    second = (hat * norm_ref[2:3] + norm_ref[3:4]).astype(bf16)
-    after_ref[...] = middle + feed_forward(second, w_up, w_down, active_ref, slope_ref)
+def spatial_forward_kernel(plan, x_ref, *refs):
+    step, last = pl.program_id(1), pl.num_programs(1) - 1
+    opening = pl.program_id(0) == 0
+    if plan is None:
+        w_qkv, w_out, w_up, w_down, norm_ref = refs[:5]
+        refs = refs[5:]
+        packed_ref, weights_ref, mixture_ref, middle_ref, active_ref, slope_ref, after_ref = refs[:7]
+        scores, mixture_all = refs[7:]
+    else:
+        shard_ref, norm_par_ref = refs[:2]
+        refs = refs[2:]
+        packed_ref, weights_ref, mixture_ref, middle_ref, active_ref, slope_ref, after_ref = refs[:7]
+        held_out, held_next, norm_ref = refs[7:10]
+        scores, mixture_all, w_qkv, w_out, w_up, w_down, held, staged, send, recv, local = refs[10:]
+        matrices = (w_qkv, w_out, w_up, w_down)
+        place = Place(lax.axis_index("dp"))
+        now = Gather(place, held, send.at[0], recv.at[0])
+        later = Gather(place, held_next, send.at[1], recv.at[1])
+        keep = pltpu.make_async_copy(held, held_out, local.at[0])
+
+        def gathered(*planes):
+            for q in planes:
+                now.finish(q)
+            assemble(plan, held, matrices, planes)
+            assemble_norms(len(plan), held, norm_ref, planes)
+
+        @pl.when(opening & (step == 0))
+        def _():
+            enter(place)
+            load_shard(plan, place.me, shard_ref.at[0], norm_par_ref, held.at[place.z, place.y, place.x, place.c])
+            now.start_z()
+            load_shard(plan, place.me, shard_ref.at[1], norm_par_ref, staged)
+            copy = pltpu.make_async_copy(
+                staged, held_next.at[place.z, place.y, place.x, place.c], local.at[1]
+            )
+            copy.start()
+            copy.wait()
+            now.begin_first(0)
+            now.begin_second(0)
+            for q in range(1, 4):
+                now.begin_first(q)
+            now.begin_third(0)
+            later.start_z()
+            gathered(0)
+
+        @pl.when(opening & (step == 1))
+        def _():
+            now.begin_second(1)
+            now.begin_second(2)
+
+        @pl.when(opening & (step == 2))
+        def _():
+            now.begin_second(3)
+
+        @pl.when(opening & (step == 3))
+        def _():
+            now.begin_third(1)
+            for q in range(4):
+                later.begin_first(q)
+
+        @pl.when(opening & (step == 4))
+        def _():
+            now.begin_third(2)
+            later.begin_second(0)
+
+        @pl.when(opening & (step == 6))
+        def _():
+            now.begin_third(3)
+            later.begin_second(1)
+
+        @pl.when(jnp.logical_not(opening) & (step == 0))
+        def _():
+            later.begin_second(2)
+            later.begin_second(3)
+            gathered(1, 2, 3)
+            keep.start()
+
+        for q in range(4):
+
+            @pl.when(jnp.logical_not(opening) & (step == 2 * q + 1))
+            def _(q=q):
+                later.begin_third(q)
+
+    tile, width = x_ref.shape
+    here = pl.ds(pl.multiple_of(step * tile, tile), tile)
+
+    @pl.when(opening)
+    def _():
+        hat, _ = normalise(x_ref[...].astype(f32))
+        first = (hat * norm_ref[0:1] + norm_ref[1:2]).astype(bf16)
+        for start in range(0, 3 * width, 512):
+            packed_ref[:, start : start + 512] = dot_nn(first, w_qkv[:, start : start + 512]).astype(bf16)
+        frame = weights_ref.shape[2]
+        low_half = lane_halves(frame)
+        for item in range(weights_ref.shape[0]):
+            span = slice(item * frame, (item + 1) * frame)
+            units = []
+            for pair in range(HEADS // 2):
+
+                def cut(part, pair=pair, span=span):
+                    start = part * width + 128 * pair
+                    return packed_ref[span, start : start + 128]
+
+                def put(value, pair=pair, span=span):
+                    mixture_ref[span, 128 * pair : 128 * (pair + 1)] = value
+
+                units.append((partial(cut, 0), partial(cut, 1), partial(cut, 2), put))
+            attend(units, scores, weights_ref.at[item], low_half, None)
+        mixture_all[here, :] = mixture_ref[...]
+
+    @pl.when(jnp.logical_not(opening))
+    def _():
+        middle = x_ref[...].astype(f32) + dot_nn(mixture_all[here, :], w_out[...])
+        middle_ref[...] = middle
+        hat, _ = normalise(middle)
+        second = (hat * norm_ref[2:3] + norm_ref[3:4]).astype(bf16)
+        after_ref[...] = middle + feed_forward(second, w_up, w_down, active_ref, slope_ref)
+
+    if plan is not None:
+
+        @pl.when(jnp.logical_not(opening) & (step == last))
+        def _():
+            for q in range(4):
+                later.finish(q)
+            keep.wait()
+            now.drain()
+            later.drain()
 
 
 def whole(shape):
@@ -173,35 +282,60 @@
     return pl.BlockSpec((tile, *rest), lambda i: (i,) + (0,) * len(rest))
 
 
-def spatial_forward(x, weights, norms, frame):
+def spatial_forward(plan, x, sources, frame, hidden):
     tokens, width = x.shape
-    hidden = weights[2].shape[1]
     tile = SPATIAL_TILE
     frames = tile // frame
+    count = tokens // tile
+
+    def opening(*rest):
+        return pl.BlockSpec(rest, lambda p, i: (i + p * (count - 1 - i),) + (0,) * (len(rest) - 1))
+
+    def closing(*rest):
+        return pl.BlockSpec(rest, lambda p, i: (i * p,) + (0,) * (len(rest) - 1))
+
+    out_specs = [
+        opening(tile, 3 * width),
+        opening(frames, HEADS // 2, frame, 2 * frame),
+        opening(tile, width),
+        closing(tile, width),
+        closing(tile, hidden),
+        closing(tile, hidden),
+        closing(tile, width),
+    ]
+    out_shape = [
+        jax.ShapeDtypeStruct((tokens, 3 * width), bf16),
+        jax.ShapeDtypeStruct((tokens // frame, HEADS // 2, frame, 2 * frame), bf16),
+        jax.ShapeDtypeStruct((tokens, width), bf16),
+        jax.ShapeDtypeStruct((tokens, width), f32),
+        jax.ShapeDtypeStruct((tokens, hidden), bf16),
+        jax.ShapeDtypeStruct((tokens, hidden), bf16),
+        jax.ShapeDtypeStruct((tokens, width), f32),
+    ]
+    scratch = [pltpu.VMEM((HEADS // 2, frame, 2 * frame), f32), pltpu.VMEM((tokens, width), bf16)]
+    params = dict(vmem_limit_bytes=60 * MIB)
+    if plan is not None:
+        held = (4, 2, 2, 2, SHARD, LANES)
+        out_specs += [pl.BlockSpec(memory_space=pl.ANY)] * 2 + [whole((8, width))]
+        out_shape += [jax.ShapeDtypeStruct(held, bf16)] * 2 + [jax.ShapeDtypeStruct((8, width), f32)]
+        scratch += [pltpu.VMEM(shape, bf16) for shape in matrix_shapes(width, hidden)]
+        scratch += [
+            pltpu.VMEM(held, bf16),
+            pltpu.VMEM((SHARD, LANES), bf16),
+            pltpu.SemaphoreType.DMA((2, 6, 4)),
+            pltpu.SemaphoreType.DMA((2, 6, 4)),
+            pltpu.SemaphoreType.DMA((2,)),
+        ]
+        params |= dict(collective_id=0, has_side_effects=True)
     return pl.pallas_call(
-        spatial_forward_kernel,
-        grid=(tokens // tile,),
-        in_specs=[tiles(tile, width)] + [whole(w.shape) for w in weights] + [whole(norms.shape)],
-        out_specs=[
-            tiles(tile, 3 * width),
-            tiles(frames, HEADS, frame, frame),
-            tiles(tile, width),
-            tiles(tile, width),
-            tiles(tile, hidden),
-            tiles(tile, hidden),
-            tiles(tile, width),
-        ],
-        out_shape=[
-            jax.ShapeDtypeStruct((tokens, 3 * width), bf16),
-            jax.ShapeDtypeStruct((tokens // frame, HEADS, frame, frame), bf16),
-            jax.ShapeDtypeStruct((tokens, width), bf16),
-            jax.ShapeDtypeStruct((tokens, width), f32),
-            jax.ShapeDtypeStruct((tokens, hidden), bf16),
-            jax.ShapeDtypeStruct((tokens, hidden), bf16),
-            jax.ShapeDtypeStruct((tokens, width), f32),
-        ],
-        compiler_params=pltpu.CompilerParams(vmem_limit_bytes=56 * MIB),
-    )(x, *weights, norms)
+        partial(spatial_forward_kernel, plan),
+        grid=(2, count),
+        in_specs=[pl.BlockSpec((tile, width), lambda p, i: (i, 0))] + [whole(a.shape) for a in sources],
+        out_specs=out_specs,
+        out_shape=out_shape,
+        scratch_shapes=scratch,
+        compiler_params=pltpu.CompilerParams(**params),
+    )(x, *sources)
 
 
 MESH_IDS = pl.DeviceIdType.MESH
@@ -418,60 +552,16 @@
             ]
 
 
-def assemble_norms(shards, held, norm_out):
+def assemble_norms(shards, held, norm_out, planes):
     per_row = norm_out.shape[1] // LANES
     for device in range(shards):
         z, y, x, c = coordinates(device)
+        if z not in planes:
+            continue
         row, column = device // per_row, device % per_row
         norm_out[row : row + 1, LANES * column : LANES * (column + 1)] = held[
             z, y, x, c, SHARD - ROW_TILE : SHARD, :
         ].astype(f32)[0:1]
-
-
-def gather_kernel(plan, shard_ref, norm_ref, *refs):
-    outs, norm_out, (held, send, recv) = refs[:8], refs[8], refs[9:]
-    place = Place(lax.axis_index("dp"))
-    enter(place)
-    gathers = [Gather(place, held.at[b], send.at[b], recv.at[b]) for b in range(2)]
-    for b in range(2):
-        load_shard(
-            plan, place.me, shard_ref.at[b], norm_ref, held.at[b, place.z, place.y, place.x, place.c]
-        )
-        gathers[b].start_z()
-    for b in range(2):
-        g = gathers[b]
-        for stage in (g.begin_first, g.begin_second, g.begin_third):
-            for q in range(4):
-                stage(q)
-        for q in range(4):
-            g.finish(q)
-        assemble(plan, held.at[b], outs[4 * b : 4 * b + 4], range(4))
-        if b == 0:
-            assemble_norms(len(plan), held.at[b], norm_out)
-    for g in gathers:
-        g.drain()
-
-
-def gather_weights(plan, params, norm_par, width, hidden):
-    size = params.shape[1]
-    vmem = pl.BlockSpec(memory_space=pltpu.VMEM)
-    shapes = matrix_shapes(width, hidden)
-    outs = pl.pallas_call(
-        partial(gather_kernel, plan),
-        in_specs=[vmem, vmem],
-        out_specs=[vmem] * 9,
-        out_shape=[jax.ShapeDtypeStruct(s, bf16) for s in shapes * 2]
-        + [jax.ShapeDtypeStruct((8, width), f32)],
-        scratch_shapes=[
-            pltpu.VMEM((2, 4, 2, 2, 2, SHARD, LANES), bf16),
-            pltpu.SemaphoreType.DMA((2, 6, 4)),
-            pltpu.SemaphoreType.DMA((2, 6, 4)),
-        ],
-        compiler_params=pltpu.CompilerParams(
-            collective_id=0, has_side_effects=True, vmem_limit_bytes=48 * MIB
-        ),
-    )(params.reshape(2, size // LANES, LANES), norm_par.reshape(1, LANES))
-    return outs[:4], outs[4:8], outs[8].reshape(2, 4, width)
 
 
 class Scatter:
@@ -681,8 +771,8 @@
             store(index, start, dot_tn(left[...], right[:, start : start + chunk]).astype(bf16))
 
 
-def grad_outputs(plan, weights):
-    shapes = [w.shape for w in weights] if plan is None else [(4, 2, 2, 2, SHARD, LANES)]
+def grad_outputs(plan, width, hidden):
+    shapes = matrix_shapes(width, hidden) if plan is None else [(4, 2, 2, 2, SHARD, LANES)]
     return [whole(s) for s in shapes], [jax.ShapeDtypeStruct(s, bf16) for s in shapes]
 
 
@@ -696,10 +786,18 @@
 
 
 def temporal_kernel(
-    plan, length_ref, rows_ref, cotangent_ref, w_qkv, w_out, w_up, w_down, norm_ref, result_ref, before_ref, *refs
+    plan, length_ref, rows_ref, cotangent_ref, *refs
 ):
-    outs, g_norm = refs[:-13], refs[-13]
-    packed, slope, weights_buf, grad_mix = refs[-12:-8]
+    sources = 5 if plan is None else 2
+    refs, sources = refs[sources:], refs[:sources]
+    result_ref, before_ref, *refs = refs
+    if plan is None:
+        w_qkv, w_out, w_up, w_down, norm_ref = sources
+    else:
+        *refs, w_qkv, w_out, w_up, w_down, local = refs
+        norm_ref = sources[1]
+    outs, g_norm = refs[:-15], refs[-15]
+    packed, slope, weights_buf, grad_mix, scores, grad_scores = refs[-14:-8]
     first_all, packed_all, mixture_all, attn_all, second_all, hidden_all, active_all, branch_all = refs[-8:]
     step = pl.program_id(0)
     steps, patches, width = rows_ref.shape
@@ -712,6 +810,8 @@
     @pl.when(step == 0)
     def _():
         g_norm[...] = jnp.zeros_like(g_norm)
+        if plan is not None:
+            load_weights(plan, sources[0], outs[0], (w_qkv, w_out, w_up, w_down), local)
 
     row = lax.broadcasted_iota(jnp.int32, (count, count), 0)
     column = lax.broadcasted_iota(jnp.int32, (count, count), 1)
@@ -732,16 +832,24 @@
         start = part * width + 128 * pair
         return source[:, place : place + group, start : start + 128].reshape(count, 128)
 
-    for place in range(0, patches, group):
-        for pair in range(HEADS // 2):
-            weights, mixture = attend(
-                *[cut(packed, part, place, pair) for part in range(3)], low_half, bias
-            )
-            for which in range(2):
-                weights_buf[place // group, 2 * pair + which] = weights[which]
-            grad_mix[:, place : place + group, 128 * pair : 128 * (pair + 1)] = mixture.reshape(
-                steps, group, 128
-            )
+    def units_of(backward):
+        units = []
+        for place in range(0, patches, group):
+            for pair in range(HEADS // 2):
+
+                def put(*values, place=place, pair=pair):
+                    for part, value in enumerate(values):
+                        start = part * width + 128 * pair
+                        into = packed if backward else grad_mix
+                        into[:, place : place + group, start : start + 128] = value.reshape(steps, group, 128)
+
+                gets = [partial(cut, packed, part, place, pair) for part in range(3)]
+                if backward:
+                    gets.append(partial(cut, grad_mix, 0, place, pair))
+                units.append((*gets, put))
+        return units
+
+    attend(units_of(False), scores, weights_buf, low_half, bias)
     mixture = grad_mix[...].reshape(tile, width)
     mixture_all[here, :] = mixture
     middle = rows + dot_nn(mixture, w_out[...])
@@ -766,19 +874,7 @@
     attn = grad_middle.astype(bf16)
     attn_all[here, :] = attn
     grad_mix[...] = dot_nt(attn, w_out[...]).astype(bf16).reshape(grad_mix.shape)
-    for place in range(0, patches, group):
-        for pair in range(HEADS // 2):
-            grads = attend_backward(
-                *[cut(packed, part, place, pair) for part in range(3)],
-                cut(grad_mix, 0, place, pair),
-                [weights_buf[place // group, 2 * pair + which] for which in range(2)],
-                low_half,
-            )
-            for part in range(3):
-                start = part * width + 128 * pair
-                packed[:, place : place + group, start : start + 128] = grads[part].reshape(
-                    steps, group, 128
-                )
+    attend_backward(units_of(True), scores, weights_buf, grad_scores, low_half)
     grad_packed = packed[...].reshape(tile, 3 * width)
     packed_all[here, :] = grad_packed
     grad_first = dot_nt(grad_packed, w_qkv[...])
@@ -796,19 +892,35 @@
         )
 
 
-def temporal_block(plan, length, rows, cotangent, weights, norms):
-    grad_specs, grad_shapes = grad_outputs(plan, weights)
+def load_weights(plan, held, room, matrices, local):
+    copy = pltpu.make_async_copy(held, room, local.at[0])
+    copy.start()
+    copy.wait()
+    assemble(plan, room, matrices, range(4))
+
+
+def weight_sources(plan, weights, norms, hidden):
+    width = norms.shape[1]
+    if plan is None:
+        return [*weights, norms], [whole(a.shape) for a in (*weights, norms)], []
+    scratch = [pltpu.VMEM(shape, bf16) for shape in matrix_shapes(width, hidden)]
+    scratch.append(pltpu.SemaphoreType.DMA((1,)))
+    return [weights, norms], [pl.BlockSpec(memory_space=pl.ANY), whole(norms.shape)], scratch
+
+
+def temporal_block(plan, length, rows, cotangent, weights, norms, hidden):
+    grad_specs, grad_shapes = grad_outputs(plan, norms.shape[1], hidden)
+    operands, specs, extra = weight_sources(plan, weights, norms, hidden)
     steps, patches, width = rows.shape
     tokens = steps * patches
-    hidden = weights[2].shape[1]
     part = TEMPORAL_TILE // steps
+    count = steps * PATCH_GROUP
+    unit_shape = (part // PATCH_GROUP * (HEADS // 2), count, 2 * count)
     slab = pl.BlockSpec((steps, part, width), lambda i: (0, i, 0))
     return pl.pallas_call(
         partial(temporal_kernel, plan),
         grid=(patches // part,),
-        in_specs=[pl.BlockSpec(memory_space=pltpu.SMEM), slab, slab]
-        + [whole(w.shape) for w in weights]
-        + [whole(norms.shape)],
+        in_specs=[pl.BlockSpec(memory_space=pltpu.SMEM), slab, slab] + specs,
         out_specs=[slab, slab] + grad_specs + [whole((4, 8, width))],
         out_shape=[
             jax.ShapeDtypeStruct(rows.shape, f32),
@@ -819,8 +931,10 @@
         scratch_shapes=[
             pltpu.VMEM((steps, part, 3 * width), bf16),
             pltpu.VMEM((TEMPORAL_TILE, hidden), bf16),
-            pltpu.VMEM((part // PATCH_GROUP, HEADS, steps * PATCH_GROUP, steps * PATCH_GROUP), bf16),
+            pltpu.VMEM(unit_shape, bf16),
             pltpu.VMEM((steps, part, width), bf16),
+            pltpu.VMEM(unit_shape, f32),
+            pltpu.VMEM(unit_shape, bf16),
             pltpu.VMEM((tokens, width), bf16),
             pltpu.VMEM((tokens, 3 * width), bf16),
             pltpu.VMEM((tokens, width), bf16),
@@ -829,18 +943,25 @@
             pltpu.VMEM((tokens, hidden), bf16),
             pltpu.VMEM((tokens, hidden), bf16),
             pltpu.VMEM((tokens, width), bf16),
-        ],
+        ]
+        + extra,
         compiler_params=pltpu.CompilerParams(vmem_limit_bytes=62 * MIB),
-    )(length, rows, cotangent, *weights, norms)
+    )(length, rows, cotangent, *operands)
 
 
 def spatial_backward_kernel(
-    plan, x_ref, grad_ref, packed_ref, weights_ref, middle_ref, slope_ref, mixture_all, active_all,
-    w_qkv, w_out, w_up, w_down, norm_ref,
-    before_ref, *refs,
+    plan, x_ref, grad_ref, packed_ref, weights_ref, middle_ref, slope_ref, mixture_all, active_all, *refs
 ):
-    outs, g_norm = refs[:-8], refs[-8]
-    grad_mix, first_all, packed_all, attn_all, second_all, hidden_all, branch_all = refs[-7:]
+    sources = 5 if plan is None else 2
+    refs, sources = refs[sources:], refs[:sources]
+    before_ref, *refs = refs
+    if plan is None:
+        w_qkv, w_out, w_up, w_down, norm_ref = sources
+    else:
+        *refs, w_qkv, w_out, w_up, w_down, local = refs
+        norm_ref = sources[1]
+    outs, g_norm = refs[:-10], refs[-10]
+    scores, grad_scores, grad_mix, first_all, packed_all, attn_all, second_all, hidden_all, branch_all = refs[-9:]
     step = pl.program_id(0)
     tile, width = x_ref.shape
     here = pl.ds(pl.multiple_of(step * tile, tile), tile)
@@ -848,6 +969,8 @@
     @pl.when(step == 0)
     def _():
         g_norm[...] = jnp.zeros_like(g_norm)
+        if plan is not None:
+            load_weights(plan, sources[0], outs[0], (w_qkv, w_out, w_up, w_down), local)
 
     grad_after = grad_ref[...]
     branch = grad_after.astype(bf16)
@@ -868,19 +991,23 @@
     for item in range(weights_ref.shape[0]):
         span = slice(item * frame, (item + 1) * frame)
         there = pl.ds(pl.multiple_of(step * tile + item * frame, frame), frame)
+        units = []
         for pair in range(HEADS // 2):
-            grads = attend_backward(
-                *[
-                    packed_ref[span, part * width + 128 * pair : part * width + 128 * (pair + 1)]
-                    for part in range(3)
-                ],
-                grad_mix[span, 128 * pair : 128 * (pair + 1)],
-                [weights_ref[item, 2 * pair + which] for which in range(2)],
-                low_half,
-            )
-            for part in range(3):
+
+            def cut(part, pair=pair, span=span):
                 start = part * width + 128 * pair
-                packed_all[there, start : start + 128] = grads[part]
+                return packed_ref[span, start : start + 128]
+
+            def cut_grad(pair=pair, span=span):
+                return grad_mix[span, 128 * pair : 128 * (pair + 1)]
+
+            def put(*values, pair=pair, there=there):
+                for part, value in enumerate(values):
+                    start = part * width + 128 * pair
+                    packed_all[there, start : start + 128] = value
+
+            units.append((partial(cut, 0), partial(cut, 1), partial(cut, 2), cut_grad, put))
+        attend_backward(units, scores, weights_ref.at[item], grad_scores, low_half)
     grad_first = dot_nt(packed_all[here, :], w_qkv[...])
     hat, scale = normalise(x_ref[...].astype(f32))
     first_all[here, :] = (hat * norm_ref[0:1] + norm_ref[1:2]).astype(bf16)
@@ -899,9 +1026,10 @@
 
 def spatial_backward(plan, x, grad, kept, weights, norms):
     packed, soft, mixture, middle, active, slope = kept
-    grad_specs, grad_shapes = grad_outputs(plan, weights)
     tokens, width = x.shape
-    hidden = weights[2].shape[1]
+    hidden = active.shape[1]
+    grad_specs, grad_shapes = grad_outputs(plan, width, hidden)
+    operands, specs, extra = weight_sources(plan, weights, norms, hidden)
     frame = soft.shape[2]
     tile = SPATIAL_TILE
     return pl.pallas_call(
@@ -911,14 +1039,13 @@
             tiles(tile, width),
             tiles(tile, width),
             tiles(tile, 3 * width),
-            tiles(tile // frame, HEADS, frame, frame),
+            tiles(tile // frame, HEADS // 2, frame, 2 * frame),
             tiles(tile, width),
             tiles(tile, hidden),
             whole(mixture.shape),
             whole(active.shape),
         ]
-        + [whole(w.shape) for w in weights]
-        + [whole(norms.shape)],
+        + specs,
         out_specs=[tiles(tile, width)]
         + grad_specs
         + [whole((4, 8, width))],
@@ -926,6 +1053,8 @@
         + grad_shapes
         + [jax.ShapeDtypeStruct((4, 8, width), f32)],
         scratch_shapes=[
+            pltpu.VMEM((HEADS // 2, frame, 2 * frame), f32),
+            pltpu.VMEM((HEADS // 2, frame, 2 * frame), bf16),
             pltpu.VMEM((tile, width), bf16),
             pltpu.VMEM((tokens, width), bf16),
             pltpu.VMEM((tokens, 3 * width), bf16),
@@ -933,9 +1062,10 @@
             pltpu.VMEM((tokens, width), bf16),
             pltpu.VMEM((tokens, hidden), bf16),
             pltpu.VMEM((tokens, width), bf16),
-        ],
+        ]
+        + extra,
         compiler_params=pltpu.CompilerParams(vmem_limit_bytes=62 * MIB),
-    )(x, grad, packed, soft, middle, slope, mixture, active, *weights, norms)
+    )(x, grad, packed, soft, middle, slope, mixture, active, *operands)
 
 
 def unpack(flat_weights, model_width, hidden_width):
@@ -975,18 +1105,21 @@
     clip_count, step_slots, patch_count, model_width = clip_tokens.shape
     shards = lax.axis_size("dp")
     plan = shard_plan(shards, model_width, FF) if shards == 32 else None
+    x = clip_tokens.reshape(-1, model_width)
     if plan is None:
         gathered = lax.all_gather(params.astype(bf16), "dp", axis=1, tiled=True)
         norm_whole = lax.all_gather(norm_par.astype(bf16), "dp", axis=0, tiled=True)
         norm_table = norm_whole.astype(f32).reshape(2, 4, model_width)
         spatial_weights = unpack(gathered[0], model_width, FF)
         temporal_weights = unpack(gathered[1], model_width, FF)
+        sources = (*spatial_weights, norm_table[0])
+        *kept, after = spatial_forward(plan, x, sources, patch_count, FF)
     else:
-        spatial_weights, temporal_weights, norm_table = gather_weights(
-            plan, params, norm_par, model_width, FF
+        sources = (params.reshape(2, -1, LANES), norm_par.reshape(1, LANES))
+        *kept, after, spatial_weights, temporal_weights, norm_table = spatial_forward(
+            plan, x, sources, patch_count, FF
         )
-    x = clip_tokens.reshape(-1, model_width)
-    *kept, after = spatial_forward(x, spatial_weights, norm_table[0], patch_count)
+        norm_table = norm_table.reshape(2, 4, model_width)
     result, grad_after, *temporal_grads, temporal_norm = temporal_block(
         plan,
         lengths,
@@ -994,6 +1127,7 @@
         cotangent.reshape(step_slots, patch_count, model_width),
         temporal_weights,
         norm_table[1],
+        FF,
     )
     grad_before, *spatial_grads, spatial_norm = spatial_backward(
         plan, x, grad_after.reshape(-1, model_width), kept, spatial_weights, norm_table[0]

time: 395 us -> 312 us (0.79)
  Pallas kernels: 376 us -> 297 us
    pallas_call x2 -> x1, Pallas kernels: 121 us -> 76.3 us  [spatial_forward(): pl.pallas_call(partial(spatial_forward_kernel, plan), grid=(2, count), in...]
    pallas_call x1, Pallas kernels: 112 us -> 83 us  [temporal_block(): pl.pallas_call(partial(temporal_kernel, plan), grid=(patches // part,), i...]
    pallas_call x1, Pallas kernels: 60.3 us -> 55.1 us  [spatial_backward(): pl.pallas_call(partial(spatial_backward_kernel, plan), grid=(tokens // ti...]
where the time goes in v3:
time: 312 us; the launch traced here: 307 us
  Pallas kernels  297 us (95%)
  other arithmetic  4.98 us (2%)
  local copies, waits for them, and re-layouts  3.5 us (1%)
    pallas_call x1, Pallas kernels, temporal_block(): pl.pallas_call(partial(temporal_kernel, plan), grid=(patches // part,), i...  83 us
    pallas_call x1, Pallas kernels, scatter_grads(): pl.pallas_call(partial(scatter_kernel, plan), in_specs=[pl.BlockSpec(memo...  82.9 us
    pallas_call x1, Pallas kernels, spatial_forward(): pl.pallas_call(partial(spatial_forward_kernel, plan), grid=(2, count), in...  76.3 us
    pallas_call x1, Pallas kernels, spatial_backward(): pl.pallas_call(partial(spatial_backward_kernel, plan), grid=(tokens // ti...  55.1 us

profile of v3, /device:TPU:0, one launch (start us, length us, event | category | flops | bytes accessed | tf_op | source)
XLA Modules:
  0.0 307.4 jit_solution(523639799050295493)
XLA Ops:
  1.3 2.1 copy.20
  3.4 76.3 %shard_map.160 = (bf16[2048,1536]{1,0:T(8,128)(2,1)}, bf16[8,4,256,512]{3,2,1,0:T(8,128)(2,1)}, bf16[2048,512]{1,0:T(8,128)(2,1)}, f32[2048,512]{1,0:T(8,128)}, ...) custom-call(bf16[2048,512]{1,0:T(8,128)(2,1)} %bitcast.22, ...), custom_call_target="tpu_custom_call" | custom-call | tf_op jit(solution)/shard_map/pallas_call | solution.py:330
  79.6 1.4 fusion.7
  81.0 83.0 %shard_map.161 = (f32[8,256,512]{2,1,0:T(8,128)}, f32[8,256,512]{2,1,0:T(8,128)}, bf16[4,2,2,2,784,128]{5,4,3,2,1,0:T(8,128)(2,1)}, f32[4,8,512]{2,1,0:T(8,128)}) custom-call(s32[1]{0:T(128)S(6)} %copy.21.length_ref, f32[8,256,512]{2,1,0:T(8,128)} %bitcast.24, bf16[8,256,512]{2,1,0:T(8,128)(2,1)} %bitcast.28, ...), custom_call_target="tpu_custom_call" | custom-call | tf_op jit(solution)/shard_map/pallas_call | solution.py:920
  164.0 55.1 %shard_map.162 = (f32[2048,512]{1,0:T(8,128)}, bf16[4,2,2,2,784,128]{5,4,3,2,1,0:T(8,128)(2,1)}, f32[4,8,512]{2,1,0:T(8,128)}) custom-call(bf16[2048,512]{1,0:T(8,128)(2,1)} %bitcast.23, f32[2048,512]{1,0:T(8,128)} %bitcast.25, bf16[2048,1536]{1,0:T(8,128)(2,1)} %get-tuple-element.32.packed_ref, bf16[8,4,256,512]{3,2,1,0:T(8,128)(2,1)} %get-tuple-element.33.weights_ref, ...), custom_call_target="tpu_custom_call" | custom-call | tf_op jit(solution)/shard_map/pallas_call | solution.py:1035
  219.1 0.0 copy-start.3
  219.1 0.0 copy-start.4
  219.2 0.0 copy-start.5
  219.2 0.0 copy-start
  219.2 0.0 copy-start.1
  219.2 0.0 copy-start.2
  219.2 82.9 %shard_map.163 = (f32[768,128]{1,0:T(8,128)S(1)}, f32[768,128]{1,0:T(8,128)S(1)}, f32[8,128]{1,0:T(8,128)S(1)}) custom-call(bf16[4,2,2,2,784,128]{5,4,3,2,1,0:T(8,128)(2,1)} %get-tuple-element.40.g0, bf16[4,2,2,2,784,128]{5,4,3,2,1,0:T(8,128)(2,1)} %get-tuple-element.41.g1), custom_call_target="tpu_custom_call" | custom-call | tf_op jit(solution)/shard_map/pallas_call | solution.py:719
  302.2 0.0 copy-done.3
  302.2 0.0 copy-done.4
  302.2 0.0 copy-done.5
  302.2 0.5 multiply_subtract_fusion.1
  302.7 0.0 copy-done
  302.7 0.0 copy-done.1
  302.7 0.0 copy-done.2
  302.7 4.4 %fusion.5 = (bf16[2,98304]{1,0:T(2,128)(2,1)}, f32[2,98304]{1,0:T(2,128)}, f32[2,98304]{1,0:T(2,128)}, f32[2,98304]{1,0:T(2,128)}) fusion(f32[2,98304]{1,0:T(2,128)S(1)} %copy-done, f32[1,98304]{1,0:T(1,128)S(1)} %bitcast.21, f32[1,98304]{1,0:T(1,128)S(1)} %bitcast.20, f32[2,98304]{1,0:T(2,128)S(1)} %copy-done.1, f32[2,98304]{1,0:T(2,128)S(1)} %copy-done.2), kind=kLoop, calls=%fused_computation.12 | loop fusion | flops 3342336 | bytes 5898240 | tf_op jit(solution)/shard_map/convert_element_type | solution.py:1160
Async XLA Ops:
  219.1 83.0 %copy-start.3 = (f32[128]{0:T(128)S(1)}, f32[128]{0:T(128)}, u32[]{:S(2)}) copy-start(f32[128]{0:T(128)} %param.15) | copy-start | bytes 1540
  219.1 83.0 %copy-start.4 = (f32[128]{0:T(128)S(1)}, f32[128]{0:T(128)}, u32[]{:S(2)}) copy-start(f32[128]{0:T(128)} %param.16) | copy-start | bytes 1540
  219.2 83.0 %copy-start.5 = (f32[128]{0:T(128)S(1)}, f32[128]{0:T(128)}, u32[]{:S(2)}) copy-start(f32[128]{0:T(128)} %param.17) | copy-start | bytes 1540
  219.2 83.6 %copy-start = (f32[2,98304]{1,0:T(2,128)S(1)}, f32[2,98304]{1,0:T(2,128)}, u32[]{:S(2)}) copy-start(f32[2,98304]{1,0:T(2,128)} %param.12) | copy-start | bytes 2359300
  219.2 83.6 %copy-start.1 = (f32[2,98304]{1,0:T(2,128)S(1)}, f32[2,98304]{1,0:T(2,128)}, u32[]{:S(2)}) copy-start(f32[2,98304]{1,0:T(2,128)} %param.13) | copy-start | bytes 2359300
  219.2 83.5 %copy-start.2 = (f32[2,98304]{1,0:T(2,128)S(1)}, f32[2,98304]{1,0:T(2,128)}, u32[]{:S(2)}) copy-start(f32[2,98304]{1,0:T(2,128)} %param.14) | copy-start | bytes 2359300

commit v4 on v3

--- a/solution.py
+++ b/solution.py
@@ -565,10 +565,20 @@
 
 
 class Scatter:
-    def __init__(self, place, own, r1, r2a, r2b, r3, r4, send, recv):
+    def __init__(self, place, own, room, send, recv, credit=None, leads=None):
         self.p, self.own = place, own
-        self.r1, self.r2a, self.r2b, self.r3, self.r4 = r1, r2a, r2b, r3, r4
-        self.send, self.recv = send, recv
+        rows, half = room[3].shape[1], room[1].shape[2]
+        self.low, self.high = pl.ds(0, half), pl.ds(half, rows - half)
+        self.r1, self.r2a, self.r2b, self.r3, self.r4 = room
+        self.send, self.recv, self.credit, self.leads = send, recv, credit, leads
+
+    def release(self, kind, q, device):
+        if self.leads is True:
+            pl.semaphore_signal(self.credit.at[kind, q], inc=1, device_id=(device,), device_id_type=MESH_IDS)
+
+    def claim(self, kind, q):
+        if self.leads is False:
+            pl.semaphore_wait(self.credit.at[kind, q], 1)
 
     def first(self, q):
         p = self.p
@@ -580,7 +590,7 @@
 
     def second(self, q):
         p = self.p
-        low, high = pl.ds(0, HALF), pl.ds(HALF, SHARD - HALF)
+        low, high = self.low, self.high
         return (
             remote(
                 self.r1.at[q, :, 1 - p.x, low], self.r2a.at[q], self.send.at[1, q], self.recv.at[1, q], p.across_x
@@ -592,7 +602,7 @@
 
     def third(self, q):
         p = self.p
-        low, high = pl.ds(0, HALF), pl.ds(HALF, SHARD - HALF)
+        low, high = self.low, self.high
         return (
             remote(
                 self.r2a.at[q, 1 - p.y], self.r3.at[q, low], self.send.at[3, q], self.recv.at[3, q], p.across_y
@@ -607,6 +617,7 @@
         return remote(self.r3.at[q], self.r4.at[p.z], self.send.at[5, q], self.recv.at[5, p.z], p.plane(q))
 
     def begin_first(self, q):
+        self.claim(0, q)
         for copy in self.first(q):
             copy.start()
 
@@ -615,7 +626,9 @@
             copy.wait_recv()
         for y in range(2):
             for x in range(2):
-                self.r1[q, y, x] = (self.r1[q, y, x].astype(f32) + mine[y, x].astype(f32)).astype(bf16)
+                self.r1[q, y, x] = self.r1[q, y, x] + mine(y, x)
+        self.claim(1, q)
+        self.claim(2, q)
         for copy in self.second(q):
             copy.start()
 
@@ -623,50 +636,79 @@
         p = self.p
         for copy in self.second(q):
             copy.wait_recv()
-        low, high = pl.ds(0, HALF), pl.ds(HALF, SHARD - HALF)
+        low, high = self.low, self.high
         for k in range(2):
-            self.r2a[q, k] = (self.r2a[q, k].astype(f32) + self.r1[q, k, p.x, low].astype(f32)).astype(bf16)
-            self.r2b[q, k] = (self.r2b[q, k].astype(f32) + self.r1[q, p.y, k, high].astype(f32)).astype(bf16)
+            self.r2a[q, k] = self.r2a[q, k] + self.r1[q, k, p.x, low]
+            self.r2b[q, k] = self.r2b[q, k] + self.r1[q, p.y, k, high]
         for copy in self.third(q):
             copy.start()
-
-    def begin_z(self, q):
+        for copy in self.second(q):
+            copy.wait_send()
+        self.release(0, q, p.sibling)
+
+    def begin_z(self, q, total):
         p = self.p
         for copy in self.third(q):
             copy.wait_recv()
-        low, high = pl.ds(0, HALF), pl.ds(HALF, SHARD - HALF)
-        self.r3[q, low] = (self.r3[q, low].astype(f32) + self.r2a[q, p.y].astype(f32)).astype(bf16)
-        self.r3[q, high] = (self.r3[q, high].astype(f32) + self.r2b[q, p.x].astype(f32)).astype(bf16)
+        low, high = self.low, self.high
+        self.r3[q, low] = self.r3[q, low] + self.r2a[q, p.y]
+        self.r3[q, high] = self.r3[q, high] + self.r2b[q, p.x]
 
         @pl.when(q != p.z)
         def _():
             self.along_z(q).start()
+
+        @pl.when(q == p.z)
+        def _():
+            total[...] = self.r3[q].astype(f32)
+
+        for copy in self.third(q):
+            copy.wait_send()
+        self.release(1, q, p.across_x)
+        self.release(2, q, p.across_y)
+
+    def leave_z(self, q):
+        p = self.p
+
+        @pl.when(q != p.z)
+        def _():
+            self.along_z(q).wait_send()
 
     def finish(self, total):
         p = self.p
-        for k in range(1, 4):
-            z = lax.rem(p.z + k, 4)
-            remote(self.r3.at[0], self.r4.at[z], self.send.at[5, 0], self.recv.at[5, z], p.me).wait_recv()
-        total[...] = self.r3[p.z].astype(f32)
-        for k in range(1, 4):
-            total[...] += self.r4[lax.rem(p.z + k, 4)].astype(f32)
-
-    def drain(self):
-        for q in range(4):
-            for copy in self.first(q) + self.second(q) + self.third(q):
+        planes = self.r3.shape[0]
+
+        @pl.when(p.z < planes)
+        def _():
+            for k in range(1, 4):
+                z = lax.rem(p.z + k, 4)
+                remote(self.r3.at[0], self.r4.at[z], self.send.at[5, 0], self.recv.at[5, z], p.me).wait_recv()
+            for k in range(1, 4):
+                total[...] += self.r4[lax.rem(p.z + k, 4)].astype(f32)
+
+        for q in range(planes):
+            for copy in self.first(q):
                 copy.wait_send()
-
-            @pl.when(q != self.p.z)
-            def _(q=q):
-                self.along_z(q).wait_send()
-
-
-SCATTER_SCRATCH = [
+            self.leave_z(q)
+
+
+SCATTER_ROOM = [
     pltpu.VMEM((4, 2, 2, SHARD, LANES), bf16),
     pltpu.VMEM((4, 2, HALF, LANES), bf16),
     pltpu.VMEM((4, 2, SHARD - HALF, LANES), bf16),
-    pltpu.VMEM((4, SHARD, LANES), bf16),
-    pltpu.VMEM((4, SHARD, LANES), bf16),
+    pltpu.VMEM((2, 4, SHARD, LANES), bf16),
+    pltpu.VMEM((2, 4, SHARD, LANES), bf16),
+]
+
+SMALL = 2 * ROW_TILE
+SMALL_ROOM = [
+    pltpu.VMEM((1, 2, 2, 2, SMALL, LANES), bf16),
+    pltpu.VMEM((1, 2, 2, SMALL, LANES), bf16),
+    pltpu.VMEM((1, 2, ROW_TILE, LANES), bf16),
+    pltpu.VMEM((1, 2, ROW_TILE, LANES), bf16),
+    pltpu.VMEM((1, SMALL, LANES), bf16),
+    pltpu.VMEM((4, SMALL, LANES), bf16),
+    pltpu.VMEM((SMALL, LANES), f32),
     pltpu.SemaphoreType.DMA((6, 4)),
     pltpu.SemaphoreType.DMA((6, 4)),
 ]
@@ -680,79 +722,26 @@
     on_pattern(plan, me, body)
 
 
-def scatter_kernel(plan, g0, g1, flat0, flat1, norm_out, total, mine, load, *rest):
-    place = Place(lax.axis_index("dp"))
-    enter(place)
-    count = len(SCATTER_SCRATCH)
-    scatters = []
-    for b, own in ((1, g1), (0, g0)):
-        s = Scatter(place, own, *rest[b * count : (b + 1) * count])
-        scatters.append((b, s, own))
-    for b, s, own in scatters:
-        for q in range(4):
-            s.begin_first(q)
-    for b, s, own in scatters:
-        for q in range(4):
-            copy = pltpu.make_async_copy(own.at[q, :, :, place.c], mine.at[b, q], load.at[b, q])
-            copy.start()
-        for q in range(4):
-            pltpu.make_async_copy(own.at[q, :, :, place.c], mine.at[b, q], load.at[b, q]).wait()
-            s.begin_second(q, mine.at[b, q])
-        for q in range(4):
-            s.begin_third(q)
-        for q in range(4):
-            s.begin_z(q)
-    for b, s, own in scatters:
-        s.finish(total)
-        unload_shard(plan, place.me, total, (flat0, flat1)[b])
-        if b == 1:
-            norm_out[...] = total[SHARD - ROW_TILE : SHARD - ROW_TILE + 8]
-        else:
-            norm_out[...] += total[SHARD - ROW_TILE : SHARD - ROW_TILE + 8]
-    for b, s, own in scatters:
-        s.drain()
-
-
-def scatter_grads(plan, grads):
-    vmem = pl.BlockSpec(memory_space=pltpu.VMEM)
-    rows = SHARD - ROW_TILE
-    flat0, flat1, norm = pl.pallas_call(
-        partial(scatter_kernel, plan),
-        in_specs=[pl.BlockSpec(memory_space=pl.ANY)] * 2,
-        out_specs=[vmem] * 3,
-        out_shape=[
-            jax.ShapeDtypeStruct((rows, LANES), f32),
-            jax.ShapeDtypeStruct((rows, LANES), f32),
-            jax.ShapeDtypeStruct((8, LANES), f32),
-        ],
-        scratch_shapes=[
-            pltpu.VMEM((SHARD, LANES), f32),
-            pltpu.VMEM((2, 4, 2, 2, SHARD, LANES), bf16),
-            pltpu.SemaphoreType.DMA((2, 4)),
-        ]
-        + SCATTER_SCRATCH * 2,
-        compiler_params=pltpu.CompilerParams(
-            collective_id=1, has_side_effects=True, vmem_limit_bytes=48 * MIB
-        ),
-    )(*grads)
-    return jnp.stack([flat0.reshape(-1), flat1.reshape(-1)]), norm[0] + norm[1]
-
-
-def store_travel(plan, own, index, start, value):
+def store_travel(plan, own, index, top, start, value):
     for device, entries in enumerate(plan):
         z, y, x, c = coordinates(device)
         for entry, row, count, block, _, _, place in entries:
             column = LANES * block - start
-            if entry == index and 0 <= column < value.shape[1]:
-                own[z, y, x, c, place : place + count, :] = value[row : row + count, column : column + LANES]
-
-
-def store_norms(plan, own, block, sums):
+            low, high = max(row, top), min(row + count, top + value.shape[0])
+            if entry == index and 0 <= column < value.shape[1] and low < high:
+                own[z, y, x, c, place + low - row : place + high - row, :] = value[
+                    low - top : high - top, column : column + LANES
+                ]
+
+
+def store_norms(plan, own, block, sums, planes, first=SHARD - ROW_TILE):
     width = sums.shape[2]
     per_row = width // LANES
     line = lax.broadcasted_iota(jnp.int32, (ROW_TILE, LANES), 0)
     for device in range(len(plan)):
         z, y, x, c = coordinates(device)
+        if z not in planes:
+            continue
         row = device // per_row - 4 * block
         if 0 <= row < 4:
             column = LANES * (device % per_row)
@@ -761,14 +750,14 @@
             rows = jnp.where(line == 0, coarse, jnp.where(line == 1, value - coarse, 0.0))
         else:
             rows = jnp.zeros((ROW_TILE, LANES), f32)
-        own[z, y, x, c, SHARD - ROW_TILE : SHARD, :] = rows.astype(bf16)
+        own[z, y, x, c, first : first + ROW_TILE, :] = rows.astype(bf16)
 
 
 def weight_grads(first, grad_packed, mixture, attn, second, grad_hidden, active, branch, store, chunk=512):
     sides = ((first, grad_packed), (mixture, attn), (second, grad_hidden), (active, branch))
     for index, (left, right) in enumerate(sides):
         for start in range(0, right.shape[1], chunk):
-            store(index, start, dot_tn(left[...], right[:, start : start + chunk]).astype(bf16))
+            store(index, 0, start, dot_tn(left[...], right[:, start : start + chunk]).astype(bf16))
 
 
 def grad_outputs(plan, width, hidden):
@@ -776,12 +765,11 @@
     return [whole(s) for s in shapes], [jax.ShapeDtypeStruct(s, bf16) for s in shapes]
 
 
-def storing(plan, block, outs, sums):
+def storing(plan, outs):
     if plan is None:
-        def store(index, start, value):
-            outs[index][:, start : start + value.shape[1]] = value
+        def store(index, top, start, value):
+            outs[index][top : top + value.shape[0], start : start + value.shape[1]] = value
         return store
-    store_norms(plan, outs[0], block, sums)
     return partial(store_travel, plan, outs[0])
 
 
@@ -886,9 +874,11 @@
 
     @pl.when(step == pl.num_programs(0) - 1)
     def _():
+        if plan is not None:
+            store_norms(plan, outs[0], 1, g_norm, range(4))
         weight_grads(
             first_all, packed_all, mixture_all, attn_all, second_all, hidden_all, active_all,
-            branch_all, storing(plan, 1, outs, g_norm),
+            branch_all, storing(plan, outs),
         )
 
 
@@ -950,121 +940,285 @@
 
 
 def spatial_backward_kernel(
-    plan, x_ref, grad_ref, packed_ref, weights_ref, middle_ref, slope_ref, mixture_all, active_all, *refs
+    plan, x_ref, grad_ref, packed_ref, weights_ref, middle_ref, slope_ref, mixture_hbm, active_hbm, *refs
 ):
-    sources = 5 if plan is None else 2
-    refs, sources = refs[sources:], refs[:sources]
-    before_ref, *refs = refs
+    step, last = pl.program_id(1), pl.num_programs(1) - 1
+    opening, midway, closing = [pl.program_id(0) == k for k in range(3)]
     if plan is None:
-        w_qkv, w_out, w_up, w_down, norm_ref = sources
+        w_qkv, w_out, w_up, w_down, norm_ref, before_ref, *outs, g_norm = refs[:11]
+        refs = refs[11:]
     else:
-        *refs, w_qkv, w_out, w_up, w_down, local = refs
-        norm_ref = sources[1]
-    outs, g_norm = refs[:-10], refs[-10]
-    scores, grad_scores, grad_mix, first_all, packed_all, attn_all, second_all, hidden_all, branch_all = refs[-9:]
-    step = pl.program_id(0)
+        held, norm_ref, own_next, before_ref, flat0, flat1, norm_out = refs[:7]
+        own_small, *room_small, total_small, send_small, recv_small = refs[-len(SMALL_ROOM) :]
+        *refs, total, total_rest, own, mine, load, send, recv, credit = refs[7 : -len(SMALL_ROOM)]
+        room, refs = refs[-5:], refs[:-5]
+        *refs, g_norm, w_qkv, w_out, w_up, w_down, local = refs
+        outs = [own]
+        place = Place(lax.axis_index("dp"))
+        rooms = [(*room[:3], room[3].at[k], room[4].at[k]) for k in range(2)]
+        lead = Scatter(place, own_next, rooms[0], send.at[0], recv.at[0], credit, True)
+        rest = Scatter(place, own, rooms[1], send.at[1], recv.at[1], credit, False)
+        small = Scatter(place, own_small, room_small, send_small, recv_small)
+    scores, grad_scores, grad_mix, middle_all, second_all, hidden_all, attn_all, branch_all, side, side_sem = refs
+    store = storing(plan, outs)
     tile, width = x_ref.shape
+    hidden = slope_ref.shape[1]
     here = pl.ds(pl.multiple_of(step * tile, tile), tile)
 
-    @pl.when(step == 0)
+    def own_shards(q):
+        return pltpu.make_async_copy(own_next.at[q, :, :, place.c], mine.at[q % 2], load.at[q % 2])
+
+    def lead_second(q):
+        own_shards(q).wait()
+        lead.begin_second(q, lambda y, x: mine[q % 2, y, x])
+        if q < 2:
+            own_shards(q + 2).start()
+
+    def rest_second(q):
+        rest.begin_second(q, lambda y, x: own[q, y, x, place.c])
+
+    def at(passing, when, *actions):
+        @pl.when(passing & (step == when))
+        def _():
+            for action, *q in actions:
+                action(*q)
+
+    def begin():
+        enter(place)
+        for q in range(4):
+            lead.begin_first(q)
+        own_shards(0).start()
+        own_shards(1).start()
+        load_weights(plan, held, own, (w_qkv, w_out, w_up, w_down), local)
+        lead_second(0)
+        lead_second(1)
+
+    def lead_finish():
+        lead.finish(total)
+        unload_shard(plan, place.me, total, flat1)
+        norm_out[...] = total[SHARD - ROW_TILE : SHARD - ROW_TILE + 8]
+
+    @pl.when(opening & (step == 0))
     def _():
         g_norm[...] = jnp.zeros_like(g_norm)
+
+    if plan is not None:
+        at(opening, 0, (begin,))
+        at(opening, 1, (lead_second, 2))
+        at(opening, 2, (lead_second, 3))
+        at(opening, 3, (lead.begin_third, 0))
+        at(opening, 5, (lead.begin_third, 1))
+        at(opening, 7, (lead.begin_z, 0, total))
+        at(midway, 0, (lead.begin_z, 3, total))
+        at(midway, 1, (rest_second, 3))
+        at(midway, 3, (rest.begin_third, 1))
+        at(midway, 5, (rest.begin_third, 2))
+        at(midway, 7, (rest.begin_z, 1, total_rest))
+        at(closing, 1, (rest_second, 0))
+        at(closing, 3, (rest.begin_z, 3, total_rest))
+        at(closing, 5, (rest.begin_third, 0))
+
+    def side_copy(k):
+        source = mixture_hbm if k == 0 else active_hbm.at[:, pl.ds((k - 1) * width, width)]
+        return pltpu.make_async_copy(source, side.at[k % 2], side_sem.at[k % 2])
+
+    @pl.when(opening & (step == last))
+    def _():
+        side_copy(0).start()
+        side_copy(1).start()
+
+    @pl.when(opening)
+    def _():
+        grad_after = grad_ref[...]
+        branch = grad_after.astype(bf16)
+        branch_all[here, :] = branch
+        hidden_backward(branch, w_down, slope_ref, hidden_all.at[here, :])
+        grad_second = dot_nt(hidden_all[here, :], w_up[...])
+        hat, scale = normalise(middle_ref[...])
+        second_all[here, :] = (hat * norm_ref[2:3] + norm_ref[3:4]).astype(bf16)
+        grad_rows, gain, shift = norm_backward(hat, scale, norm_ref[2:3], grad_second)
+        g_norm[2] += gain
+        g_norm[3] += shift
+        grad_middle = grad_after + grad_rows
+        middle_all[here, :] = grad_middle
+        attn_all[here, :] = grad_middle.astype(bf16)
+
+    @pl.when(opening & (step == last))
+    def _():
         if plan is not None:
-            load_weights(plan, sources[0], outs[0], (w_qkv, w_out, w_up, w_down), local)
-
-    grad_after = grad_ref[...]
-    branch = grad_after.astype(bf16)
-    branch_all[here, :] = branch
-    hidden_backward(branch, w_down, slope_ref, hidden_all.at[here, :])
-    grad_second = dot_nt(hidden_all[here, :], w_up[...])
-    hat, scale = normalise(middle_ref[...])
-    second_all[here, :] = (hat * norm_ref[2:3] + norm_ref[3:4]).astype(bf16)
-    grad_rows, gain, shift = norm_backward(hat, scale, norm_ref[2:3], grad_second)
-    g_norm[2] += gain
-    g_norm[3] += shift
-    grad_middle = grad_after + grad_rows
-    attn = grad_middle.astype(bf16)
-    attn_all[here, :] = attn
-    grad_mix[...] = dot_nt(attn, w_out[...]).astype(bf16)
-    frame = weights_ref.shape[2]
-    low_half = lane_halves(frame)
-    for item in range(weights_ref.shape[0]):
-        span = slice(item * frame, (item + 1) * frame)
-        there = pl.ds(pl.multiple_of(step * tile + item * frame, frame), frame)
-        units = []
-        for pair in range(HEADS // 2):
-
-            def cut(part, pair=pair, span=span):
-                start = part * width + 128 * pair
-                return packed_ref[span, start : start + 128]
-
-            def cut_grad(pair=pair, span=span):
-                return grad_mix[span, 128 * pair : 128 * (pair + 1)]
-
-            def put(*values, pair=pair, there=there):
-                for part, value in enumerate(values):
+            lead.begin_third(2)
+        for start in range(0, hidden, width):
+            value = dot_tn(second_all[...], hidden_all[:, start : start + width])
+            store(2, 0, start, value.astype(bf16))
+        if plan is not None:
+            lead.begin_third(3)
+        side_copy(0).wait()
+        store(1, 0, 0, dot_tn(side[0], attn_all[...]).astype(bf16))
+        if plan is not None:
+            store_norms(plan, own, 0, g_norm, (0, 1, 2, 3))
+            rest.begin_first(1)
+            lead.begin_z(1, total)
+        count = hidden // width
+        for k in range(1, count + 1):
+            if k < count:
+                side_copy(k + 1).start()
+            side_copy(k).wait()
+            store(3, (k - 1) * width, 0, dot_tn(side[k % 2], branch_all[...]).astype(bf16))
+            if plan is not None:
+                if k == 1:
+                    rest.begin_first(2)
+                if k == 2:
+                    lead.begin_z(2, total)
+                    rest_second(1)
+        if plan is not None:
+            rest.begin_first(3)
+            rest_second(2)
+
+    @pl.when(midway)
+    def _():
+        hat, _ = normalise(x_ref[...].astype(f32))
+        second_all[here, :] = (hat * norm_ref[0:1] + norm_ref[1:2]).astype(bf16)
+        grad_mix[...] = dot_nt(attn_all[here, :], w_out[...]).astype(bf16)
+        frame = weights_ref.shape[2]
+        low_half = lane_halves(frame)
+        for item in range(weights_ref.shape[0]):
+            span = slice(item * frame, (item + 1) * frame)
+            there = pl.ds(pl.multiple_of(step * tile + item * frame, frame), frame)
+            units = []
+            for pair in range(HEADS // 2):
+
+                def cut(part, pair=pair, span=span):
                     start = part * width + 128 * pair
-                    packed_all[there, start : start + 128] = value
-
-            units.append((partial(cut, 0), partial(cut, 1), partial(cut, 2), cut_grad, put))
-        attend_backward(units, scores, weights_ref.at[item], grad_scores, low_half)
-    grad_first = dot_nt(packed_all[here, :], w_qkv[...])
-    hat, scale = normalise(x_ref[...].astype(f32))
-    first_all[here, :] = (hat * norm_ref[0:1] + norm_ref[1:2]).astype(bf16)
-    grad_rows, gain, shift = norm_backward(hat, scale, norm_ref[0:1], grad_first)
-    g_norm[0] += gain
-    g_norm[1] += shift
-    before_ref[...] = grad_middle + grad_rows
-
-    @pl.when(step == pl.num_programs(0) - 1)
+                    return packed_ref[span, start : start + 128]
+
+                def cut_grad(pair=pair, span=span):
+                    return grad_mix[span, 128 * pair : 128 * (pair + 1)]
+
+                def put(*values, pair=pair, there=there):
+                    for part, value in enumerate(values):
+                        start = part * width + 128 * pair
+                        hidden_all[there, start : start + 128] = value
+
+                units.append((partial(cut, 0), partial(cut, 1), partial(cut, 2), cut_grad, put))
+            attend_backward(units, scores, weights_ref.at[item], grad_scores, low_half)
+
+    @pl.when(midway & (step == last))
     def _():
-        weight_grads(
-            first_all, packed_all, mixture_all, attn_all, second_all, hidden_all, active_all,
-            branch_all, storing(plan, 0, outs, g_norm),
-        )
-
-
-def spatial_backward(plan, x, grad, kept, weights, norms):
+        for start in range(0, 3 * width, width):
+            value = dot_tn(second_all[...], hidden_all[:, start : start + width])
+            store(0, 0, start, value.astype(bf16))
+        if plan is not None:
+            rest.begin_first(0)
+            rest.begin_third(3)
+            rest.begin_z(2, total_rest)
+            lead_finish()
+
+    @pl.when(closing)
+    def _():
+        grad_first = dot_nt(hidden_all[here, 0 : 3 * width], w_qkv[...])
+        hat, scale = normalise(x_ref[...].astype(f32))
+        grad_rows, gain, shift = norm_backward(hat, scale, norm_ref[0:1], grad_first)
+        g_norm[0] += gain
+        g_norm[1] += shift
+        before_ref[...] = middle_all[here, :] + grad_rows
+
+    if plan is not None:
+
+        @pl.when(closing & (step == last))
+        def _():
+            own_small[...] = jnp.zeros_like(own_small)
+            store_norms(plan, own_small, 0, g_norm, (0,), 0)
+            small.begin_first(0)
+            rest.begin_z(0, total_rest)
+            small.begin_second(0, lambda y, x: own_small[0, y, x, place.c])
+            small.begin_third(0)
+            total_small[...] = jnp.zeros_like(total_small)
+            small.begin_z(0, total_small)
+            small.finish(total_small)
+            rest.finish(total_rest)
+            unload_shard(plan, place.me, total_rest, flat0)
+            norm_out[...] += total_rest[SHARD - ROW_TILE : SHARD - ROW_TILE + 8]
+
+            @pl.when(place.z == 0)
+            def _():
+                norm_out[...] += total_small[0:8]
+
+
+def spatial_backward(plan, x, grad, kept, weights, norms, own_next):
     packed, soft, mixture, middle, active, slope = kept
     tokens, width = x.shape
     hidden = active.shape[1]
-    grad_specs, grad_shapes = grad_outputs(plan, width, hidden)
     operands, specs, extra = weight_sources(plan, weights, norms, hidden)
     frame = soft.shape[2]
     tile = SPATIAL_TILE
+    count = tokens // tile
+
+    def opening(*rest):
+        return pl.BlockSpec(rest, lambda p, i: (i + (p + 1) // 2 * (count - 1 - i),) + (0,) * (len(rest) - 1))
+
+    def midway(*rest):
+        return pl.BlockSpec(rest, lambda p, i: (p * (2 - p) * i + p // 2 * (count - 1),) + (0,) * (len(rest) - 1))
+
+    def closing(*rest):
+        return pl.BlockSpec(rest, lambda p, i: (p // 2 * i,) + (0,) * (len(rest) - 1))
+
+    anywhere = pl.BlockSpec(memory_space=pl.ANY)
+    norm_sums = (4, 8, width)
+    out_specs, out_shape = [closing(tile, width)], [jax.ShapeDtypeStruct((tokens, width), f32)]
+    scratch = [
+        pltpu.VMEM((HEADS // 2, frame, 2 * frame), f32),
+        pltpu.VMEM((HEADS // 2, frame, 2 * frame), bf16),
+        pltpu.VMEM((tile, width), bf16),
+        pltpu.VMEM((tokens, width), f32),
+        pltpu.VMEM((tokens, width), bf16),
+        pltpu.VMEM((tokens, hidden), bf16),
+        pltpu.VMEM((tokens, width), bf16),
+        pltpu.VMEM((tokens, width), bf16),
+        pltpu.VMEM((2, tokens, width), bf16),
+        pltpu.SemaphoreType.DMA((2,)),
+    ]
+    params = dict(vmem_limit_bytes=63 * MIB)
+    if plan is None:
+        grad_specs, grad_shapes = grad_outputs(plan, width, hidden)
+        out_specs += grad_specs + [whole(norm_sums)]
+        out_shape += grad_shapes + [jax.ShapeDtypeStruct(norm_sums, f32)]
+    else:
+        rows = SHARD - ROW_TILE
+        for shape in ((rows, LANES), (rows, LANES), (8, LANES)):
+            out_specs.append(whole(shape))
+            out_shape.append(jax.ShapeDtypeStruct(shape, f32))
+        scratch += [pltpu.VMEM(norm_sums, f32)] + extra + SCATTER_ROOM
+        scratch += [
+            pltpu.VMEM((SHARD, LANES), f32),
+            pltpu.VMEM((SHARD, LANES), f32),
+            pltpu.VMEM((4, 2, 2, 2, SHARD, LANES), bf16),
+            pltpu.VMEM((2, 2, 2, SHARD, LANES), bf16),
+            pltpu.SemaphoreType.DMA((2,)),
+            pltpu.SemaphoreType.DMA((2, 6, 4)),
+            pltpu.SemaphoreType.DMA((2, 6, 4)),
+            pltpu.SemaphoreType.REGULAR((3, 4)),
+        ]
+        scratch += SMALL_ROOM
+        operands, specs = operands + [own_next], specs + [anywhere]
+        params |= dict(collective_id=1, has_side_effects=True)
     return pl.pallas_call(
         partial(spatial_backward_kernel, plan),
-        grid=(tokens // tile,),
+        grid=(3, count),
         in_specs=[
-            tiles(tile, width),
-            tiles(tile, width),
-            tiles(tile, 3 * width),
-            tiles(tile // frame, HEADS // 2, frame, 2 * frame),
-            tiles(tile, width),
-            tiles(tile, hidden),
-            whole(mixture.shape),
-            whole(active.shape),
+            pl.BlockSpec((tile, width), lambda p, i: ((p + 1) // 2 * i, 0)),
+            opening(tile, width),
+            midway(tile, 3 * width),
+            midway(tile // frame, HEADS // 2, frame, 2 * frame),
+            opening(tile, width),
+            opening(tile, hidden),
+            anywhere,
+            anywhere,
         ]
         + specs,
-        out_specs=[tiles(tile, width)]
-        + grad_specs
-        + [whole((4, 8, width))],
-        out_shape=[jax.ShapeDtypeStruct((tokens, width), f32)]
-        + grad_shapes
-        + [jax.ShapeDtypeStruct((4, 8, width), f32)],
-        scratch_shapes=[
-            pltpu.VMEM((HEADS // 2, frame, 2 * frame), f32),
-            pltpu.VMEM((HEADS // 2, frame, 2 * frame), bf16),
-            pltpu.VMEM((tile, width), bf16),
-            pltpu.VMEM((tokens, width), bf16),
-            pltpu.VMEM((tokens, 3 * width), bf16),
-            pltpu.VMEM((tokens, width), bf16),
-            pltpu.VMEM((tokens, width), bf16),
-            pltpu.VMEM((tokens, hidden), bf16),
-            pltpu.VMEM((tokens, width), bf16),
-        ]
-        + extra,
-        compiler_params=pltpu.CompilerParams(vmem_limit_bytes=62 * MIB),
+        out_specs=out_specs,
+        out_shape=out_shape,
+        scratch_shapes=scratch,
+        compiler_params=pltpu.CompilerParams(**params),
     )(x, grad, packed, soft, middle, slope, mixture, active, *operands)
 
 
@@ -1130,9 +1284,8 @@
         FF,
     )
     grad_before, *spatial_grads, spatial_norm = spatial_backward(
-        plan, x, grad_after.reshape(-1, model_width), kept, spatial_weights, norm_table[0]
+        plan, x, grad_after.reshape(-1, model_width), kept, spatial_weights, norm_table[0], temporal_grads[0]
     )
-
     if plan is None:
 
         def scatter(grads):
@@ -1143,7 +1296,8 @@
         norm_grad = jnp.stack([spatial_norm, temporal_norm]).sum(axis=2).reshape(-1)
         norm_sum = lax.psum_scatter(norm_grad, "dp", scatter_dimension=0, tiled=True)
     else:
-        weight_sum, norm_sum = scatter_grads(plan, (spatial_grads[0], temporal_grads[0]))
+        weight_sum = jnp.stack([g.reshape(-1) for g in spatial_grads])
+        norm_sum = spatial_norm[0] + spatial_norm[1]
     step_value = float(STEP)
     new_params, new_moment, new_second = adamw(
         params, param_moment, param_second, weight_sum, step_value, learn_rate, weight_decay

time: 312 us -> 289 us (0.926)
  Pallas kernels: 297 us -> 270 us
    pallas_call x2 -> x1, Pallas kernels: 138 us -> 120 us  [spatial_backward(): pl.pallas_call(partial(spatial_backward_kernel, plan), grid=(3, count), i...]
    pallas_call x1, Pallas kernels: 83 us -> 72.8 us  [temporal_block(): pl.pallas_call(partial(temporal_kernel, plan), grid=(patches // part,), i...]
where the time goes in v4:
time: 289 us; the launch traced here: 284 us
  Pallas kernels  270 us (93%)
  other arithmetic  7.01 us (2%)
  local copies, waits for them, and re-layouts  5.51 us (2%)
    pallas_call x1, Pallas kernels, spatial_backward(): pl.pallas_call(partial(spatial_backward_kernel, plan), grid=(3, count), i...  120 us
    pallas_call x1, Pallas kernels, spatial_forward(): pl.pallas_call(partial(spatial_forward_kernel, plan), grid=(2, count), in...  76.4 us
    pallas_call x1, Pallas kernels, temporal_block(): pl.pallas_call(partial(temporal_kernel, plan), grid=(patches // part,), i...  72.8 us

profile of v4, /device:TPU:0, one launch (start us, length us, event | category | flops | bytes accessed | tf_op | source)
XLA Modules:
  0.0 283.6 jit_solution(12946161313376639959)
XLA Ops:
  1.3 2.1 copy.20
  3.4 76.4 %shard_map.160 = (bf16[2048,1536]{1,0:T(8,128)(2,1)}, bf16[8,4,256,512]{3,2,1,0:T(8,128)(2,1)}, bf16[2048,512]{1,0:T(8,128)(2,1)}, f32[2048,512]{1,0:T(8,128)}, ...) custom-call(bf16[2048,512]{1,0:T(8,128)(2,1)} %bitcast.20, ...), custom_call_target="tpu_custom_call" | custom-call | tf_op jit(solution)/shard_map/pallas_call | solution.py:330
  79.8 1.4 fusion.7
  81.2 72.8 %shard_map.161 = (f32[8,256,512]{2,1,0:T(8,128)}, f32[8,256,512]{2,1,0:T(8,128)}, bf16[4,2,2,2,784,128]{5,4,3,2,1,0:T(8,128)(2,1)}, f32[4,8,512]{2,1,0:T(8,128)}) custom-call(s32[1]{0:T(128)S(6)} %copy.22.length_ref, f32[8,256,512]{2,1,0:T(8,128)} %bitcast.23, bf16[8,256,512]{2,1,0:T(8,128)(2,1)} %bitcast.27, ...), custom_call_target="tpu_custom_call" | custom-call | tf_op jit(solution)/shard_map/pallas_call | solution.py:910
  154.0 0.0 copy-start.2
  154.0 0.0 copy-start.3
  154.0 0.0 copy-start.4
  154.0 0.0 copy-start.1
  154.0 120.3 %shard_map.162 = (f32[2048,512]{1,0:T(8,128)}, f32[768,128]{1,0:T(8,128)}, f32[768,128]{1,0:T(8,128)}, f32[8,128]{1,0:T(8,128)}) custom-call(bf16[2048,512]{1,0:T(8,128)(2,1)} %bitcast.21, f32[2048,512]{1,0:T(8,128)} %bitcast.24, bf16[2048,1536]{1,0:T(8,128)(2,1)} %get-tuple-element.31.packed_ref, bf16[8,4,256,512]{3,2,1,0:T(8,128)(2,1)} %get-tuple-element.32.weights_ref, ...), custom_call_target="tpu_custom_call" | custom-call | tf_op jit(solution)/shard_map/pallas_call | solution.py:1204
  274.4 0.0 copy-start
  274.4 0.0 copy-done.2
  274.4 0.0 copy-done.3
  274.4 0.0 copy-done.4
  274.4 1.4 multiply_subtract_fusion.1
  275.8 0.0 copy-done.1
  275.8 5.6 %fusion.5 = (bf16[2,98304]{1,0:T(2,128)(2,1)}, f32[2,98304]{1,0:T(2,128)}, f32[2,98304]{1,0:T(2,128)}, f32[2,98304]{1,0:T(2,128)}) fusion(f32[2,98304]{1,0:T(2,128)S(1)} %copy-done.1, f32[1,98304]{1,0:T(1,128)} %bitcast.29, f32[1,98304]{1,0:T(1,128)} %bitcast.28, f32[2,98304]{1,0:T(2,128)} %param.13, f32[2,98304]{1,0:T(2,128)} %param.14), kind=kLoop, calls=%fused_computation.12 | loop fusion | flops 3342336 | bytes 5898240 | tf_op jit(solution)/shard_map/convert_element_type | solution.py:1314
  281.4 0.0 copy-done
  281.4 2.0 copy.23
Async XLA Ops:
  154.0 120.4 %copy-start.2 = (f32[128]{0:T(128)S(1)}, f32[128]{0:T(128)}, u32[]{:S(2)}) copy-start(f32[128]{0:T(128)} %param.15) | copy-start | bytes 1540
  154.0 120.4 %copy-start.3 = (f32[128]{0:T(128)S(1)}, f32[128]{0:T(128)}, u32[]{:S(2)}) copy-start(f32[128]{0:T(128)} %param.16) | copy-start | bytes 1540
  154.0 120.4 %copy-start.4 = (f32[128]{0:T(128)S(1)}, f32[128]{0:T(128)}, u32[]{:S(2)}) copy-start(f32[128]{0:T(128)} %param.17) | copy-start | bytes 1540
  154.0 121.8 %copy-start.1 = (f32[2,98304]{1,0:T(2,128)S(1)}, f32[2,98304]{1,0:T(2,128)}, u32[]{:S(2)}) copy-start(f32[2,98304]{1,0:T(2,128)} %param.12) | copy-start | bytes 2359300
  274.4 7.1 %copy-start = (f32[2048,512]{1,0:T(8,128)S(1)}, f32[2048,512]{1,0:T(8,128)}, u32[]{:S(2)}) copy-start(f32[2048,512]{1,0:T(8,128)} %get-tuple-element.39) | copy-start | bytes 12582916

commit v5 on v4

--- a/solution.py
+++ b/solution.py
@@ -174,9 +174,9 @@
         @pl.when(opening & (step == 0))
         def _():
             enter(place)
-            load_shard(plan, place.me, shard_ref.at[0], norm_par_ref, held.at[place.z, place.y, place.x, place.c])
+            load_shard(plan, place.me, 0, shard_ref, norm_par_ref, held.at[place.z, place.y, place.x, place.c])
             now.start_z()
-            load_shard(plan, place.me, shard_ref.at[1], norm_par_ref, staged)
+            load_shard(plan, place.me, 1, shard_ref, norm_par_ref, staged)
             copy = pltpu.make_async_copy(
                 staged, held_next.at[place.z, place.y, place.x, place.c], local.at[1]
             )
@@ -186,8 +186,8 @@
             now.begin_second(0)
             for q in range(1, 4):
                 now.begin_first(q)
+            later.start_z()
             now.begin_third(0)
-            later.start_z()
             gathered(0)
 
         @pl.when(opening & (step == 1))
@@ -199,32 +199,34 @@
         def _():
             now.begin_second(3)
 
-        @pl.when(opening & (step == 3))
+        @pl.when(opening & (step == 4))
         def _():
             now.begin_third(1)
+            now.begin_third(2)
+
+        @pl.when(opening & (step == 5))
+        def _():
             for q in range(4):
                 later.begin_first(q)
 
-        @pl.when(opening & (step == 4))
-        def _():
-            now.begin_third(2)
-            later.begin_second(0)
-
-        @pl.when(opening & (step == 6))
+        @pl.when(opening & (step == 7))
         def _():
             now.begin_third(3)
-            later.begin_second(1)
 
         @pl.when(jnp.logical_not(opening) & (step == 0))
         def _():
-            later.begin_second(2)
-            later.begin_second(3)
             gathered(1, 2, 3)
             keep.start()
 
         for q in range(4):
 
-            @pl.when(jnp.logical_not(opening) & (step == 2 * q + 1))
+            @pl.when(jnp.logical_not(opening) & (step == q + 1))
+            def _(q=q):
+                later.begin_second(q)
+
+        for q in range(3):
+
+            @pl.when(jnp.logical_not(opening) & (step == q + 5))
             def _(q=q):
                 later.begin_third(q)
 
@@ -267,6 +269,7 @@
 
         @pl.when(jnp.logical_not(opening) & (step == last))
         def _():
+            later.begin_third(3)
             for q in range(4):
                 later.finish(q)
             keep.wait()
@@ -528,10 +531,10 @@
                 copy.wait_send()
 
 
-def load_shard(plan, me, shard_ref, norm_ref, held_here):
+def load_shard(plan, me, block, shard_ref, norm_ref, held_here):
     def body(layout):
         for count, flat, stride, place in layout:
-            held_here[pl.ds(place, count), :] = shard_ref[pl.ds(flat, count, stride), :].astype(bf16)
+            held_here[pl.ds(place, count), :] = shard_ref[pl.ds(2 * flat + block, count, 2 * stride), :].astype(bf16)
 
     on_pattern(plan, me, body)
     held_here[SHARD - ROW_TILE :, :] = jnp.broadcast_to(norm_ref[...], (ROW_TILE, LANES)).astype(bf16)
@@ -564,11 +567,21 @@
         ].astype(f32)[0:1]
 
 
+def accumulate(into, part, chunk):
+    def body(i, _):
+        span = pl.ds(pl.multiple_of(i * chunk, ROW_TILE), chunk)
+        into[span, :] = into[span, :] + part[span, :]
+        return 0
+
+    lax.fori_loop(0, into.shape[0] // chunk, body, 0)
+
+
 class Scatter:
     def __init__(self, place, own, room, send, recv, credit=None, leads=None):
         self.p, self.own = place, own
         rows, half = room[3].shape[1], room[1].shape[2]
         self.low, self.high = pl.ds(0, half), pl.ds(half, rows - half)
+        self.chunk, self.chunk_low, self.chunk_high = (112, 128, 80) if rows == SHARD else (ROW_TILE,) * 3
         self.r1, self.r2a, self.r2b, self.r3, self.r4 = room
         self.send, self.recv, self.credit, self.leads = send, recv, credit, leads
 
@@ -626,7 +639,7 @@
             copy.wait_recv()
         for y in range(2):
             for x in range(2):
-                self.r1[q, y, x] = self.r1[q, y, x] + mine(y, x)
+                accumulate(self.r1.at[q, y, x], mine(y, x), self.chunk)
         self.claim(1, q)
         self.claim(2, q)
         for copy in self.second(q):
@@ -638,8 +651,8 @@
             copy.wait_recv()
         low, high = self.low, self.high
         for k in range(2):
-            self.r2a[q, k] = self.r2a[q, k] + self.r1[q, k, p.x, low]
-            self.r2b[q, k] = self.r2b[q, k] + self.r1[q, p.y, k, high]
+            accumulate(self.r2a.at[q, k], self.r1.at[q, k, p.x, low], self.chunk_low)
+            accumulate(self.r2b.at[q, k], self.r1.at[q, p.y, k, high], self.chunk_high)
         for copy in self.third(q):
             copy.start()
         for copy in self.second(q):
@@ -651,8 +664,8 @@
         for copy in self.third(q):
             copy.wait_recv()
         low, high = self.low, self.high
-        self.r3[q, low] = self.r3[q, low] + self.r2a[q, p.y]
-        self.r3[q, high] = self.r3[q, high] + self.r2b[q, p.x]
+        accumulate(self.r3.at[q, low], self.r2a.at[q, p.y], self.chunk_low)
+        accumulate(self.r3.at[q, high], self.r2b.at[q, p.x], self.chunk_high)
 
         @pl.when(q != p.z)
         def _():
@@ -714,10 +727,10 @@
 ]
 
 
-def unload_shard(plan, me, total, flat_ref):
+def unload_shard(plan, me, block, total, flat_ref):
     def body(layout):
         for count, flat, stride, place in layout:
-            flat_ref[pl.ds(flat, count, stride), :] = total[pl.ds(place, count), :]
+            flat_ref[pl.ds(2 * flat + block, count, 2 * stride), :] = total[pl.ds(place, count), :]
 
     on_pattern(plan, me, body)
 
@@ -783,7 +796,7 @@
         w_qkv, w_out, w_up, w_down, norm_ref = sources
     else:
         *refs, w_qkv, w_out, w_up, w_down, local = refs
-        norm_ref = sources[1]
+        norm_ref = sources[1].at[4:8]
     outs, g_norm = refs[:-15], refs[-15]
     packed, slope, weights_buf, grad_mix, scores, grad_scores = refs[-14:-8]
     first_all, packed_all, mixture_all, attn_all, second_all, hidden_all, active_all, branch_all = refs[-8:]
@@ -948,9 +961,9 @@
         w_qkv, w_out, w_up, w_down, norm_ref, before_ref, *outs, g_norm = refs[:11]
         refs = refs[11:]
     else:
-        held, norm_ref, own_next, before_ref, flat0, flat1, norm_out = refs[:7]
+        held, norm_ref, own_next, before_ref, flat, norm_out = refs[:6]
         own_small, *room_small, total_small, send_small, recv_small = refs[-len(SMALL_ROOM) :]
-        *refs, total, total_rest, own, mine, load, send, recv, credit = refs[7 : -len(SMALL_ROOM)]
+        *refs, total, total_rest, own, mine, load, send, recv, credit = refs[6 : -len(SMALL_ROOM)]
         room, refs = refs[-5:], refs[:-5]
         *refs, g_norm, w_qkv, w_out, w_up, w_down, local = refs
         outs = [own]
@@ -970,12 +983,12 @@
 
     def lead_second(q):
         own_shards(q).wait()
-        lead.begin_second(q, lambda y, x: mine[q % 2, y, x])
+        lead.begin_second(q, lambda y, x: mine.at[q % 2, y, x])
         if q < 2:
             own_shards(q + 2).start()
 
     def rest_second(q):
-        rest.begin_second(q, lambda y, x: own[q, y, x, place.c])
+        rest.begin_second(q, lambda y, x: own.at[q, y, x, place.c])
 
     def at(passing, when, *actions):
         @pl.when(passing & (step == when))
@@ -990,12 +1003,10 @@
         own_shards(0).start()
         own_shards(1).start()
         load_weights(plan, held, own, (w_qkv, w_out, w_up, w_down), local)
-        lead_second(0)
-        lead_second(1)
 
     def lead_finish():
         lead.finish(total)
-        unload_shard(plan, place.me, total, flat1)
+        unload_shard(plan, place.me, 1, total, flat)
         norm_out[...] = total[SHARD - ROW_TILE : SHARD - ROW_TILE + 8]
 
     @pl.when(opening & (step == 0))
@@ -1004,19 +1015,20 @@
 
     if plan is not None:
         at(opening, 0, (begin,))
-        at(opening, 1, (lead_second, 2))
-        at(opening, 2, (lead_second, 3))
-        at(opening, 3, (lead.begin_third, 0))
-        at(opening, 5, (lead.begin_third, 1))
-        at(opening, 7, (lead.begin_z, 0, total))
-        at(midway, 0, (lead.begin_z, 3, total))
-        at(midway, 1, (rest_second, 3))
-        at(midway, 3, (rest.begin_third, 1))
-        at(midway, 5, (rest.begin_third, 2))
+        at(opening, 1, (lead_second, 0))
+        at(opening, 2, (lead_second, 1))
+        at(opening, 4, (lead.begin_third, 0))
+        at(opening, 5, (lead_second, 2))
+        at(opening, 6, (lead.begin_third, 1))
+        at(opening, 7, (lead_second, 3))
+        at(midway, 0, (lead.begin_z, 3, total), (rest_second, 2))
+        at(midway, 2, (rest_second, 3))
+        at(midway, 4, (rest.begin_third, 1))
+        at(midway, 6, (rest.begin_third, 2))
         at(midway, 7, (rest.begin_z, 1, total_rest))
         at(closing, 1, (rest_second, 0))
-        at(closing, 3, (rest.begin_z, 3, total_rest))
-        at(closing, 5, (rest.begin_third, 0))
+        at(closing, 4, (rest.begin_z, 3, total_rest))
+        at(closing, 7, (rest.begin_third, 0))
 
     def side_copy(k):
         source = mixture_hbm if k == 0 else active_hbm.at[:, pl.ds((k - 1) * width, width)]
@@ -1045,19 +1057,19 @@
 
     @pl.when(opening & (step == last))
     def _():
-        if plan is not None:
-            lead.begin_third(2)
         for start in range(0, hidden, width):
             value = dot_tn(second_all[...], hidden_all[:, start : start + width])
             store(2, 0, start, value.astype(bf16))
+            if plan is not None and start == width:
+                lead.begin_third(2)
+                lead.begin_z(0, total)
         if plan is not None:
-            lead.begin_third(3)
+            lead.begin_z(1, total)
         side_copy(0).wait()
         store(1, 0, 0, dot_tn(side[0], attn_all[...]).astype(bf16))
         if plan is not None:
             store_norms(plan, own, 0, g_norm, (0, 1, 2, 3))
             rest.begin_first(1)
-            lead.begin_z(1, total)
         count = hidden // width
         for k in range(1, count + 1):
             if k < count:
@@ -1067,12 +1079,13 @@
             if plan is not None:
                 if k == 1:
                     rest.begin_first(2)
+                    lead.begin_third(3)
                 if k == 2:
                     lead.begin_z(2, total)
+                if k == 3:
                     rest_second(1)
         if plan is not None:
             rest.begin_first(3)
-            rest_second(2)
 
     @pl.when(midway)
     def _():
@@ -1130,13 +1143,13 @@
             store_norms(plan, own_small, 0, g_norm, (0,), 0)
             small.begin_first(0)
             rest.begin_z(0, total_rest)
-            small.begin_second(0, lambda y, x: own_small[0, y, x, place.c])
+            small.begin_second(0, lambda y, x: own_small.at[0, y, x, place.c])
             small.begin_third(0)
             total_small[...] = jnp.zeros_like(total_small)
             small.begin_z(0, total_small)
             small.finish(total_small)
             rest.finish(total_rest)
-            unload_shard(plan, place.me, total_rest, flat0)
+            unload_shard(plan, place.me, 0, total_rest, flat)
             norm_out[...] += total_rest[SHARD - ROW_TILE : SHARD - ROW_TILE + 8]
 
             @pl.when(place.z == 0)
@@ -1184,7 +1197,7 @@
         out_shape += grad_shapes + [jax.ShapeDtypeStruct(norm_sums, f32)]
     else:
         rows = SHARD - ROW_TILE
-        for shape in ((rows, LANES), (rows, LANES), (8, LANES)):
+        for shape in ((2 * rows, LANES), (8, LANES)):
             out_specs.append(whole(shape))
             out_shape.append(jax.ShapeDtypeStruct(shape, f32))
         scratch += [pltpu.VMEM(norm_sums, f32)] + extra + SCATTER_ROOM
@@ -1245,6 +1258,14 @@
     return (param_next, moment_next, second_next)
 
 
+def interleave(pair):
+    return pair.reshape(2, -1, LANES).swapaxes(0, 1).reshape(-1, LANES)
+
+
+def separate(rows):
+    return rows.reshape(-1, 2, LANES).swapaxes(0, 1).reshape(2, -1)
+
+
 def on_device(
     clip_tokens,
     cotangent,
@@ -1269,22 +1290,22 @@
         sources = (*spatial_weights, norm_table[0])
         *kept, after = spatial_forward(plan, x, sources, patch_count, FF)
     else:
-        sources = (params.reshape(2, -1, LANES), norm_par.reshape(1, LANES))
+        sources = (interleave(params), norm_par.reshape(1, LANES))
         *kept, after, spatial_weights, temporal_weights, norm_table = spatial_forward(
             plan, x, sources, patch_count, FF
         )
-        norm_table = norm_table.reshape(2, 4, model_width)
     result, grad_after, *temporal_grads, temporal_norm = temporal_block(
         plan,
         lengths,
         after.reshape(step_slots, patch_count, model_width),
         cotangent.reshape(step_slots, patch_count, model_width),
         temporal_weights,
-        norm_table[1],
+        norm_table[1] if plan is None else norm_table,
         FF,
     )
     grad_before, *spatial_grads, spatial_norm = spatial_backward(
-        plan, x, grad_after.reshape(-1, model_width), kept, spatial_weights, norm_table[0], temporal_grads[0]
+        plan, x, grad_after.reshape(-1, model_width), kept, spatial_weights, norm_table[0] if plan is None else norm_table,
+        temporal_grads[0],
     )
     if plan is None:
 
@@ -1296,12 +1317,19 @@
         norm_grad = jnp.stack([spatial_norm, temporal_norm]).sum(axis=2).reshape(-1)
         norm_sum = lax.psum_scatter(norm_grad, "dp", scatter_dimension=0, tiled=True)
     else:
-        weight_sum = jnp.stack([g.reshape(-1) for g in spatial_grads])
+        weight_sum = spatial_grads[0]
         norm_sum = spatial_norm[0] + spatial_norm[1]
     step_value = float(STEP)
-    new_params, new_moment, new_second = adamw(
-        params, param_moment, param_second, weight_sum, step_value, learn_rate, weight_decay
-    )
+    state = (params, param_moment, param_second)
+    if plan is None:
+        updated = adamw(*state, weight_sum, step_value, learn_rate, weight_decay)
+        new_copy = updated[0].astype(bf16)
+    else:
+        state = lax.optimization_barrier([interleave(part) for part in state])
+        updated = adamw(*state, weight_sum, step_value, learn_rate, weight_decay)
+        new_copy = separate(updated[0].astype(bf16))
+        updated = [separate(part) for part in updated]
+    new_params, new_moment, new_second = updated
     new_norm, new_norm_moment, new_norm_second = adamw(
         norm_par, norm_moment, norm_second, norm_sum, step_value, norm_rate, 0.0
     )
@@ -1311,7 +1339,7 @@
         new_params,
         new_moment,
         new_second,
-        new_params.astype(bf16),
+        new_copy,
         new_norm,
         new_norm_moment,
         new_norm_second,

time: 289 us -> 270 us (0.934); the launches traced: 284 us -> 271 us
  Pallas kernels: 270 us -> 263 us
  local copies, waits for them, and re-layouts: 5.51 us -> 2.04 us
    pallas_call x1, Pallas kernels: 120 us -> 115 us  [spatial_backward(): pl.pallas_call(partial(spatial_backward_kernel, plan), grid=(3, count), i...]
where the time goes in v5:
time: 270 us; the launch traced here: 271 us
  Pallas kernels  263 us (97%)
  other arithmetic  4.89 us (2%)
    pallas_call x1, Pallas kernels, spatial_backward(): pl.pallas_call(partial(spatial_backward_kernel, plan), grid=(3, count), i...  115 us
    pallas_call x1, Pallas kernels, spatial_forward(): pl.pallas_call(partial(spatial_forward_kernel, plan), grid=(2, count), in...  75.1 us
    pallas_call x1, Pallas kernels, temporal_block(): pl.pallas_call(partial(temporal_kernel, plan), grid=(patches // part,), i...  72.8 us

profile of v5, /device:TPU:0, one launch (start us, length us, event | category | flops | bytes accessed | tf_op | source)
XLA Modules:
  0.0 271.3 jit_solution(9814589838481431365)
XLA Ops:
  1.3 75.1 %shard_map.160 = (bf16[2048,1536]{1,0:T(8,128)(2,1)}, bf16[8,4,256,512]{3,2,1,0:T(8,128)(2,1)}, bf16[2048,512]{1,0:T(8,128)(2,1)}, f32[2048,512]{1,0:T(8,128)}, ...) custom-call(bf16[2048,512]{1,0:T(8,128)(2,1)} %bitcast.49, ...), custom_call_target="tpu_custom_call" | custom-call | tf_op jit(solution)/shard_map/pallas_call | solution.py:333
  76.4 72.8 %shard_map.161 = (f32[8,256,512]{2,1,0:T(8,128)}, f32[8,256,512]{2,1,0:T(8,128)}, bf16[4,2,2,2,784,128]{5,4,3,2,1,0:T(8,128)(2,1)}, f32[4,8,512]{2,1,0:T(8,128)}) custom-call(s32[1]{0:T(128)S(6)} %copy.26.length_ref, f32[8,256,512]{2,1,0:T(8,128)} %bitcast.51, bf16[8,256,512]{2,1,0:T(8,128)(2,1)} %bitcast.56, ...), custom_call_target="tpu_custom_call" | custom-call | tf_op jit(solution)/shard_map/pallas_call | solution.py:923
  149.3 0.0 copy-start.2
  149.3 0.0 copy-start.3
  149.3 0.0 copy-start.4
  149.3 0.0 copy-start.1
  149.3 114.8 %shard_map.162 = (f32[2048,512]{1,0:T(8,128)}, f32[1536,128]{1,0:T(8,128)}, f32[8,128]{1,0:T(8,128)}) custom-call(bf16[2048,512]{1,0:T(8,128)(2,1)} %bitcast.50, f32[2048,512]{1,0:T(8,128)} %bitcast.53, bf16[2048,1536]{1,0:T(8,128)(2,1)} %get-tuple-element.33.packed_ref, bf16[8,4,256,512]{3,2,1,0:T(8,128)(2,1)} %get-tuple-element.34.weights_ref, ...), custom_call_target="tpu_custom_call" | custom-call | tf_op jit(solution)/shard_map/pallas_call | solution.py:1217
  264.1 0.0 copy-start
  264.1 0.0 copy-done.2
  264.2 0.0 copy-done.3
  264.2 0.0 copy-done.4
  264.2 1.4 multiply_subtract_fusion.1
  265.6 0.0 copy-done.1
  265.6 3.5 %fusion.5 = (bf16[1536,128]{1,0:T(8,128)(2,1)}, f32[1536,128]{1,0:T(8,128)}, f32[1536,128]{1,0:T(8,128)}, f32[1536,128]{1,0:T(8,128)}) fusion(f32[1536,128]{1,0:T(8,128)S(1)} %bitcast.55, f32[1536,128]{1,0:T(8,128)} %get-tuple-element.44, f32[1536,128]{1,0:T(8,128)} %bitcast.57, f32[1536,128]{1,0:T(8,128)} %bitcast.58), kind=kLoop, calls=%fused_computation.10 | loop fusion | flops 3145728 | bytes 5898240 | tf_op jit(solution)/shard_map/convert_element_type | solution.py:1330
  269.1 0.0 copy-done
  269.1 2.0 copy.27
Async XLA Ops:
  149.3 114.9 %copy-start.2 = (f32[128]{0:T(128)S(1)}, f32[128]{0:T(128)}, u32[]{:S(2)}) copy-start(f32[128]{0:T(128)} %param.15) | copy-start | bytes 1540
  149.3 114.9 %copy-start.3 = (f32[128]{0:T(128)S(1)}, f32[128]{0:T(128)}, u32[]{:S(2)}) copy-start(f32[128]{0:T(128)} %param.16) | copy-start | bytes 1540
  149.3 114.9 %copy-start.4 = (f32[128]{0:T(128)S(1)}, f32[128]{0:T(128)}, u32[]{:S(2)}) copy-start(f32[128]{0:T(128)} %param.17) | copy-start | bytes 1540
  149.3 116.2 %copy-start.1 = (f32[2,98304]{1,0:T(2,128)S(1)}, f32[2,98304]{1,0:T(2,128)}, u32[]{:S(2)}) copy-start(f32[2,98304]{1,0:T(2,128)} %param.12) | copy-start | bytes 2359300
  264.1 4.9 %copy-start = (f32[2048,512]{1,0:T(8,128)S(1)}, f32[2048,512]{1,0:T(8,128)}, u32[]{:S(2)}) copy-start(f32[2048,512]{1,0:T(8,128)} %get-tuple-element.41) | copy-start | bytes 12582916

commit v6 on v5

--- a/solution.py
+++ b/solution.py
@@ -161,6 +161,7 @@
         scores, mixture_all, w_qkv, w_out, w_up, w_down, held, staged, send, recv, local = refs[10:]
         matrices = (w_qkv, w_out, w_up, w_down)
         place = Place(lax.axis_index("dp"))
+        order = [place.z] + [k - (place.z + 4 - k) // 4 for k in range(1, 4)]
         now = Gather(place, held, send.at[0], recv.at[0])
         later = Gather(place, held_next, send.at[1], recv.at[1])
         keep = pltpu.make_async_copy(held, held_out, local.at[0])
@@ -182,53 +183,42 @@
             )
             copy.start()
             copy.wait()
-            now.begin_first(0)
-            now.begin_second(0)
-            for q in range(1, 4):
-                now.begin_first(q)
+            now.begin_first(order[0])
+            later.begin_first(order[0])
+            now.begin_second(order[0])
+            later.begin_second(order[0])
+            now.begin_first(order[1])
+            now.begin_third(order[0])
+            now.begin_second(order[1])
+            now.begin_third(order[1])
+            now.begin_first(order[2])
+            now.begin_first(order[3])
             later.start_z()
-            now.begin_third(0)
             gathered(0)
 
-        @pl.when(opening & (step == 1))
-        def _():
-            now.begin_second(1)
-            now.begin_second(2)
-
-        @pl.when(opening & (step == 2))
-        def _():
-            now.begin_second(3)
-
-        @pl.when(opening & (step == 4))
-        def _():
-            now.begin_third(1)
-            now.begin_third(2)
-
-        @pl.when(opening & (step == 5))
-        def _():
-            for q in range(4):
-                later.begin_first(q)
-
-        @pl.when(opening & (step == 7))
-        def _():
-            now.begin_third(3)
+        def at(passing, when, *actions):
+            @pl.when(passing & (step == when))
+            def _():
+                for action, k in actions:
+                    action(order[k])
+
+        closing = jnp.logical_not(opening)
+        at(opening, 1, (now.begin_second, 2))
+        at(opening, 2, (now.begin_second, 3))
+        at(opening, 3, (now.begin_third, 2))
+        at(opening, 4, (later.begin_first, 1), (later.begin_first, 2), (later.begin_first, 3))
+        at(opening, 5, (now.begin_third, 3))
+        at(opening, 6, (later.begin_second, 1), (later.begin_third, 0))
+        at(opening, 7, (later.begin_second, 2))
+        at(closing, 0, (later.begin_second, 3))
+        at(closing, 1, (later.begin_third, 1))
+        at(closing, 3, (later.begin_third, 2))
+        at(closing, 6, (later.begin_third, 3))
 
         @pl.when(jnp.logical_not(opening) & (step == 0))
         def _():
             gathered(1, 2, 3)
             keep.start()
-
-        for q in range(4):
-
-            @pl.when(jnp.logical_not(opening) & (step == q + 1))
-            def _(q=q):
-                later.begin_second(q)
-
-        for q in range(3):
-
-            @pl.when(jnp.logical_not(opening) & (step == q + 5))
-            def _(q=q):
-                later.begin_third(q)
 
     tile, width = x_ref.shape
     here = pl.ds(pl.multiple_of(step * tile, tile), tile)
@@ -269,7 +259,6 @@
 
         @pl.when(jnp.logical_not(opening) & (step == last))
         def _():
-            later.begin_third(3)
             for q in range(4):
                 later.finish(q)
             keep.wait()

time: 270 us -> 264 us (0.978)
  Pallas kernels: 263 us -> 256 us
    pallas_call x1, Pallas kernels: 115 us -> 105 us  [spatial_backward(): pl.pallas_call(partial(spatial_backward_kernel, plan), grid=(3, count), i...]
    pallas_call x1, Pallas kernels: 75.1 us -> 78.6 us  [spatial_forward(): pl.pallas_call(partial(spatial_forward_kernel, plan), grid=(2, count), in...]
where the time goes in v6:
time: 264 us; the launch traced here: 265 us
  Pallas kernels  256 us (97%)
  other arithmetic  4.89 us (2%)
    pallas_call x1, Pallas kernels, spatial_backward(): pl.pallas_call(partial(spatial_backward_kernel, plan), grid=(3, count), i...  105 us
    pallas_call x1, Pallas kernels, spatial_forward(): pl.pallas_call(partial(spatial_forward_kernel, plan), grid=(2, count), in...  78.6 us
    pallas_call x1, Pallas kernels, temporal_block(): pl.pallas_call(partial(temporal_kernel, plan), grid=(patches // part,), i...  72.8 us

profile of v6, /device:TPU:0, one launch (start us, length us, event | category | flops | bytes accessed | tf_op | source)
XLA Modules:
  0.0 265.0 jit_solution(16594487304249072122)
XLA Ops:
  1.3 78.6 %shard_map.160 = (bf16[2048,1536]{1,0:T(8,128)(2,1)}, bf16[8,4,256,512]{3,2,1,0:T(8,128)(2,1)}, bf16[2048,512]{1,0:T(8,128)(2,1)}, f32[2048,512]{1,0:T(8,128)}, ...) custom-call(bf16[2048,512]{1,0:T(8,128)(2,1)} %bitcast.49, ...), custom_call_target="tpu_custom_call" | custom-call | tf_op jit(solution)/shard_map/pallas_call | solution.py:322
  79.8 72.8 %shard_map.161 = (f32[8,256,512]{2,1,0:T(8,128)}, f32[8,256,512]{2,1,0:T(8,128)}, bf16[4,2,2,2,784,128]{5,4,3,2,1,0:T(8,128)(2,1)}, f32[4,8,512]{2,1,0:T(8,128)}) custom-call(s32[1]{0:T(128)S(6)} %copy.26.length_ref, f32[8,256,512]{2,1,0:T(8,128)} %bitcast.51, bf16[8,256,512]{2,1,0:T(8,128)(2,1)} %bitcast.56, ...), custom_call_target="tpu_custom_call" | custom-call | tf_op jit(solution)/shard_map/pallas_call | solution.py:912
  152.7 0.0 copy-start.2
  152.7 0.0 copy-start.3
  152.7 0.0 copy-start.4
  152.7 0.0 copy-start.1
  152.7 105.1 %shard_map.162 = (f32[2048,512]{1,0:T(8,128)}, f32[1536,128]{1,0:T(8,128)}, f32[8,128]{1,0:T(8,128)}) custom-call(bf16[2048,512]{1,0:T(8,128)(2,1)} %bitcast.50, f32[2048,512]{1,0:T(8,128)} %bitcast.53, bf16[2048,1536]{1,0:T(8,128)(2,1)} %get-tuple-element.33.packed_ref, bf16[8,4,256,512]{3,2,1,0:T(8,128)(2,1)} %get-tuple-element.34.weights_ref, ...), custom_call_target="tpu_custom_call" | custom-call | tf_op jit(solution)/shard_map/pallas_call | solution.py:1206
  257.9 0.0 copy-start
  257.9 0.0 copy-done.2
  257.9 0.0 copy-done.3
  257.9 0.0 copy-done.4
  257.9 1.4 multiply_subtract_fusion.1
  259.3 0.0 copy-done.1
  259.3 3.5 %fusion.5 = (bf16[1536,128]{1,0:T(8,128)(2,1)}, f32[1536,128]{1,0:T(8,128)}, f32[1536,128]{1,0:T(8,128)}, f32[1536,128]{1,0:T(8,128)}) fusion(f32[1536,128]{1,0:T(8,128)S(1)} %bitcast.55, f32[1536,128]{1,0:T(8,128)} %get-tuple-element.44, f32[1536,128]{1,0:T(8,128)} %bitcast.57, f32[1536,128]{1,0:T(8,128)} %bitcast.58), kind=kLoop, calls=%fused_computation.10 | loop fusion | flops 3145728 | bytes 5898240 | tf_op jit(solution)/shard_map/convert_element_type | solution.py:1319
  262.8 0.0 copy-done
  262.8 2.0 copy.27
Async XLA Ops:
  152.7 105.2 %copy-start.2 = (f32[128]{0:T(128)S(1)}, f32[128]{0:T(128)}, u32[]{:S(2)}) copy-start(f32[128]{0:T(128)} %param.15) | copy-start | bytes 1540
  152.7 105.2 %copy-start.3 = (f32[128]{0:T(128)S(1)}, f32[128]{0:T(128)}, u32[]{:S(2)}) copy-start(f32[128]{0:T(128)} %param.16) | copy-start | bytes 1540
  152.7 105.2 %copy-start.4 = (f32[128]{0:T(128)S(1)}, f32[128]{0:T(128)}, u32[]{:S(2)}) copy-start(f32[128]{0:T(128)} %param.17) | copy-start | bytes 1540
  152.7 106.5 %copy-start.1 = (f32[2,98304]{1,0:T(2,128)S(1)}, f32[2,98304]{1,0:T(2,128)}, u32[]{:S(2)}) copy-start(f32[2,98304]{1,0:T(2,128)} %param.12) | copy-start | bytes 2359300
  257.9 4.9 %copy-start = (f32[2048,512]{1,0:T(8,128)S(1)}, f32[2048,512]{1,0:T(8,128)}, u32[]{:S(2)}) copy-start(f32[2048,512]{1,0:T(8,128)} %get-tuple-element.41) | copy-start | bytes 12582916

commit v7 on v6

--- a/solution.py
+++ b/solution.py
@@ -190,10 +190,10 @@
             now.begin_first(order[1])
             now.begin_third(order[0])
             now.begin_second(order[1])
+            later.start_z()
             now.begin_third(order[1])
             now.begin_first(order[2])
             now.begin_first(order[3])
-            later.start_z()
             gathered(0)
 
         def at(passing, when, *actions):
@@ -694,6 +694,73 @@
             self.leave_z(q)
 
 
+class Relay(Scatter):
+    def hand_on(self, room, send, recv, device):
+        return remote(self.r3.at[0], room, send.at[0], recv.at[0], device)
+
+    def start_tail(self, total, room, send, recv):
+        p = self.p
+        for copy in self.third(0):
+            copy.wait_recv()
+        accumulate(self.r3.at[0, self.low], self.r2a.at[0, p.y], self.chunk_low)
+        accumulate(self.r3.at[0, self.high], self.r2b.at[0, p.x], self.chunk_high)
+
+        @pl.when(p.z == 3)
+        def _():
+            self.hand_on(room, send, recv, p.plane(2)).start()
+
+        @pl.when(p.z == 1)
+        def _():
+            self.along_z(0).start()
+
+        @pl.when(p.z == 0)
+        def _():
+            total[...] = self.r3[0].astype(f32)
+
+        for copy in self.third(0):
+            copy.wait_send()
+
+    def go_on(self, room, send, recv):
+        @pl.when(self.p.z == 2)
+        def _():
+            self.hand_on(room, send, recv, self.p.me).wait_recv()
+            accumulate(self.r3.at[0], room, self.chunk)
+            self.along_z(0).start()
+
+    def finish_tail(self, total, room, send, recv):
+        p = self.p
+
+        def arrive(z):
+            remote(self.r3.at[0], self.r4.at[z], self.send.at[5, 0], self.recv.at[5, z], p.me).wait_recv()
+
+        @pl.when(p.z == 0)
+        def _():
+            for z in (1, 2):
+                arrive(z)
+                total[...] += self.r4[z].astype(f32)
+
+        @pl.when(p.z > 0)
+        def _():
+            for k in range(1, 4):
+                z = lax.rem(p.z + k, 4)
+                arrive(z)
+                total[...] += self.r4[z].astype(f32)
+
+        for q in range(4):
+            for copy in self.first(q):
+                copy.wait_send()
+        for q in range(1, 4):
+            self.leave_z(q)
+
+        @pl.when((p.z == 1) | (p.z == 2))
+        def _():
+            self.along_z(0).wait_send()
+
+        @pl.when(p.z == 3)
+        def _():
+            self.hand_on(room, send, recv, p.plane(2)).wait_send()
+
+
 SCATTER_ROOM = [
     pltpu.VMEM((4, 2, 2, SHARD, LANES), bf16),
     pltpu.VMEM((4, 2, HALF, LANES), bf16),
@@ -951,15 +1018,16 @@
         refs = refs[11:]
     else:
         held, norm_ref, own_next, before_ref, flat, norm_out = refs[:6]
-        own_small, *room_small, total_small, send_small, recv_small = refs[-len(SMALL_ROOM) :]
-        *refs, total, total_rest, own, mine, load, send, recv, credit = refs[6 : -len(SMALL_ROOM)]
+        own_small, *room_small, total_small, send_small, recv_small = refs[-len(SMALL_ROOM) - 3 : -3]
+        relay = refs[-3:]
+        *refs, total, total_rest, own, mine, load, send, recv, credit = refs[6 : -len(SMALL_ROOM) - 3]
         room, refs = refs[-5:], refs[:-5]
         *refs, g_norm, w_qkv, w_out, w_up, w_down, local = refs
         outs = [own]
         place = Place(lax.axis_index("dp"))
         rooms = [(*room[:3], room[3].at[k], room[4].at[k]) for k in range(2)]
         lead = Scatter(place, own_next, rooms[0], send.at[0], recv.at[0], credit, True)
-        rest = Scatter(place, own, rooms[1], send.at[1], recv.at[1], credit, False)
+        rest = Relay(place, own, rooms[1], send.at[1], recv.at[1], credit, False)
         small = Scatter(place, own_small, room_small, send_small, recv_small)
     scores, grad_scores, grad_mix, middle_all, second_all, hidden_all, attn_all, branch_all, side, side_sem = refs
     store = storing(plan, outs)
@@ -1131,13 +1199,14 @@
             own_small[...] = jnp.zeros_like(own_small)
             store_norms(plan, own_small, 0, g_norm, (0,), 0)
             small.begin_first(0)
-            rest.begin_z(0, total_rest)
+            rest.start_tail(total_rest, *relay)
             small.begin_second(0, lambda y, x: own_small.at[0, y, x, place.c])
             small.begin_third(0)
+            rest.go_on(*relay)
             total_small[...] = jnp.zeros_like(total_small)
             small.begin_z(0, total_small)
             small.finish(total_small)
-            rest.finish(total_rest)
+            rest.finish_tail(total_rest, *relay)
             unload_shard(plan, place.me, 0, total_rest, flat)
             norm_out[...] += total_rest[SHARD - ROW_TILE : SHARD - ROW_TILE + 8]
 
@@ -1201,6 +1270,11 @@
             pltpu.SemaphoreType.REGULAR((3, 4)),
         ]
         scratch += SMALL_ROOM
+        scratch += [
+            pltpu.VMEM((SHARD, LANES), bf16),
+            pltpu.SemaphoreType.DMA((1,)),
+            pltpu.SemaphoreType.DMA((1,)),
+        ]
         operands, specs = operands + [own_next], specs + [anywhere]
         params |= dict(collective_id=1, has_side_effects=True)
     return pl.pallas_call(

time: 264 us -> 261 us (0.989)
  Pallas kernels: 256 us -> 253 us
    pallas_call x1, Pallas kernels: 105 us -> 101 us  [spatial_backward(): pl.pallas_call(partial(spatial_backward_kernel, plan), grid=(3, count), i...]
where the time goes in v7:
time: 261 us; the launch traced here: 262 us
  Pallas kernels  253 us (97%)
  other arithmetic  4.89 us (2%)
    pallas_call x1, Pallas kernels, spatial_backward(): pl.pallas_call(partial(spatial_backward_kernel, plan), grid=(3, count), i...  101 us
    pallas_call x1, Pallas kernels, spatial_forward(): pl.pallas_call(partial(spatial_forward_kernel, plan), grid=(2, count), in...  79.4 us
    pallas_call x1, Pallas kernels, temporal_block(): pl.pallas_call(partial(temporal_kernel, plan), grid=(patches // part,), i...  72.8 us

profile of v7, /device:TPU:0, one launch (start us, length us, event | category | flops | bytes accessed | tf_op | source)
XLA Modules:
  0.0 261.8 jit_solution(504964489780354248)
XLA Ops:
  1.3 79.4 %shard_map.160 = (bf16[2048,1536]{1,0:T(8,128)(2,1)}, bf16[8,4,256,512]{3,2,1,0:T(8,128)(2,1)}, bf16[2048,512]{1,0:T(8,128)(2,1)}, f32[2048,512]{1,0:T(8,128)}, ...) custom-call(bf16[2048,512]{1,0:T(8,128)(2,1)} %bitcast.49, ...), custom_call_target="tpu_custom_call" | custom-call | tf_op jit(solution)/shard_map/pallas_call | solution.py:322
  80.7 72.8 %shard_map.161 = (f32[8,256,512]{2,1,0:T(8,128)}, f32[8,256,512]{2,1,0:T(8,128)}, bf16[4,2,2,2,784,128]{5,4,3,2,1,0:T(8,128)(2,1)}, f32[4,8,512]{2,1,0:T(8,128)}) custom-call(s32[1]{0:T(128)S(6)} %copy.26.length_ref, f32[8,256,512]{2,1,0:T(8,128)} %bitcast.51, bf16[8,256,512]{2,1,0:T(8,128)(2,1)} %bitcast.56, ...), custom_call_target="tpu_custom_call" | custom-call | tf_op jit(solution)/shard_map/pallas_call | solution.py:979
  153.5 0.0 copy-start.2
  153.5 0.0 copy-start.3
  153.5 0.0 copy-start.4
  153.5 0.0 copy-start.1
  153.6 101.1 %shard_map.162 = (f32[2048,512]{1,0:T(8,128)}, f32[1536,128]{1,0:T(8,128)}, f32[8,128]{1,0:T(8,128)}) custom-call(bf16[2048,512]{1,0:T(8,128)(2,1)} %bitcast.50, f32[2048,512]{1,0:T(8,128)} %bitcast.53, bf16[2048,1536]{1,0:T(8,128)(2,1)} %get-tuple-element.33.packed_ref, bf16[8,4,256,512]{3,2,1,0:T(8,128)(2,1)} %get-tuple-element.34.weights_ref, ...), custom_call_target="tpu_custom_call" | custom-call | tf_op jit(solution)/shard_map/pallas_call | solution.py:1280
  254.7 0.0 copy-start
  254.7 0.0 copy-done.2
  254.7 0.0 copy-done.3
  254.7 0.0 copy-done.4
  254.7 1.4 multiply_subtract_fusion.1
  256.1 0.0 copy-done.1
  256.1 3.5 %fusion.5 = (bf16[1536,128]{1,0:T(8,128)(2,1)}, f32[1536,128]{1,0:T(8,128)}, f32[1536,128]{1,0:T(8,128)}, f32[1536,128]{1,0:T(8,128)}) fusion(f32[1536,128]{1,0:T(8,128)S(1)} %bitcast.55, f32[1536,128]{1,0:T(8,128)} %get-tuple-element.44, f32[1536,128]{1,0:T(8,128)} %bitcast.57, f32[1536,128]{1,0:T(8,128)} %bitcast.58), kind=kLoop, calls=%fused_computation.10 | loop fusion | flops 3145728 | bytes 5898240 | tf_op jit(solution)/shard_map/convert_element_type | solution.py:1393
  259.6 0.0 copy-done
  259.6 2.0 copy.27
Async XLA Ops:
  153.5 101.2 %copy-start.2 = (f32[128]{0:T(128)S(1)}, f32[128]{0:T(128)}, u32[]{:S(2)}) copy-start(f32[128]{0:T(128)} %param.15) | copy-start | bytes 1540
  153.5 101.2 %copy-start.3 = (f32[128]{0:T(128)S(1)}, f32[128]{0:T(128)}, u32[]{:S(2)}) copy-start(f32[128]{0:T(128)} %param.16) | copy-start | bytes 1540
  153.5 101.2 %copy-start.4 = (f32[128]{0:T(128)S(1)}, f32[128]{0:T(128)}, u32[]{:S(2)}) copy-start(f32[128]{0:T(128)} %param.17) | copy-start | bytes 1540
  153.5 102.5 %copy-start.1 = (f32[2,98304]{1,0:T(2,128)S(1)}, f32[2,98304]{1,0:T(2,128)}, u32[]{:S(2)}) copy-start(f32[2,98304]{1,0:T(2,128)} %param.12) | copy-start | bytes 2359300
  254.7 4.9 %copy-start = (f32[2048,512]{1,0:T(8,128)S(1)}, f32[2048,512]{1,0:T(8,128)}, u32[]{:S(2)}) copy-start(f32[2048,512]{1,0:T(8,128)} %get-tuple-element.41) | copy-start | bytes 12582916

commit v8 on v7

--- a/solution.py
+++ b/solution.py
@@ -952,10 +952,12 @@
 
 
 def load_weights(plan, held, room, matrices, local):
-    copy = pltpu.make_async_copy(held, room, local.at[0])
-    copy.start()
-    copy.wait()
-    assemble(plan, room, matrices, range(4))
+    copies = [pltpu.make_async_copy(held.at[z], room.at[z], local.at[z]) for z in range(4)]
+    for copy in copies:
+        copy.start()
+    for z, copy in enumerate(copies):
+        copy.wait()
+        assemble(plan, room, matrices, (z,))
 
 
 def weight_sources(plan, weights, norms, hidden):
@@ -963,7 +965,7 @@
     if plan is None:
         return [*weights, norms], [whole(a.shape) for a in (*weights, norms)], []
     scratch = [pltpu.VMEM(shape, bf16) for shape in matrix_shapes(width, hidden)]
-    scratch.append(pltpu.SemaphoreType.DMA((1,)))
+    scratch.append(pltpu.SemaphoreType.DMA((4,)))
     return [weights, norms], [pl.BlockSpec(memory_space=pl.ANY), whole(norms.shape)], scratch
 
 

time: 261 us -> 259 us (level)
  no operation moved by 1% of the time
where the time goes in v8:
time: 259 us; the launch traced here: 260 us
  Pallas kernels  252 us (97%)
  other arithmetic  4.89 us (2%)
    pallas_call x1, Pallas kernels, spatial_backward(): pl.pallas_call(partial(spatial_backward_kernel, plan), grid=(3, count), i...  100 us
    pallas_call x1, Pallas kernels, spatial_forward(): pl.pallas_call(partial(spatial_forward_kernel, plan), grid=(2, count), in...  79.4 us
    pallas_call x1, Pallas kernels, temporal_block(): pl.pallas_call(partial(temporal_kernel, plan), grid=(patches // part,), i...  72.2 us

profile of v8, /device:TPU:0, one launch (start us, length us, event | category | flops | bytes accessed | tf_op | source)
XLA Modules:
  0.0 260.5 jit_solution(4476409552753597132)
XLA Ops:
  1.3 79.4 %shard_map.160 = (bf16[2048,1536]{1,0:T(8,128)(2,1)}, bf16[8,4,256,512]{3,2,1,0:T(8,128)(2,1)}, bf16[2048,512]{1,0:T(8,128)(2,1)}, f32[2048,512]{1,0:T(8,128)}, ...) custom-call(bf16[2048,512]{1,0:T(8,128)(2,1)} %bitcast.49, ...), custom_call_target="tpu_custom_call" | custom-call | tf_op jit(solution)/shard_map/pallas_call | solution.py:322
  80.7 72.2 %shard_map.161 = (f32[8,256,512]{2,1,0:T(8,128)}, f32[8,256,512]{2,1,0:T(8,128)}, bf16[4,2,2,2,784,128]{5,4,3,2,1,0:T(8,128)(2,1)}, f32[4,8,512]{2,1,0:T(8,128)}) custom-call(s32[1]{0:T(128)S(6)} %copy.26.length_ref, f32[8,256,512]{2,1,0:T(8,128)} %bitcast.51, bf16[8,256,512]{2,1,0:T(8,128)(2,1)} %bitcast.56, ...), custom_call_target="tpu_custom_call" | custom-call | tf_op jit(solution)/shard_map/pallas_call | solution.py:981
  152.8 0.0 copy-start.2
  152.8 0.0 copy-start.3
  152.8 0.0 copy-start.4
  152.9 0.0 copy-start.1
  152.9 100.5 %shard_map.162 = (f32[2048,512]{1,0:T(8,128)}, f32[1536,128]{1,0:T(8,128)}, f32[8,128]{1,0:T(8,128)}) custom-call(bf16[2048,512]{1,0:T(8,128)(2,1)} %bitcast.50, f32[2048,512]{1,0:T(8,128)} %bitcast.53, bf16[2048,1536]{1,0:T(8,128)(2,1)} %get-tuple-element.33.packed_ref, bf16[8,4,256,512]{3,2,1,0:T(8,128)(2,1)} %get-tuple-element.34.weights_ref, ...), custom_call_target="tpu_custom_call" | custom-call | tf_op jit(solution)/shard_map/pallas_call | solution.py:1282
  253.3 0.0 copy-start
  253.3 0.0 copy-done.2
  253.4 0.0 copy-done.3
  253.4 0.0 copy-done.4
  253.4 1.4 multiply_subtract_fusion.1
  254.7 0.0 copy-done.1
  254.7 3.5 %fusion.5 = (bf16[1536,128]{1,0:T(8,128)(2,1)}, f32[1536,128]{1,0:T(8,128)}, f32[1536,128]{1,0:T(8,128)}, f32[1536,128]{1,0:T(8,128)}) fusion(f32[1536,128]{1,0:T(8,128)S(1)} %bitcast.55, f32[1536,128]{1,0:T(8,128)} %get-tuple-element.44, f32[1536,128]{1,0:T(8,128)} %bitcast.57, f32[1536,128]{1,0:T(8,128)} %bitcast.58), kind=kLoop, calls=%fused_computation.10 | loop fusion | flops 3145728 | bytes 5898240 | tf_op jit(solution)/shard_map/convert_element_type | solution.py:1395
  258.3 0.0 copy-done
  258.3 2.0 copy.27
Async XLA Ops:
  152.8 100.5 %copy-start.2 = (f32[128]{0:T(128)S(1)}, f32[128]{0:T(128)}, u32[]{:S(2)}) copy-start(f32[128]{0:T(128)} %param.15) | copy-start | bytes 1540
  152.8 100.5 %copy-start.3 = (f32[128]{0:T(128)S(1)}, f32[128]{0:T(128)}, u32[]{:S(2)}) copy-start(f32[128]{0:T(128)} %param.16) | copy-start | bytes 1540
  152.8 100.5 %copy-start.4 = (f32[128]{0:T(128)S(1)}, f32[128]{0:T(128)}, u32[]{:S(2)}) copy-start(f32[128]{0:T(128)} %param.17) | copy-start | bytes 1540
  152.9 101.9 %copy-start.1 = (f32[2,98304]{1,0:T(2,128)S(1)}, f32[2,98304]{1,0:T(2,128)}, u32[]{:S(2)}) copy-start(f32[2,98304]{1,0:T(2,128)} %param.12) | copy-start | bytes 2359300
  253.3 4.9 %copy-start = (f32[2048,512]{1,0:T(8,128)S(1)}, f32[2048,512]{1,0:T(8,128)}, u32[]{:S(2)}) copy-start(f32[2048,512]{1,0:T(8,128)} %get-tuple-element.41) | copy-start | bytes 12582916
